TPU v7x, 32 devices: a whole 2x2x4 slice. The times are simulated.
32 devices in a mesh: pb: 8 (over y, x, core), slot: 4 (over z).
Axes of the slice: x: 2, y: 2, z: 4, core: 2. Of those that a mesh axis runs over, the one named last changes fastest.
Arguments:
- x_in: bfloat16 [8, 16, 128, 1024], P(None, 'pb', 'slot'), may hold values from -6 to 6
- memory: bfloat16 [8, 16, 384, 1024], P(None, 'pb', 'slot'), may hold values from -6 to 6
- doc_scores: float32 [16, 8], P('pb'), may hold values from -6 to 6
- valid_count: int32 [16], P('pb'), may hold values from 2 to 8, as said below
- target_ids: int32 [16, 128], P('pb'), may hold values from 0 to 50175
- target_len: int32 [16], P('pb'), may hold values from 64 to 128, as said below
- mem_len: int32 [8, 16], P('slot', 'pb'), may hold values from 192 to 384, as said below
- attn_w: bfloat16 [8192, 1024], P(('pb', 'slot')), as said below
- ffn_in: bfloat16 [4096, 1024], P(('pb', 'slot')), may hold values from -0.1875 to 0.1875
- ffn_out: bfloat16 [4096, 1024], P(('pb', 'slot')), may hold values from -0.09375 to 0.09375
- ffn_bias: float32 [4096], replicated, may hold values from -4 to 4
- norms: float32 [6, 1024], replicated, as said below
- embedding: bfloat16 [50176, 1024], P('slot'), may hold values from -0.375 to 0.375
Outputs:
- loss: float32 [], replicated
- entropy: float32 [], replicated
- grad_x: bfloat16 [8, 16, 128, 1024], P(None, 'pb', 'slot')
- grad_memory: bfloat16 [8, 16, 384, 1024], P(None, 'pb', 'slot')
- grad_attn: float32 [8192, 1024], P(('pb', 'slot'))
- grad_ffn_in: float32 [4096, 1024], P(('pb', 'slot'))
- grad_ffn_out: float32 [4096, 1024], P(('pb', 'slot'))
- grad_ffn_bias: float32 [4096], P(('pb', 'slot'))
- grad_norms: float32 [6, 1024], replicated
- grad_embedding: float32 [50176, 1024], P('slot', 'pb')
Inputs may be any that keep to these rules, and one draw needn't show every extreme that they name: `valid_count`: some question has 8 valid slots and some other question has 2. `target_len`: some question has 128 real tokens and some other question has 64; real tokens come first. `mem_len`: for every slot, some question has 384 real positions and some other question has 192; real positions come first. `attn_w`: independent normal entries with a fixed scale for each of the eight blocks. `norms`: gains in rows 0, 2, 4 and shifts in rows 1, 3, 5.
All inputs are finite; a program needn't handle non-finite values.
Results may differ from a plain program's by a relative error of at most 0.03.
Values may be sent and summed in bfloat16 or wider, within the bound.
A program may use at most 448 MiB of HBM per device.

v0:
```python
import jax
import jax.numpy as jnp
from jax import lax
from jax.sharding import PartitionSpec as P

HEADS = 16


eps_norm = 1e-05
entropy_weight = 0.25
mask_fill = -1e30
root_half = 0.7071067811865476
inv_root_tau = 0.3989422804014327


def merged(value, axis, join):
    pieces = jax.tree.map(lambda part: lax.all_gather(part, axis), value)
    head = jax.tree.map(lambda part: part[0], pieces)
    tail = jax.tree.map(lambda part: part[1:], pieces)
    running, _ = lax.scan(lambda running, section: (join(running, section), None), head, tail)
    return running


def product(left, right):
    return jnp.dot(left, right, preferred_element_type=jnp.float32)


def contract_rows(left, right):
    return lax.dot_general(
        left, right, (((0,), (0,)), ((), ())), preferred_element_type=jnp.float32
    )


def contract_cols(left, right):
    return lax.dot_general(
        left, right, (((1,), (1,)), ((), ())), preferred_element_type=jnp.float32
    )


def norm_forward(resid, gain, shift):
    row_mean = jnp.mean(resid, axis=-1, keepdims=True)
    centered = resid - row_mean
    inv_root = lax.rsqrt(jnp.mean(centered * centered, axis=-1, keepdims=True) + eps_norm)
    normed = centered * inv_root
    return (normed * gain + shift, normed, inv_root)


def norm_backward(grad_out, normed, inv_root, gain):
    scaled = grad_out * gain
    grad_in = inv_root * (
        scaled
        - jnp.mean(scaled, axis=-1, keepdims=True)
        - normed * jnp.mean(scaled * normed, axis=-1, keepdims=True)
    )
    return (grad_in, jnp.sum(grad_out * normed, axis=0), jnp.sum(grad_out, axis=0))


def attend_forward(queries, key_rows, value_rows, allowed):
    scores = jnp.einsum("nqhe,nkhe->nhqk", queries, key_rows, preferred_element_type=jnp.float32)
    scores = jnp.where(allowed, scores, mask_fill)
    row_max = jnp.max(scores, axis=-1, keepdims=True)
    expos = jnp.exp(scores - row_max)
    row_sum = jnp.sum(expos, axis=-1, keepdims=True)
    probs_low = (expos / row_sum).astype(jnp.bfloat16)
    result = jnp.einsum(
        "nhqk,nkhe->nqhe", probs_low, value_rows, preferred_element_type=jnp.float32
    )
    return (result, row_max + jnp.log(row_sum))


def attend_backward(queries, key_rows, value_rows, allowed, row_lse, grad_out):
    scores = jnp.einsum("nqhe,nkhe->nhqk", queries, key_rows, preferred_element_type=jnp.float32)
    scores = jnp.where(allowed, scores, mask_fill)
    attn_probs = jnp.exp(scores - row_lse)
    grad_values = jnp.einsum(
        "nhqk,nqhe->nkhe",
        attn_probs.astype(jnp.bfloat16),
        grad_out,
        preferred_element_type=jnp.float32,
    )
    grad_probs = jnp.einsum(
        "nqhe,nkhe->nhqk", grad_out, value_rows, preferred_element_type=jnp.float32
    )
    row_delta = jnp.sum(grad_probs * attn_probs, axis=-1, keepdims=True)
    grad_scores = (attn_probs * (grad_probs - row_delta)).astype(jnp.bfloat16)
    grad_queries = jnp.einsum(
        "nhqk,nkhe->nqhe", grad_scores, key_rows, preferred_element_type=jnp.float32
    )
    grad_keys = jnp.einsum(
        "nhqk,nqhe->nkhe", grad_scores, queries, preferred_element_type=jnp.float32
    )
    return (grad_queries, grad_keys, grad_values)


def body(
    x_in,
    memory,
    doc_scores,
    valid_count,
    target_ids,
    target_len,
    mem_len,
    attn_w,
    ffn_in,
    ffn_out,
    ffn_bias,
    norms,
    embedding,
):
    x_here, mem_here = (
        lax.all_to_all(x_in, "slot", split_axis=0, concat_axis=2, tiled=True),
        lax.all_to_all(memory, "slot", split_axis=0, concat_axis=2, tiled=True),
    )
    slots_here, questions, tgt_steps, model_width = x_here.shape
    mem_steps = mem_here.shape[2]
    seq_count = slots_here * questions
    head_dim = model_width // HEADS
    scaling = head_dim ** (-0.5)
    attn_full, in_full, out_full = (
        lax.all_gather(attn_w, ("pb", "slot"), axis=0, tiled=True),
        lax.all_gather(ffn_in, ("pb", "slot"), axis=0, tiled=True),
        lax.all_gather(ffn_out, ("pb", "slot"), axis=0, tiled=True),
    )
    blocks = [
        attn_full[block_index * model_width : (block_index + 1) * model_width]
        for block_index in range(8)
    ]

    def split_heads(value, steps):
        return value.reshape(seq_count, steps, HEADS, head_dim)

    def merge_rows(value):
        return value.reshape(-1, model_width)

    inputs = x_here.reshape(seq_count * tgt_steps, model_width)
    memory_rows = mem_here.reshape(seq_count * mem_steps, model_width)
    positions = jnp.arange(tgt_steps)
    causal = (positions[None, :] <= positions[:, None])[None, None]
    seen = (jnp.arange(mem_steps)[None, None, :] < mem_len[:, :, None]).reshape(
        seq_count, 1, 1, mem_steps
    )
    queries = (product(inputs, blocks[0]) * scaling).astype(jnp.bfloat16)
    key_rows = product(inputs, blocks[1]).astype(jnp.bfloat16)
    value_rows = product(inputs, blocks[2]).astype(jnp.bfloat16)
    self_out, self_lse = attend_forward(
        split_heads(queries, tgt_steps),
        split_heads(key_rows, tgt_steps),
        split_heads(value_rows, tgt_steps),
        causal,
    )
    self_out = merge_rows(self_out).astype(jnp.bfloat16)
    hidden_one, normed_one, root_one = norm_forward(
        inputs.astype(jnp.float32) + product(self_out, blocks[3]), norms[0], norms[1]
    )
    one_low = hidden_one.astype(jnp.bfloat16)
    cross_queries = (product(one_low, blocks[4]) * scaling).astype(jnp.bfloat16)
    cross_keys = product(memory_rows, blocks[5]).astype(jnp.bfloat16)
    cross_values = product(memory_rows, blocks[6]).astype(jnp.bfloat16)
    cross_out, cross_lse = attend_forward(
        split_heads(cross_queries, tgt_steps),
        split_heads(cross_keys, mem_steps),
        split_heads(cross_values, mem_steps),
        seen,
    )
    cross_out = merge_rows(cross_out).astype(jnp.bfloat16)
    hidden_two, normed_two, root_two = norm_forward(
        hidden_one + product(cross_out, blocks[7]), norms[2], norms[3]
    )
    two_low = hidden_two.astype(jnp.bfloat16)
    pre_act = contract_cols(two_low, in_full) + ffn_bias
    act_low = jax.nn.gelu(pre_act, approximate=False).astype(jnp.bfloat16)
    hidden_three, normed_three, root_three = norm_forward(
        hidden_two + product(act_low, out_full), norms[4], norms[5]
    )
    three_low = hidden_three.astype(jnp.bfloat16).reshape(
        slots_here, questions, tgt_steps, model_width
    )
    vocab_here = embedding.shape[0]
    vocab_start = lax.axis_index("slot") * vocab_here
    local_ids = target_ids - vocab_start
    piece = lax.all_gather(three_low, "slot", axis=0, tiled=True)
    flat_rows = piece.reshape(-1, model_width)
    logits = contract_cols(flat_rows, embedding).reshape(
        piece.shape[0], questions, tgt_steps, vocab_here
    )
    rows_all = piece
    onehot = jnp.arange(vocab_here)[None, None, None, :] == local_ids[None, :, :, None]
    row_max = jnp.max(logits, axis=-1)
    row_sum = jnp.sum(jnp.exp(logits - row_max[..., None]), axis=-1)
    target_logit = jnp.sum(jnp.where(onehot, logits, 0.0), axis=-1)

    def merge_stats(first, second):
        joint_max = jnp.maximum(first[0], second[0])
        joint_sum = first[1] * jnp.exp(first[0] - joint_max) + second[1] * jnp.exp(
            second[0] - joint_max
        )
        return (joint_max, joint_sum, first[2] + second[2])

    row_max, row_sum, target_logit = merged((row_max, row_sum, target_logit), "slot", merge_stats)
    log_norm = row_max + jnp.log(row_sum)
    live = positions[None, :] < target_len[:, None]
    lengths = target_len.astype(jnp.float32)
    per_slot = (
        jnp.sum(jnp.where(live[None], target_logit - log_norm, 0.0), axis=2) / lengths[None, :]
    )
    valid = jnp.arange(per_slot.shape[0])[:, None] < valid_count[None, :]
    scores_t = doc_scores.T
    joint = jnp.where(valid, scores_t + per_slot, mask_fill)
    prior = jnp.where(valid, scores_t, mask_fill)
    joint_total = jax.nn.logsumexp(joint, axis=0)
    neg_marginal = jax.nn.logsumexp(prior, axis=0) - joint_total
    log_post = joint - joint_total
    posterior = jnp.exp(log_post)
    entropy_q = -jnp.sum(posterior * log_post, axis=0)
    objective_part = jnp.sum(lengths * (neg_marginal + entropy_weight * entropy_q))
    sum_objective, sum_lengths, sum_entropy = lax.psum(
        (objective_part, jnp.sum(lengths), jnp.sum(entropy_q)), "pb"
    )
    loss = sum_objective / sum_lengths
    entropy = sum_entropy / (questions * lax.axis_size("pb"))
    slot_weight = -posterior * (1.0 + entropy_weight * (log_post + entropy_q[None, :]))
    token_weight = jnp.where(live[None], slot_weight[:, :, None], 0.0)
    soft_probs = jnp.exp(logits - log_norm[..., None])
    grad_logits = (token_weight[..., None] * (onehot.astype(jnp.float32) - soft_probs)).astype(
        jnp.bfloat16
    )
    grad_embed = contract_rows(
        grad_logits.reshape(-1, vocab_here), rows_all.reshape(-1, model_width)
    )
    grad_embed = lax.psum_scatter(
        grad_embed.astype(jnp.bfloat16), "pb", scatter_dimension=1, tiled=True
    ).astype(jnp.float32)
    piece = grad_logits
    grad_three = (
        lax.psum_scatter(
            product(piece.reshape(-1, vocab_here), embedding)
            .reshape(slots_here * lax.axis_size("slot"), questions, tgt_steps, model_width)
            .astype(jnp.bfloat16),
            "slot",
            scatter_dimension=0,
            tiled=True,
        )
        .astype(jnp.float32)
        .reshape(-1, model_width)
    )
    attn_back, in_back, out_back = (
        lax.all_gather(attn_w, ("pb", "slot"), axis=0, tiled=True),
        lax.all_gather(ffn_in, ("pb", "slot"), axis=0, tiled=True),
        lax.all_gather(ffn_out, ("pb", "slot"), axis=0, tiled=True),
    )
    back_blocks = [
        attn_back[block_index * model_width : (block_index + 1) * model_width]
        for block_index in range(8)
    ]
    grad_res_three, gain_three, shift_three = norm_backward(
        grad_three, normed_three, root_three, norms[4]
    )
    grad_ffn = grad_res_three.astype(jnp.bfloat16)
    grad_out_w = contract_rows(act_low, grad_ffn)
    grad_act = contract_cols(grad_ffn, out_back)
    cdf_part = 0.5 * (1.0 + lax.erf(pre_act * root_half))
    pdf_part = pre_act * inv_root_tau * jnp.exp(-0.5 * pre_act * pre_act)
    grad_pre = (grad_act * (cdf_part + pdf_part)).astype(jnp.bfloat16)
    grad_in_w = contract_rows(grad_pre, two_low)
    grad_bias = jnp.sum(grad_pre.astype(jnp.float32), axis=0)
    grad_two = grad_res_three + product(grad_pre, in_back)
    grad_res_two, gain_two, shift_two = norm_backward(grad_two, normed_two, root_two, norms[2])
    grad_cross = grad_res_two.astype(jnp.bfloat16)
    grad_w7 = contract_rows(cross_out, grad_cross)
    grad_cross_out = contract_cols(grad_cross, back_blocks[7]).astype(jnp.bfloat16)
    cq_grad, ck_grad, cv_grad = attend_backward(
        split_heads(cross_queries, tgt_steps),
        split_heads(cross_keys, mem_steps),
        split_heads(cross_values, mem_steps),
        seen,
        cross_lse,
        split_heads(grad_cross_out, tgt_steps),
    )
    cq_grad = merge_rows(cq_grad).astype(jnp.bfloat16)
    ck_grad = merge_rows(ck_grad).astype(jnp.bfloat16)
    cv_grad = merge_rows(cv_grad).astype(jnp.bfloat16)
    grad_w4 = contract_rows(one_low, cq_grad) * scaling
    grad_w5 = contract_rows(memory_rows, ck_grad)
    grad_w6 = contract_rows(memory_rows, cv_grad)
    grad_memory = (
        contract_cols(ck_grad, back_blocks[5]) + contract_cols(cv_grad, back_blocks[6])
    ).astype(jnp.bfloat16)
    grad_one = grad_res_two + contract_cols(cq_grad, back_blocks[4]) * scaling
    grad_res_one, gain_one, shift_one = norm_backward(grad_one, normed_one, root_one, norms[0])
    grad_attn_out = grad_res_one.astype(jnp.bfloat16)
    grad_w3 = contract_rows(self_out, grad_attn_out)
    grad_self_out = contract_cols(grad_attn_out, back_blocks[3]).astype(jnp.bfloat16)
    sq_grad, sk_grad, sv_grad = attend_backward(
        split_heads(queries, tgt_steps),
        split_heads(key_rows, tgt_steps),
        split_heads(value_rows, tgt_steps),
        causal,
        self_lse,
        split_heads(grad_self_out, tgt_steps),
    )
    sq_grad = merge_rows(sq_grad).astype(jnp.bfloat16)
    sk_grad = merge_rows(sk_grad).astype(jnp.bfloat16)
    sv_grad = merge_rows(sv_grad).astype(jnp.bfloat16)
    grad_w0 = contract_rows(inputs, sq_grad) * scaling
    grad_w1 = contract_rows(inputs, sk_grad)
    grad_w2 = contract_rows(inputs, sv_grad)
    grad_inputs = (
        grad_res_one
        + contract_cols(sq_grad, back_blocks[0]) * scaling
        + contract_cols(sk_grad, back_blocks[1])
        + contract_cols(sv_grad, back_blocks[2])
    )
    grad_inputs = grad_inputs.astype(jnp.bfloat16).reshape(
        slots_here, questions, tgt_steps, model_width
    )
    grad_memory = grad_memory.reshape(slots_here, questions, mem_steps, model_width)
    grad_inputs, grad_memory = (
        lax.all_to_all(grad_inputs, "slot", split_axis=2, concat_axis=0, tiled=True),
        lax.all_to_all(grad_memory, "slot", split_axis=2, concat_axis=0, tiled=True),
    )
    grad_attn = jnp.concatenate(
        [grad_w0, grad_w1, grad_w2, grad_w3, grad_w4, grad_w5, grad_w6, grad_w7], axis=0
    )
    grad_attn, grad_in_w, grad_out_w, grad_bias = (
        lax.psum_scatter(grad_attn, ("pb", "slot"), scatter_dimension=0, tiled=True),
        lax.psum_scatter(grad_in_w, ("pb", "slot"), scatter_dimension=0, tiled=True),
        lax.psum_scatter(grad_out_w, ("pb", "slot"), scatter_dimension=0, tiled=True),
        lax.psum_scatter(grad_bias, ("pb", "slot"), scatter_dimension=0, tiled=True),
    )
    grad_norms = lax.psum(
        jnp.stack([gain_one, shift_one, gain_two, shift_two, gain_three, shift_three], axis=0),
        ("pb", "slot"),
    )
    return (
        loss,
        entropy,
        grad_inputs,
        grad_memory,
        grad_attn,
        grad_in_w,
        grad_out_w,
        grad_bias,
        grad_norms,
        grad_embed,
    )


def solution(mesh):
    placed = (
        P(None, "pb", "slot", None),
        P(None, "pb", "slot", None),
        P("pb", None),
        P("pb"),
        P("pb", None),
        P("pb"),
        P("slot", "pb"),
        P(("pb", "slot"), None),
        P(("pb", "slot"), None),
        P(("pb", "slot"), None),
        P(),
        P(),
        P("slot", None),
    )
    return jax.shard_map(
        body,
        mesh=mesh,
        in_specs=placed,
        out_specs=(
            P(),
            P(),
            P(None, "pb", "slot", None),
            P(None, "pb", "slot", None),
            P(("pb", "slot"), None),
            P(("pb", "slot"), None),
            P(("pb", "slot"), None),
            P(("pb", "slot")),
            P(),
            P("slot", "pb"),
        ),
        check_vma=False,
    )
```

profile of v0, /device:TPU:0, one launch (start us, length us, event | category | flops | bytes accessed | tf_op | source)
XLA Modules:
  0.0 2477.1 jit_solution(15302564795332511898)
XLA Ops:
  8.7 43.4 %all_to_all.66 = bf16[8,2,32,1024]{3,2,1,0:T(8,128)(2,1)} all-to-all(bf16[8,2,32,1024]{3,2,1,0:T(8,128)(2,1)} %param.15), channel_id=1, replica_groups=mesh['pb'=8,'slot'=4] {'slot'}, dimensions={0} | all-to-all | bytes 2097152 | tf_op jit(solution)/shard_map/all_to_all | solution.py:111
  59.9 126.7 %all-to-all-done.1 = bf16[8,2,96,1024]{3,2,1,0:T(8,128)(2,1)S(1)} async-done(((bf16[8,2,96,1024]{3,2,1,0:T(8,128)(2,1)}), bf16[8,2,96,1024]{3,2,1,0:T(8,128)(2,1)S(1)}, u32[]{:S(2)}, u32[]{:S(2)}) %all-to-all-start.1) | async-done | bytes 3145760 | tf_op jit(solution)/shard_map/all_to_all | solution.py:112
  292.8 27.4 %fusion.9 = (bf16[512,4096]{1,0:T(8,128)(2,1)}, f32[512,4096]{1,0:T(8,128)}) fusion(f32[4096]{0:T(1024)S(1)} %copy-done.97, bf16[4096,1024]{1,0:T(8,128)(2,1)} %all-gather.10.cloned.1.call-done, f32[512,1024]{1,0:T(8,128)S(1)} %get-tuple-element.113, f32[1024]{0:T(1024)S(1)} %bitcast.308, f32[1024]{0:T(1024)S(1)} %bitcast.295, f32[512]{0:T(512)S(1)} %add_rsqrt_fusion.1, ...), kind=kOutput, calls=%fused_computation.26 | convolution fusion | flops 4436000768 | bytes 23097344 | tf_op jit(solution)/shard_map/dot_general | solution.py:35
  320.2 33.5 %all-gather.12.cloned.1.call-done = bf16[4096,1024]{1,0:T(8,128)(2,1)} async-done(((bf16[128,1024]{1,0:T(8,128)(2,1)}), bf16[4096,1024]{1,0:T(8,128)(2,1)}) %all-gather.12.cloned.1.call-update) | async-done | bytes 8388624 | tf_op jit(solution)/shard_map/all_gather | solution.py:122
  353.7 8.6 fusion.172
  374.4 70.2 %all-gather.14.cloned.1.call-done = bf16[8,2,128,1024]{3,2,1,0:T(8,128)(2,1)} async-done(((bf16[2,2,128,1024]{3,2,1,0:T(8,128)(2,1)}), bf16[8,2,128,1024]{3,2,1,0:T(8,128)(2,1)}) %all-gather.14.cloned.1.call-update) | async-done | bytes 4194320 | tf_op jit(solution)/shard_map/all_gather | solution.py:181
  444.6 65.0 %fusion.173 = (f32[8,2,128]{2,1,0:T(2,128)S(1)}, f32[8,2,128,12544]{3,2,1,0:T(8,128)}) fusion(bf16[8,2,128,1024]{3,2,1,0:T(8,128)(2,1)} %all-gather.14.cloned.1.call-done, bf16[12544,1024]{1,0:T(8,128)(2,1)} %param.27), kind=kOutput, calls=%fused_computation.246 | convolution fusion | flops 52639039488 | bytes 132653056 | tf_op jit(solution)/shard_map/dot_general | solution.py:35
  509.5 13.1 all-gather
  522.7 51.4 %select_reduce_fusion = (f32[8,2,128]{2,1,0:T(2,128)S(1)}, f32[8,2,128]{2,1,0:T(2,128)S(1)}) fusion(f32[8,2,128,12544]{3,2,1,0:T(8,128)} %get-tuple-element.119, pred[2,128,12544]{2,1,0:T(8,128)(4,1)S(1)} %get-tuple-element.104, f32[8,2,128]{2,1,0:T(2,128)S(1)} %get-tuple-element.118), kind=kLoop, calls=%fused_computation.7 | loop fusion | flops 102756352 | bytes 105996288 | tf_op jit(solution)/shard_map/reduce_sum | solution.py:190
  574.1 13.1 all-gather.1
  587.3 13.1 all-gather.2
  602.1 69.1 %fusion.31 = bf16[8,2,128,1024]{3,2,1,0:T(8,128)(2,1)} fusion(bf16[12544,1024]{1,0:T(8,128)(2,1)} %param.27, f32[8,2,128,12544]{3,2,1,0:T(8,128)} %get-tuple-element.119, f32[8,2,128]{2,1,0:T(2,128)S(1)} %get-tuple-element.94, f32[2,128,12544]{2,1,0:T(8,128)} %get-tuple-element.103, f32[8,2,128]{2,1,0:T(2,128)S(1)} %broadcast_select_fusion), kind=kOutput, calls=%fused_computation.73 | convolution fusion | flops 52718206976 | bytes 145506304 | tf_op jit(solution)/shard_map/dot_general | solution.py:25
  671.2 73.0 %bitcast_convert_fusion = bf16[12544,1024]{1,0:T(8,128)(2,1)} fusion(bf16[8,2,128,1024]{3,2,1,0:T(8,128)(2,1)} %all-gather.14.cloned.1.call-done, f32[8,2,128,12544]{3,2,1,0:T(8,128)} %get-tuple-element.119, f32[8,2,128]{2,1,0:T(2,128)S(1)} %get-tuple-element.94, f32[2,128,12544]{2,1,0:T(8,128)} %get-tuple-element.103, f32[8,2,128]{2,1,0:T(2,128)S(1)} %broadcast_select_fusion), kind=kOutput, calls=%fused_computation.9 | convolution fusion | flops 52728954880 | bytes 145506304 | tf_op jit(solution)/shard_map/dot_general | solution.py:29
  744.2 31.0 %copy.186 = bf16[12544,1024]{0,1:T(8,128)(2,1)} copy(bf16[12544,1024]{1,0:T(8,128)(2,1)} %bitcast_convert_fusion) | data formatting | bytes 51380224
  781.9 15.5 convert_reduce_fusion
  799.9 9.9 fusion.161
  809.8 13.3 fusion.148
  823.9 10.7 multiply_reduce_fusion.2
  971.9 34.9 %all-to-all-done.2 = bf16[2,2,128,1024]{3,1,0,2:T(2,128)(2,1)S(1)} async-done(((bf16[2,2,128,1024]{3,1,0,2:T(2,128)(2,1)}), bf16[2,2,128,1024]{3,1,0,2:T(2,128)(2,1)S(1)}, u32[]{:S(2)}, u32[]{:S(2)}) %all-to-all-start.2) | async-done | bytes 1048608 | tf_op jit(solution)/shard_map/all_to_all | solution.py:318
  1014.7 12.7 all-reduce.2
  1029.5 142.5 %all-reduce.1 = (f32[4096]{0:T(1024)S(1)}, f32[6,1024]{1,0:T(8,128)}) all-reduce(f32[4096]{0:T(1024)S(1)} %copy-done.73, f32[6,1024]{1,0:T(8,128)S(1)} %stack.27), channel_id=9, replica_groups=mesh['pb'=8,'slot'=4] {'pb','slot'}, use_global_device_ids=true, to_apply=%region_40.41.clone | all-reduce | flops 10240 | bytes 81920
  1185.4 200.3 %reduce-scatter.12.cloned.1.call-done = f32[128,1024]{1,0:T(8,128)} async-done(((f32[4096,1024]{1,0:T(8,128)}), f32[128,1024]{1,0:T(8,128)}) %reduce-scatter.12.cloned.1.call-update) | async-done | bytes 524304 | tf_op jit(solution)/shard_map/reduce_scatter | solution.py:326
  1385.7 369.6 %reduce-scatter.14.cloned.1.call-done = f32[128,1024]{1,0:T(8,128)} async-done(((f32[4096,1024]{1,0:T(8,128)}), f32[128,1024]{1,0:T(8,128)}) %reduce-scatter.14.cloned.1.call-update) | async-done | bytes 524304 | tf_op jit(solution)/shard_map/reduce_scatter | solution.py:327
  1755.3 712.8 %reduce-scatter.10.cloned.1.call-done = f32[256,1024]{1,0:T(8,128)} async-done(((f32[8192,1024]{1,0:T(8,128)}), f32[256,1024]{1,0:T(8,128)}) %reduce-scatter.10.cloned.1.call-update) | async-done | bytes 1048592 | tf_op jit(solution)/shard_map/reduce_scatter | solution.py:325
  (368 shorter events, 296.1 us)
Async XLA Ops:
  7.2 187.9 %all-gather.8.cloned.1.call-start = ((), (), s32[]{:S(2)}) async-start(), calls=%async_computation.9 | async-start | bytes 17301504 | tf_op jit(solution)/shard_map/all_gather | solution.py:120
  7.9 284.9 %all-gather.10.cloned.1.call-start = ((), (), s32[]{:S(2)}) async-start(), calls=%async_computation.10 | async-start | bytes 8650752 | tf_op jit(solution)/shard_map/all_gather | solution.py:121
  52.0 134.5 %all-to-all-start.1 = ((bf16[8,2,96,1024]{3,2,1,0:T(8,128)(2,1)}), bf16[8,2,96,1024]{3,2,1,0:T(8,128)(2,1)S(1)}, u32[]{:S(2)}, u32[]{:S(2)}) async-start(bf16[8,2,96,1024]{3,2,1,0:T(8,128)(2,1)} %param.16), calls=%async_computation.1 | async-start | bytes 6291456 | tf_op jit(solution)/shard_map/all_to_all | solution.py:112
  56.0 297.7 %all-gather.12.cloned.1.call-start = ((), (), s32[]{:S(2)}) async-start(), calls=%async_computation.11 | async-start | bytes 8650752 | tf_op jit(solution)/shard_map/all_gather | solution.py:122
  56.7 387.9 %all-gather.14.cloned.1.call-start = ((), (), s32[]{:S(2)}) async-start(), calls=%async_computation.12 | async-start | bytes 5242880 | tf_op jit(solution)/shard_map/all_gather | solution.py:181
  56.9 182.9 %copy-start.45 = (pred[128,128]{0,1:T(8,128)(4,1)}, pred[128,128]{0,1:T(8,128)(4,1)S(1)}, u32[]{:S(2)}) copy-start(pred[128,128]{0,1:T(8,128)(4,1)S(1)} %iota_compare_fusion.1) | copy-start | bytes 49156
  57.0 223.8 %copy-start.51 = (pred[4,384]{1,0:T(4,128)(4,1)}, pred[4,384]{1,0:T(4,128)(4,1)S(1)}, u32[]{:S(2)}) copy-start(pred[4,384]{1,0:T(4,128)(4,1)S(1)} %iota_compare_fusion.2) | copy-start | bytes 4612
  57.6 231.3 %copy-start.74 = (f32[1,1024]{1,0:T(1,128)}, f32[1,1024]{1,0:T(1,128)S(1)}, u32[]{:S(2)}) copy-start(f32[1,1024]{1,0:T(1,128)S(1)} %get-tuple-element.100) | copy-start | bytes 12292
  57.6 231.3 %copy-start.82 = (f32[1,1024]{1,0:T(1,128)}, f32[1,1024]{1,0:T(1,128)S(1)}, u32[]{:S(2)}) copy-start(f32[1,1024]{1,0:T(1,128)S(1)} %get-tuple-element.99) | copy-start | bytes 12292
  57.6 296.1 %copy-start.76 = (f32[1,1024]{1,0:T(1,128)}, f32[1,1024]{1,0:T(1,128)S(1)}, u32[]{:S(2)}) copy-start(f32[1,1024]{1,0:T(1,128)S(1)} %get-tuple-element.98) | copy-start | bytes 12292
  57.6 296.1 %copy-start.84 = (f32[1,1024]{1,0:T(1,128)}, f32[1,1024]{1,0:T(1,128)S(1)}, u32[]{:S(2)}) copy-start(f32[1,1024]{1,0:T(1,128)S(1)} %get-tuple-element.97) | copy-start | bytes 12292
  365.1 410.3 %reduce-scatter.8.cloned.1.call-start = ((), (), s32[]{:S(2)}) async-start(), calls=%async_computation.13 | async-start | bytes 5242880 | tf_op jit(solution)/shard_map/reduce_scatter | solution.py:235
  522.7 78.0 %copy-start.62 = (f32[2,8]{0,1:T(8,128)S(1)}, f32[2,8]{0,1:T(8,128)}, u32[]{:S(2)}) copy-start(f32[2,8]{0,1:T(8,128)} %copy-done.61) | copy-start | bytes 196
  522.7 78.0 %copy-start.90 = (s32[2]{0:T(128)S(1)}, s32[2]{0:T(128)}, u32[]{:S(2)}) copy-start(s32[2]{0:T(128)} %param.18) | copy-start | bytes 28
  522.7 78.0 %copy-start.95 = (f32[2]{0:T(128)S(1)}, f32[2]{0:T(128)}, u32[]{:S(2)}) copy-start(f32[2]{0:T(128)} %convert_element_type.186) | copy-start | bytes 28
  522.7 78.0 %copy-start.96 = (f32[2]{0:T(128)S(1)}, f32[2]{0:T(128)}, u32[]{:S(2)}) copy-start(f32[2]{0:T(128)} %is-finite_select_fusion.1) | copy-start | bytes 28
  522.7 78.6 %copy-start.88 = (f32[2]{0:T(128)S(1)}, f32[2]{0:T(128)}, u32[]{:S(2)}) copy-start(f32[2]{0:T(128)} %copy-done.87) | copy-start | bytes 28
  522.7 78.6 %copy-start.94 = (s32[2]{0:T(128)S(1)}, s32[2]{0:T(128)}, u32[]{:S(2)}) copy-start(s32[2]{0:T(128)} %param.20) | copy-start | bytes 28
  671.2 506.7 %reduce-scatter.16.cloned.1.call-start = ((), (), s32[]{:S(2)}) async-start(), calls=%async_computation.17 | async-start | bytes 28901376
  775.3 610.5 %reduce-scatter.12.cloned.1.call-start = ((), (), s32[]{:S(2)}) async-start(), calls=%async_computation.15 | async-start | bytes 17301504 | tf_op jit(solution)/shard_map/reduce_scatter | solution.py:326
  809.8 945.6 %reduce-scatter.14.cloned.1.call-start = ((), (), s32[]{:S(2)}) async-start(), calls=%async_computation.16 | async-start | bytes 17301504 | tf_op jit(solution)/shard_map/reduce_scatter | solution.py:327
  823.1 1645.0 %reduce-scatter.10.cloned.1.call-start = ((), (), s32[]{:S(2)}) async-start(), calls=%async_computation.14 | async-start | bytes 34603008 | tf_op jit(solution)/shard_map/reduce_scatter | solution.py:325
  951.4 55.5 %all-to-all-start.2 = ((bf16[2,2,128,1024]{3,1,0,2:T(2,128)(2,1)}), bf16[2,2,128,1024]{3,1,0,2:T(2,128)(2,1)S(1)}, u32[]{:S(2)}, u32[]{:S(2)}) async-start(bf16[2,2,128,1024]{3,1,0,2:T(2,128)(2,1)} %copy.169), calls=%async_computation.3 | async-start | bytes 2097152 | tf_op jit(solution)/shard_map/all_to_all | solution.py:318
  1007.8 167.3 %all-to-all-start.3 = ((bf16[2,2,384,1024]{3,1,0,2:T(2,128)(2,1)}), bf16[2,2,384,1024]{3,1,0,2:T(2,128)(2,1)S(1)}, u32[]{:S(2)}, u32[]{:S(2)}) async-start(bf16[2,2,384,1024]{3,1,0,2:T(2,128)(2,1)} %copy.175), calls=%async_computation.4 | async-start | bytes 6291456 | tf_op jit(solution)/shard_map/all_to_all | solution.py:319
  (94 other events, 1028.0 us)
Sparse Core Ops, SparseCore 0:
  11.0 184.0 all-gather.7
  198.0 76.4 all-gather.9
  277.4 76.1 all-gather.11
  365.2 79.3 all-gather.13
  671.3 75.1 reduce-scatter.7
  775.4 157.7 reduce-scatter.15
  936.0 449.6 reduce-scatter.11
  1388.6 366.6 reduce-scatter.13
  1758.2 709.8 reduce-scatter.9
where the time goes:
time: 2480 us
  waiting for transfers between devices  1560 us (63%)
  matrix products  420 us (17%)
  blocking collectives  238 us (10%)
  local copies, waits for them, and re-layouts  140 us (6%)
  other arithmetic  87.6 us (4%)
    reduce_scatter x1, waiting for transfers between devices, body(): lax.psum_scatter(grad_attn, ('pb', 'slot'), scatter_dimension=0, tiled=True)  713 us
    reduce_scatter x1, waiting for transfers between devices, body(): lax.psum_scatter(grad_out_w, ('pb', 'slot'), scatter_dimension=0, tiled=T...  370 us
    reduce_scatter x1, waiting for transfers between devices, body(): lax.psum_scatter(grad_in_w, ('pb', 'slot'), scatter_dimension=0, tiled=True)  200 us
    unnamed x1, blocking collectives  143 us
    dot_general x11, matrix products, contract_cols(): lax.dot_general(left, right, (((1,), (1,)), ((), ())), preferred_element_...  139 us
    all_to_all x1, waiting for transfers between devices, body(): lax.all_to_all(memory, 'slot', split_axis=0, concat_axis=2, tiled=True)  127 us
    dot_general x11, matrix products, contract_rows(): lax.dot_general(left, right, (((0,), (0,)), ((), ())), preferred_element_...  127 us
    dot_general x11, matrix products, product(): return jnp.dot(left, right, preferred_element_type=jnp.float32)  120 us
  transfers between devices with their start and end apart: 12, of which 8 were waited for; matrix products, arithmetic and copies ran while one was open for 18% of the time, Pallas kernels for 0%

commit v1 on v0

--- a/solution.py
+++ b/solution.py
@@ -14,11 +14,158 @@
 
 
 def merged(value, axis, join):
-    pieces = jax.tree.map(lambda part: lax.all_gather(part, axis), value)
+    size = lax.axis_size(axis)
+    packed = jnp.stack(value)
+    me = lax.axis_index(axis)
+    parts = jnp.stack([packed] + [shifted(packed, axis, step) for step in range(1, size)])
+    parts = parts[(me - jnp.arange(size)) % size]
+    pieces = tuple(parts[:, i] for i in range(len(value)))
     head = jax.tree.map(lambda part: part[0], pieces)
     tail = jax.tree.map(lambda part: part[1:], pieces)
     running, _ = lax.scan(lambda running, section: (join(running, section), None), head, tail)
     return running
+
+
+def grid_of(n_pb):
+    cores = 2 if n_pb % 2 == 0 else 1
+    chips = n_pb // cores
+    wide = max(d for d in range(1, chips + 1) if chips % d == 0 and d * d <= chips)
+    return chips // wide, wide, cores
+
+
+def shifted(value, axis, step):
+    if axis == "slot":
+        size = lax.axis_size("slot")
+        return lax.ppermute(value, "slot", [(i, (i + step) % size) for i in range(size)])
+    n_pb = lax.axis_size("pb")
+    tall, wide, cores = grid_of(n_pb)
+    pairs = []
+    for i in range(n_pb):
+        y, x, c = i // (wide * cores), i // cores % wide, i % cores
+        if axis == "y":
+            y = (y + step) % tall
+        elif axis == "x":
+            x = (x + step) % wide
+        else:
+            c = (c + step) % cores
+        pairs.append((i, (y * wide + x) * cores + c))
+    return lax.ppermute(value, "pb", pairs)
+
+
+def place_of(axis):
+    if axis == "slot":
+        return lax.axis_index("slot"), lax.axis_size("slot")
+    tall, wide, cores = grid_of(lax.axis_size("pb"))
+    i = lax.axis_index("pb")
+    if axis == "y":
+        return i // (wide * cores), tall
+    if axis == "x":
+        return i // cores % wide, wide
+    return i % cores, cores
+
+
+def pick(value, index, dim):
+    return lax.dynamic_index_in_dim(value, index, dim, keepdims=False)
+
+
+def ring_gather(value, axis):
+    me, size = place_of(axis)
+    found = [(me, value)]
+    for step in range(1, size):
+        value = shifted(value, axis, 1)
+        found.append(((me - step) % size, value))
+    return found
+
+
+def ring_scatter(value, axis, dim):
+    me, size = place_of(axis)
+    total = pick(value, (me - 1) % size, dim).astype(jnp.bfloat16)
+    for step in range(1, size):
+        part = pick(value, (me - 1 - step) % size, dim)
+        total = shifted(total, axis, 1).astype(jnp.float32) + part.astype(jnp.float32)
+        if step < size - 1:
+            total = total.astype(jnp.bfloat16)
+    return total
+
+
+def gather_all(shard):
+    tall, wide, cores = grid_of(lax.axis_size("pb"))
+    rows, width = shard.shape
+    slots = lax.axis_size("slot")
+    column = jnp.zeros((slots, rows, width), shard.dtype)
+    for index, block in ring_gather(shard, "slot"):
+        column = lax.dynamic_update_index_in_dim(column, block, index, 0)
+    column = column.reshape(slots * rows, width)
+    half = slots * rows // 2
+    core, _ = place_of("core")
+    whole = jnp.zeros((tall * wide, cores, 2, half, width), shard.dtype)
+    for side, (first, second) in enumerate((("x", "y"), ("y", "x"))):
+        part = column[side * half : (side + 1) * half]
+        for at_first, block in ring_gather(part, first):
+            for at_second, block in ring_gather(block, second):
+                x, y = (at_first, at_second) if first == "x" else (at_second, at_first)
+                for at_core, block in ring_gather(block, "core"):
+                    whole = lax.dynamic_update_slice(
+                        whole, block[None, None, None], (y * wide + x, at_core, side, 0, 0)
+                    )
+    return whole.reshape(tall * wide * cores, slots * rows, width)
+
+
+def scatter_pb(value):
+    tall, wide, cores = grid_of(lax.axis_size("pb"))
+    rest = value.shape[1:]
+    value = value.reshape((tall * wide, cores) + rest)
+    value = ring_scatter(value, "core", 1).astype(jnp.bfloat16)
+    value = value.reshape((tall, wide) + rest)
+    half = rest[0] // 2
+    first = ring_scatter(value[:, :, :half], "x", 1)
+    second = ring_scatter(value[:, :, half:], "y", 0)
+    first = ring_scatter(first.astype(jnp.bfloat16), "y", 0)
+    second = ring_scatter(second.astype(jnp.bfloat16), "x", 0)
+    return jnp.concatenate([first, second], axis=0)
+
+
+def scatter_all(value):
+    n_pb, slots = lax.axis_size("pb"), lax.axis_size("slot")
+    rows = value.shape[0] // (n_pb * slots)
+    value = value.reshape((n_pb, slots, rows) + value.shape[1:])
+    column = scatter_pb(value)
+    return ring_scatter(column.astype(jnp.bfloat16), "slot", 0)
+
+
+def sum_all(value, axes):
+    for axis in axes:
+        me, size = place_of(axis)
+        parts = [value] + [shifted(value, axis, step) for step in range(1, size)]
+        placed = jnp.stack(parts)
+        value = jnp.sum(placed[(me - jnp.arange(size)) % size], axis=0)
+    return value
+
+
+def to_slots(value):
+    me, size = place_of("slot")
+    every, questions, steps, width = value.shape
+    chunks = value.reshape(size, every // size, questions, steps, width)
+    result = jnp.zeros((every // size, questions, size, steps, width), value.dtype)
+    for step in range(size):
+        block = pick(chunks, (me + step) % size, 0)
+        if step:
+            block = shifted(block, "slot", step)
+        result = lax.dynamic_update_index_in_dim(result, block, (me - step) % size, 2)
+    return result.reshape(every // size, questions, size * steps, width)
+
+
+def to_positions(value):
+    me, size = place_of("slot")
+    own, questions, steps, width = value.shape
+    chunks = value.reshape(own, questions, size, steps // size, width)
+    result = jnp.zeros((size, own, questions, steps // size, width), value.dtype)
+    for step in range(size):
+        block = pick(chunks, (me + step) % size, 2)
+        if step:
+            block = shifted(block, "slot", step)
+        result = lax.dynamic_update_index_in_dim(result, block, (me - step) % size, 0)
+    return result.reshape(size * own, questions, steps // size, width)
 
 
 def product(left, right):
@@ -108,8 +255,8 @@
     embedding,
 ):
     x_here, mem_here = (
-        lax.all_to_all(x_in, "slot", split_axis=0, concat_axis=2, tiled=True),
-        lax.all_to_all(memory, "slot", split_axis=0, concat_axis=2, tiled=True),
+        to_slots(x_in),
+        to_slots(memory),
     )
     slots_here, questions, tgt_steps, model_width = x_here.shape
     mem_steps = mem_here.shape[2]
@@ -117,9 +264,9 @@
     head_dim = model_width // HEADS
     scaling = head_dim ** (-0.5)
     attn_full, in_full, out_full = (
-        lax.all_gather(attn_w, ("pb", "slot"), axis=0, tiled=True),
-        lax.all_gather(ffn_in, ("pb", "slot"), axis=0, tiled=True),
-        lax.all_gather(ffn_out, ("pb", "slot"), axis=0, tiled=True),
+        gather_all(attn_w).reshape(-1, model_width),
+        gather_all(ffn_in).reshape(-1, model_width),
+        gather_all(ffn_out).reshape(-1, model_width),
     )
     blocks = [
         attn_full[block_index * model_width : (block_index + 1) * model_width]
@@ -178,7 +325,11 @@
     vocab_here = embedding.shape[0]
     vocab_start = lax.axis_index("slot") * vocab_here
     local_ids = target_ids - vocab_start
-    piece = lax.all_gather(three_low, "slot", axis=0, tiled=True)
+    slot_count = lax.axis_size("slot")
+    piece = jnp.zeros((slot_count,) + three_low.shape, three_low.dtype)
+    for index, block in ring_gather(three_low, "slot"):
+        piece = lax.dynamic_update_index_in_dim(piece, block, index, 0)
+    piece = piece.reshape((-1,) + three_low.shape[1:])
     flat_rows = piece.reshape(-1, model_width)
     logits = contract_cols(flat_rows, embedding).reshape(
         piece.shape[0], questions, tgt_steps, vocab_here
@@ -227,31 +378,20 @@
     grad_embed = contract_rows(
         grad_logits.reshape(-1, vocab_here), rows_all.reshape(-1, model_width)
     )
-    grad_embed = lax.psum_scatter(
-        grad_embed.astype(jnp.bfloat16), "pb", scatter_dimension=1, tiled=True
-    ).astype(jnp.float32)
+    grad_embed = scatter_pb(
+        grad_embed.astype(jnp.bfloat16)
+        .reshape(vocab_here, lax.axis_size("pb"), -1)
+        .transpose(1, 0, 2)
+    )
     piece = grad_logits
-    grad_three = (
-        lax.psum_scatter(
-            product(piece.reshape(-1, vocab_here), embedding)
-            .reshape(slots_here * lax.axis_size("slot"), questions, tgt_steps, model_width)
-            .astype(jnp.bfloat16),
-            "slot",
-            scatter_dimension=0,
-            tiled=True,
-        )
-        .astype(jnp.float32)
-        .reshape(-1, model_width)
-    )
-    attn_back, in_back, out_back = (
-        lax.all_gather(attn_w, ("pb", "slot"), axis=0, tiled=True),
-        lax.all_gather(ffn_in, ("pb", "slot"), axis=0, tiled=True),
-        lax.all_gather(ffn_out, ("pb", "slot"), axis=0, tiled=True),
-    )
-    back_blocks = [
-        attn_back[block_index * model_width : (block_index + 1) * model_width]
-        for block_index in range(8)
-    ]
+    grad_three = ring_scatter(
+        product(piece.reshape(-1, vocab_here), embedding)
+        .astype(jnp.bfloat16)
+        .reshape(slot_count, -1, model_width),
+        "slot",
+        0,
+    )
+    back_blocks, in_back, out_back = blocks, in_full, out_full
     grad_res_three, gain_three, shift_three = norm_backward(
         grad_three, normed_three, root_three, norms[4]
     )
@@ -315,21 +455,32 @@
     )
     grad_memory = grad_memory.reshape(slots_here, questions, mem_steps, model_width)
     grad_inputs, grad_memory = (
-        lax.all_to_all(grad_inputs, "slot", split_axis=2, concat_axis=0, tiled=True),
-        lax.all_to_all(grad_memory, "slot", split_axis=2, concat_axis=0, tiled=True),
+        to_positions(grad_inputs),
+        to_positions(grad_memory),
     )
     grad_attn = jnp.concatenate(
         [grad_w0, grad_w1, grad_w2, grad_w3, grad_w4, grad_w5, grad_w6, grad_w7], axis=0
     )
-    grad_attn, grad_in_w, grad_out_w, grad_bias = (
-        lax.psum_scatter(grad_attn, ("pb", "slot"), scatter_dimension=0, tiled=True),
-        lax.psum_scatter(grad_in_w, ("pb", "slot"), scatter_dimension=0, tiled=True),
-        lax.psum_scatter(grad_out_w, ("pb", "slot"), scatter_dimension=0, tiled=True),
-        lax.psum_scatter(grad_bias, ("pb", "slot"), scatter_dimension=0, tiled=True),
-    )
-    grad_norms = lax.psum(
-        jnp.stack([gain_one, shift_one, gain_two, shift_two, gain_three, shift_three], axis=0),
-        ("pb", "slot"),
+    grad_attn, grad_in_w, grad_out_w = (
+        scatter_all(grad_attn),
+        scatter_all(grad_in_w),
+        scatter_all(grad_out_w),
+    )
+    small = jnp.concatenate(
+        [
+            jnp.stack([gain_one, shift_one, gain_two, shift_two, gain_three, shift_three], axis=0),
+            grad_bias.reshape(-1, model_width),
+        ],
+        axis=0,
+    )
+    small = sum_all(small, ("core", "x", "y", "slot"))
+    grad_norms = small[:6]
+    grad_bias = small[6:].reshape(-1)
+    own_bias = grad_bias.shape[0] // (lax.axis_size("pb") * slot_count)
+    grad_bias = lax.dynamic_slice_in_dim(
+        grad_bias,
+        (lax.axis_index("pb") * slot_count + lax.axis_index("slot")) * own_bias,
+        own_bias,
     )
     return (
         loss,

time: 2480 us -> 1530 us (0.62)
  waiting for transfers between devices: 1560 us -> 480 us
  blocking collectives: 238 us -> 27.1 us
  starting transfers between devices: 14.4 us -> 160 us
  other arithmetic: 87.6 us -> 197 us
  local copies, waits for them, and re-layouts: 140 us -> 246 us
    reduce_scatter x4 -> x0, waiting for transfers between devices: 1280 us -> none  [the longest x1 713 us: body(): lax.psum_scatter(grad_attn, ('pb', 'slot'), scatter_dimension=0, tiled=True)]
    ppermute x0 -> x107, waiting for transfers between devices: none -> 480 us  [the longest x65 301 us: shifted(): return lax.ppermute(value, 'pb', pairs)]
    all_to_all x3 -> x0, waiting for transfers between devices: 162 us -> none  [the longest x1 127 us: body(): lax.all_to_all(memory, 'slot', split_axis=0, concat_axis=2, tiled=True)]
    ppermute x0 -> x107, starting transfers between devices: none -> 160 us  [the longest x42 128 us: shifted(): lax.ppermute(value, 'slot', [(i, (i + step) % size) for i in range(size)])]
    unnamed x1 -> x0, blocking collectives: 143 us -> none
    all_gather x4 -> x0, waiting for transfers between devices: 110 us -> none  [the longest x1 70.2 us: body(): piece = lax.all_gather(three_low, 'slot', axis=0, tiled=True)]
    convert_element_type x1 -> x21, other arithmetic: 2.97 us -> 102 us  [the longest x1 53.6 us: body(): (token_weight[..., None] * (onehot.astype(jnp.float32) - soft_probs)).ast...]
    all_to_all x1 -> x0, blocking collectives: 43.4 us -> none  [body(): lax.all_to_all(x_in, 'slot', split_axis=0, concat_axis=2, tiled=True)]
  transfers between devices with their start and end apart: 12 -> 107, of which waited for: 8 -> 48; matrix products, arithmetic and copies ran while one was open for 18% -> 30% of each run, Pallas kernels for 0% -> 0%
where the time goes in v1:
time: 1530 us; the launch traced here: 1520 us
  waiting for transfers between devices  480 us (31%)
  matrix products  404 us (26%)
  local copies, waits for them, and re-layouts  246 us (16%)
  other arithmetic  197 us (13%)
  starting transfers between devices  160 us (10%)
  blocking collectives  27.1 us (2%)
    ppermute x65, waiting for transfers between devices, shifted(): return lax.ppermute(value, 'pb', pairs)  301 us
    ppermute x42, waiting for transfers between devices, shifted(): lax.ppermute(value, 'slot', [(i, (i + step) % size) for i in range(size)])  179 us
    dot_general x11, matrix products, contract_cols(): lax.dot_general(left, right, (((1,), (1,)), ((), ())), preferred_element_...  139 us
    ppermute x42, starting transfers between devices, shifted(): lax.ppermute(value, 'slot', [(i, (i + step) % size) for i in range(size)])  128 us
    dot_general x11, matrix products, contract_rows(): lax.dot_general(left, right, (((0,), (0,)), ((), ())), preferred_element_...  117 us
    dot_general x11, matrix products, product(): return jnp.dot(left, right, preferred_element_type=jnp.float32)  107 us
    reshape x16, local copies, waits for them, and re-layouts, split_heads(): return value.reshape(seq_count, steps, HEADS, head_dim)  66.9 us
    convert_element_type x1, other arithmetic, body(): (token_weight[..., None] * (onehot.astype(jnp.float32) - soft_probs)).ast...  53.6 us
  transfers between devices with their start and end apart: 107, of which 48 were waited for; matrix products, arithmetic and copies ran while one was open for 30% of the time, Pallas kernels for 0%

profile of v1, /device:TPU:0, one launch (start us, length us, event | category | flops | bytes accessed | tf_op | source)
XLA Modules:
  0.0 1523.6 jit_solution(2552343442910626705)
XLA Ops:
  53.4 25.9 %collective-permute-start.21 = (bf16[2,2,96,1024]{3,2,1,0:T(8,128)(2,1)}, bf16[2,2,96,1024]{3,2,1,0:T(8,128)(2,1)}, u32[]{:S(2)}, u32[]{:S(2)}) collective-permute-start(bf16[2,2,96,1024]{3,2,1,0:T(8,128)(2,1)} %get-tuple-element.136), channel_id=1, source_target_pairs={{0,2},{1,3},{2,0},{3,1},{4,6},{5,7},{6,4},{7,5},{8,10},{9,11},{10,... | collective-permute-start | bytes 2359304 | tf_op jit(solution)/shard_map/ppermute | solution.py:39
  86.7 20.4 %collective-permute-done.25 = bf16[128,1024]{1,0:T(8,128)(2,1)S(1)} collective-permute-done((bf16[128,1024]{1,0:T(8,128)(2,1)S(1)}, bf16[128,1024]{1,0:T(8,128)(2,1)S(1)}, u32[]{:S(2)}, u32[]{:S(2)}) %collective-permute-start.25) | collective-permute-done | bytes 262176 | tf_op jit(solution)/shard_map/ppermute | solution.py:39
  107.1 30.3 %collective-permute-start.4 = (bf16[256,1024]{1,0:T(8,128)(2,1)}, bf16[256,1024]{1,0:T(8,128)(2,1)}, u32[]{:S(2)}, u32[]{:S(2)}) collective-permute-start(bf16[256,1024]{1,0:T(8,128)(2,1)} %collective-permute-done.3), channel_id=1, source_target_pairs={{0,1},{1,2},{2,3},{3,0},{4,5},{5,6},{6,7},{7,4},{8,9},{9,10},{10,1... | collective-permute-start | bytes 1572872 | tf_op jit(solution)/shard_map/ppermute | solution.py:39
  250.9 19.2 %collective-permute-done.9 = bf16[512,1024]{1,0:T(8,128)(2,1)S(1)} collective-permute-done((bf16[512,1024]{1,0:T(8,128)(2,1)S(1)}, bf16[512,1024]{1,0:T(8,128)(2,1)S(1)}, u32[]{:S(2)}, u32[]{:S(2)}) %collective-permute-start.9) | collective-permute-done | bytes 1048608 | tf_op jit(solution)/shard_map/ppermute | solution.py:52
  275.6 21.5 %collective-permute-done.11 = bf16[512,1024]{1,0:T(8,128)(2,1)S(1)} collective-permute-done((bf16[512,1024]{1,0:T(8,128)(2,1)S(1)}, bf16[512,1024]{1,0:T(8,128)(2,1)S(1)}, u32[]{:S(2)}, u32[]{:S(2)}) %collective-permute-start.11) | collective-permute-done | bytes 1048608 | tf_op jit(solution)/shard_map/ppermute | solution.py:52
  298.3 18.6 %collective-permute-done.18 = bf16[512,1024]{1,0:T(8,128)(2,1)S(1)} collective-permute-done((bf16[512,1024]{1,0:T(8,128)(2,1)S(1)}, bf16[512,1024]{1,0:T(8,128)(2,1)S(1)}, u32[]{:S(2)}, u32[]{:S(2)}) %collective-permute-start.18) | collective-permute-done | bytes 1048608 | tf_op jit(solution)/shard_map/ppermute | solution.py:52
  429.2 25.3 %fusion.11 = (bf16[512,4096]{1,0:T(8,128)(2,1)S(1)}, f32[512,4096]{1,0:T(8,128)}) fusion(f32[4096]{0:T(1024)S(1)} %copy-done.129, bf16[4096,1024]{1,0:T(8,128)(2,1)S(1)} %bitcast.653, f32[512,1024]{1,0:T(8,128)S(1)} %get-tuple-element.175, f32[1024]{0:T(1024)S(1)} %bitcast.745, f32[1024]{0:T(1024)S(1)} %bitcast.737, f32[512]{0:T(512)S(1)} %add_rsqrt_fusion.1, ...), kind=kOutput, calls=%fused_computation.38 | convolution fusion | flops 4436000768 | bytes 23097344 | tf_op jit(solution)/shard_map/dot_general | solution.py:182
  464.4 23.9 %collective-permute-done.57 = bf16[2,2,128,1024]{3,2,1,0:T(8,128)(2,1)} collective-permute-done((bf16[2,2,128,1024]{3,2,1,0:T(8,128)(2,1)S(1)}, bf16[2,2,128,1024]{3,2,1,0:T(8,128)(2,1)}, u32[]{:S(2)}, u32[]{:S(2)}) %collective-permute-start.57) | collective-permute-done | bytes 1048608 | tf_op jit(solution)/shard_map/ppermute | solution.py:39
  497.1 17.7 %collective-permute-done.58 = bf16[2,2,128,1024]{3,2,1,0:T(8,128)(2,1)} collective-permute-done((bf16[2,2,128,1024]{3,2,1,0:T(8,128)(2,1)}, bf16[2,2,128,1024]{3,2,1,0:T(8,128)(2,1)}, u32[]{:S(2)}, u32[]{:S(2)}) %collective-permute-start.58) | collective-permute-done | bytes 1048608 | tf_op jit(solution)/shard_map/ppermute | solution.py:39
  542.6 65.4 %fusion.236 = (f32[8,2,128]{2,1,0:T(2,128)S(1)}, f32[8,2,128,12544]{3,2,1,0:T(8,128)}) fusion(bf16[8,2,128,1024]{3,2,1,0:T(8,128)(2,1)} %bitcast.104, bf16[12544,1024]{1,0:T(8,128)(2,1)} %param.27), kind=kOutput, calls=%fused_computation.525 | convolution fusion | flops 52639039488 | bytes 132653056 | tf_op jit(solution)/shard_map/dot_general | solution.py:182
  608.1 48.0 %exponential_reduce_fusion = (f32[8,2,128]{2,1,0:T(2,128)S(1)}, f32[8,2,128]{2,1,0:T(2,128)S(1)}) fusion(f32[8,2,128,12544]{3,2,1,0:T(8,128)} %get-tuple-element.181, f32[8,2,128]{2,1,0:T(2,128)S(1)} %get-tuple-element.180, pred[2,128,12544]{2,1,0:T(8,128)(4,1)S(1)} %get-tuple-element.166), kind=kLoop, calls=%fused_computation.17 | loop fusion | flops 102756352 | bytes 105996288 | tf_op jit(solution)/shard_map/reduce_sum | solution.py:340
  665.1 53.6 %multiply_convert_fusion = bf16[8,2,128,12544]{3,2,1,0:T(8,128)(2,1)} fusion(f32[8,2,128,12544]{3,2,1,0:T(8,128)} %get-tuple-element.181, f32[8,2,128]{2,1,0:T(2,128)S(1)} %get-tuple-element.120, f32[2,128,12544]{2,1,0:T(8,128)} %get-tuple-element.165, f32[8,2,128]{2,1,0:T(2,128)S(1)} %broadcast_select_fusion), kind=kLoop, calls=%fused_computation.15 | loop fusion | flops 102760448 | bytes 167002112 | tf_op jit(solution)/shard_map/convert_element_type | solution.py:375
  718.8 59.5 %convolution_convert_fusion.1 = bf16[2048,1024]{1,0:T(8,128)(2,1)S(1)} fusion(bf16[2048,12544]{1,0:T(8,128)(2,1)} %bitcast.613, bf16[12544,1024]{1,0:T(8,128)(2,1)} %param.27), kind=kOutput, calls=%fused_computation.92 | convolution fusion | flops 52615446528 | bytes 81264640 | tf_op jit(solution)/shard_map/dot_general | solution.py:172
  785.6 17.7 %collective-permute-done.63 = bf16[512,1024]{1,0:T(8,128)(2,1)S(1)} collective-permute-done((bf16[512,1024]{1,0:T(8,128)(2,1)S(1)}, bf16[512,1024]{1,0:T(8,128)(2,1)S(1)}, u32[]{:S(2)}, u32[]{:S(2)}) %collective-permute-start.63) | collective-permute-done | bytes 1048608 | tf_op jit(solution)/shard_map/ppermute | solution.py:39
  805.5 61.6 %convolution_convert_fusion = bf16[12544,1024]{0,1:T(8,128)(2,1)} fusion(bf16[2048,12544]{1,0:T(8,128)(2,1)} %bitcast.614, bf16[2048,1024]{1,0:T(8,128)(2,1)} %bitcast.218), kind=kOutput, calls=%fused_computation.22 | convolution fusion | flops 52626194432 | bytes 81264640 | tf_op jit(solution)/shard_map/dot_general | solution.py:176
  869.9 17.3 %constant_dynamic-slice_fusion.3 = (bf16[4,1,12544,128]{2,3,1,0:T(8,128)(2,1)}, bf16[4,1,12544,128]{2,3,1,0:T(8,128)(2,1)}) fusion(bf16[4,2,12544,128]{2,3,1,0:T(8,128)(2,1)} %bitcast.619, s32[]{:T(128)S(6)} %select_n.906, s32[]{:T(128)S(6)} %select_n.888), kind=kLoop, calls=%fused_computation.420 | loop fusion | bytes 51380232 | tf_op jit(solution)/shard_map/jit(dynamic_index_in_dim)/dynamic_slice | solution.py:68
  887.2 17.6 %copy.241 = bf16[4,1,12544,128]{3,2,0,1:T(8,128)(2,1)} copy(bf16[4,1,12544,128]{2,3,1,0:T(8,128)(2,1)} %get-tuple-element.123) | data formatting | bytes 25690112 | tf_op jit(solution)/shard_map/jit(dynamic_index_in_dim)/dynamic_slice | solution.py:68
  905.4 27.1 %all-reduce = (f32[]{:T(128)}, f32[]{:T(128)}, f32[]{:T(128)}) all-reduce(f32[]{:T(128)} %get-tuple-element.97, f32[]{:T(128)} %get-tuple-element.96, f32[]{:T(128)S(6)} %neg.17), channel_id=1, replica_groups=mesh['pb'=8,'slot'=4] {'pb'}, use_global_device_ids=true, to_apply=%region_22.23 | all-reduce | flops 3 | bytes 24 | tf_op jit(solution)/shard_map/psum | solution.py:367
  932.5 17.7 %copy.273 = bf16[4,1,12544,128]{3,2,0,1:T(8,128)(2,1)} copy(bf16[4,1,12544,128]{2,3,1,0:T(8,128)(2,1)} %get-tuple-element.122) | data formatting | bytes 25690112
  1287.3 22.9 %collective-permute-done.93 = bf16[128,1024]{1,0:T(8,128)(2,1)S(1)} collective-permute-done((bf16[128,1024]{1,0:T(8,128)(2,1)S(1)}, bf16[128,1024]{1,0:T(8,128)(2,1)S(1)}, u32[]{:S(2)}, u32[]{:S(2)}) %collective-permute-start.93) | collective-permute-done | bytes 262176 | tf_op jit(solution)/shard_map/ppermute | solution.py:39
  1345.6 23.9 %collective-permute-done.75 = bf16[2,2,256,1024]{3,2,1,0:T(8,128)(2,1)} collective-permute-done((bf16[2,2,256,1024]{3,2,1,0:T(8,128)(2,1)}, bf16[2,2,256,1024]{3,2,1,0:T(8,128)(2,1)}, u32[]{:S(2)}, u32[]{:S(2)}) %collective-permute-start.75) | collective-permute-done | bytes 2097184 | tf_op jit(solution)/shard_map/ppermute | solution.py:52
  1385.9 16.6 %collective-permute-done.76 = bf16[2,256,1024]{2,1,0:T(8,128)(2,1)S(1)} collective-permute-done((bf16[2,256,1024]{2,1,0:T(8,128)(2,1)S(1)}, bf16[2,256,1024]{2,1,0:T(8,128)(2,1)S(1)}, u32[]{:S(2)}, u32[]{:S(2)}) %collective-permute-start.76) | collective-permute-done | bytes 1048608 | tf_op jit(solution)/shard_map/ppermute | solution.py:52
  1437.7 27.1 %collective-permute-done.103 = bf16[2,6272,128]{2,1,0:T(8,128)(2,1)S(1)} collective-permute-done((bf16[2,6272,128]{2,1,0:T(8,128)(2,1)S(1)}, bf16[2,6272,128]{2,1,0:T(8,128)(2,1)S(1)}, u32[]{:S(2)}, u32[]{:S(2)}) %collective-permute-start.103) | collective-permute-done | bytes 3211296 | tf_op jit(solution)/shard_map/ppermute | solution.py:52
  1466.7 26.8 %collective-permute-done.105 = bf16[2,6272,128]{2,1,0:T(8,128)(2,1)S(1)} collective-permute-done((bf16[2,6272,128]{2,1,0:T(8,128)(2,1)S(1)}, bf16[2,6272,128]{2,1,0:T(8,128)(2,1)S(1)}, u32[]{:S(2)}, u32[]{:S(2)}) %collective-permute-start.105) | collective-permute-done | bytes 3211296 | tf_op jit(solution)/shard_map/ppermute | solution.py:52
  (830 shorter events, 809.0 us)
Async XLA Ops:
  5.3 76.5 %collective-permute-start.3 = (bf16[256,1024]{1,0:T(8,128)(2,1)}, bf16[256,1024]{1,0:T(8,128)(2,1)}, u32[]{:S(2)}, u32[]{:S(2)}) collective-permute-start(bf16[256,1024]{1,0:T(8,128)(2,1)} %param.22), channel_id=1, source_target_pairs={{0,1},{1,2},{2,3},{3,0},{4,5},{5,6},{6,7},{7,4},{8,9},{9,10},{10,1... | collective-permute-start | bytes 1572872 | tf_op jit(solution)/shard_map/ppermute | solution.py:39
  26.9 115.7 %collective-permute-start.20 = (bf16[2,2,96,1024]{3,2,1,0:T(8,128)(2,1)}, bf16[2,2,96,1024]{3,2,1,0:T(8,128)(2,1)S(1)}, u32[]{:S(2)}, u32[]{:S(2)}) collective-permute-start(bf16[2,2,96,1024]{3,2,1,0:T(8,128)(2,1)} %get-tuple-element.137), channel_id=1, source_target_pairs={{0,1},{1,2},{2,3},{3,0},{4,5},{5,6},{6,7},{7,4},{8,9},{9,10},{10,1... | collective-permute-start | bytes 2359304 | tf_op jit(solution)/shard_map/ppermute | solution.py:39
  35.8 45.2 %collective-permute-start.41 = (bf16[128,1024]{1,0:T(8,128)(2,1)}, bf16[128,1024]{1,0:T(8,128)(2,1)S(1)}, u32[]{:S(2)}, u32[]{:S(2)}) collective-permute-start(bf16[128,1024]{1,0:T(8,128)(2,1)} %collective-permute-done.40), channel_id=1, source_target_pairs={{0,1},{1,2},{2,3},{3,0},{4,5},{5,6},{6,7},{7,4},{8,9},{9,10},{10,1... | collective-permute-start | bytes 786440 | tf_op jit(solution)/shard_map/ppermute | solution.py:39
  53.4 91.7 %collective-permute-start.21 = (bf16[2,2,96,1024]{3,2,1,0:T(8,128)(2,1)}, bf16[2,2,96,1024]{3,2,1,0:T(8,128)(2,1)}, u32[]{:S(2)}, u32[]{:S(2)}) collective-permute-start(bf16[2,2,96,1024]{3,2,1,0:T(8,128)(2,1)} %get-tuple-element.136), channel_id=1, source_target_pairs={{0,2},{1,3},{2,0},{3,1},{4,6},{5,7},{6,4},{7,5},{8,10},{9,11},{10,... | collective-permute-start | bytes 2359304 | tf_op jit(solution)/shard_map/ppermute | solution.py:39
  81.0 56.3 %collective-permute-start.42 = (bf16[128,1024]{1,0:T(8,128)(2,1)S(1)}, bf16[128,1024]{1,0:T(8,128)(2,1)S(1)}, u32[]{:S(2)}, u32[]{:S(2)}) collective-permute-start(bf16[128,1024]{1,0:T(8,128)(2,1)S(1)} %collective-permute-done.41), channel_id=1, source_target_pairs={{0,1},{1,2},{2,3},{3,0},{4,5},{5,6},{6,7},{7,4},{8,9},{9,10},{10,1... | collective-permute-start | bytes 786440 | tf_op jit(solution)/shard_map/ppermute | solution.py:39
  81.8 66.7 %collective-permute-start.22 = (bf16[2,2,96,1024]{3,2,1,0:T(8,128)(2,1)}, bf16[2,2,96,1024]{3,2,1,0:T(8,128)(2,1)}, u32[]{:S(2)}, u32[]{:S(2)}) collective-permute-start(bf16[2,2,96,1024]{3,2,1,0:T(8,128)(2,1)} %get-tuple-element.135), channel_id=1, source_target_pairs={{0,3},{1,0},{2,1},{3,2},{4,7},{5,4},{6,5},{7,6},{8,11},{9,8},{10,9... | collective-permute-start | bytes 2359304 | tf_op jit(solution)/shard_map/ppermute | solution.py:39
  107.1 43.6 %collective-permute-start.4 = (bf16[256,1024]{1,0:T(8,128)(2,1)}, bf16[256,1024]{1,0:T(8,128)(2,1)}, u32[]{:S(2)}, u32[]{:S(2)}) collective-permute-start(bf16[256,1024]{1,0:T(8,128)(2,1)} %collective-permute-done.3), channel_id=1, source_target_pairs={{0,1},{1,2},{2,3},{3,0},{4,5},{5,6},{6,7},{7,4},{8,9},{9,10},{10,1... | collective-permute-start | bytes 1572872 | tf_op jit(solution)/shard_map/ppermute | solution.py:39
  160.5 42.2 %collective-permute-start.50 = (bf16[256,1024]{1,0:T(8,128)(2,1)}, bf16[256,1024]{1,0:T(8,128)(2,1)S(1)}, u32[]{:S(2)}, u32[]{:S(2)}) collective-permute-start(bf16[256,1024]{1,0:T(8,128)(2,1)} %bitcast.88), channel_id=1, source_target_pairs={{0,4},{4,0},{8,12},{12,8},{16,20},{20,16},{24,28},{28,24},{1,5},{5... | collective-permute-start | bytes 1572872 | tf_op jit(solution)/shard_map/ppermute | solution.py:52
  804.9 62.2 %collective-permute-start.64 = (bf16[512,1024]{1,0:T(8,128)(2,1)S(1)}, bf16[512,1024]{1,0:T(8,128)(2,1)S(1)}, u32[]{:S(2)}, u32[]{:S(2)}) collective-permute-start(bf16[512,1024]{1,0:T(8,128)(2,1)S(1)} %fusion.53), channel_id=1, source_target_pairs={{0,1},{1,2},{2,3},{3,0},{4,5},{5,6},{6,7},{7,4},{8,9},{9,10},{10,1... | collective-permute-start | bytes 3145736 | tf_op jit(solution)/shard_map/ppermute | solution.py:39
  869.7 82.5 %collective-permute-start.65 = (bf16[512,1024]{1,0:T(8,128)(2,1)}, bf16[512,1024]{1,0:T(8,128)(2,1)S(1)}, u32[]{:S(2)}, u32[]{:S(2)}) collective-permute-start(bf16[512,1024]{1,0:T(8,128)(2,1)} %fusion.52), channel_id=1, source_target_pairs={{0,1},{1,2},{2,3},{3,0},{4,5},{5,6},{6,7},{7,4},{8,9},{9,10},{10,1... | collective-permute-start | bytes 3145736 | tf_op jit(solution)/shard_map/ppermute | solution.py:39
  904.7 430.4 %collective-permute-start.102 = (bf16[4,12544,128]{2,1,0:T(8,128)(2,1)}, bf16[4,12544,128]{2,1,0:T(8,128)(2,1)}, u32[]{:S(2)}, u32[]{:S(2)}) collective-permute-start(bf16[4,12544,128]{2,1,0:T(8,128)(2,1)} %bitcast.638), channel_id=1, source_target_pairs={{0,4},{4,0},{8,12},{12,8},{16,20},{20,16},{24,28},{28,24},{1,5},{5... | collective-permute-start | bytes 38535176 | tf_op jit(solution)/shard_map/ppermute | solution.py:52
  1063.6 83.6 %collective-permute-start.96 = (f32[10,1024]{1,0:T(8,128)S(1)}, f32[10,1024]{1,0:T(8,128)S(1)}, u32[]{:S(2)}, u32[]{:S(2)}) collective-permute-start(f32[10,1024]{1,0:T(8,128)S(1)} %concatenate.25), channel_id=1, source_target_pairs={{0,4},{4,0},{8,12},{12,8},{16,20},{20,16},{24,28},{28,24},{1,5},{5... | collective-permute-start | bytes 122888 | tf_op jit(solution)/shard_map/ppermute | solution.py:52
  1069.7 136.6 %collective-permute-start.88 = (bf16[4,4,128,1024]{3,2,1,0:T(8,128)(2,1)}, bf16[4,4,128,1024]{3,2,1,0:T(8,128)(2,1)}, u32[]{:S(2)}, u32[]{:S(2)}) collective-permute-start(bf16[4,4,128,1024]{3,2,1,0:T(8,128)(2,1)} %fusion.37), channel_id=1, source_target_pairs={{0,4},{4,0},{8,12},{12,8},{16,20},{20,16},{24,28},{28,24},{1,5},{5... | collective-permute-start | bytes 12582920 | tf_op jit(solution)/shard_map/ppermute | solution.py:52
  1076.4 137.9 %collective-permute-start.80 = (bf16[4,4,128,1024]{3,2,1,0:T(8,128)(2,1)}, bf16[4,4,128,1024]{3,2,1,0:T(8,128)(2,1)}, u32[]{:S(2)}, u32[]{:S(2)}) collective-permute-start(bf16[4,4,128,1024]{3,2,1,0:T(8,128)(2,1)} %fusion.36), channel_id=1, source_target_pairs={{0,4},{4,0},{8,12},{12,8},{16,20},{20,16},{24,28},{28,24},{1,5},{5... | collective-permute-start | bytes 12582920 | tf_op jit(solution)/shard_map/ppermute | solution.py:52
  1135.1 183.6 %collective-permute-start.72 = (bf16[4,4,256,1024]{3,2,1,0:T(8,128)(2,1)}, bf16[4,4,256,1024]{3,2,1,0:T(8,128)(2,1)}, u32[]{:S(2)}, u32[]{:S(2)}) collective-permute-start(bf16[4,4,256,1024]{3,2,1,0:T(8,128)(2,1)} %fusion.17), channel_id=1, source_target_pairs={{0,4},{4,0},{8,12},{12,8},{16,20},{20,16},{24,28},{28,24},{1,5},{5... | collective-permute-start | bytes 25165832 | tf_op jit(solution)/shard_map/ppermute | solution.py:52
  1243.3 43.0 %collective-permute-start.70 = (bf16[2,2,96,1024]{3,2,1,0:T(8,128)(2,1)S(1)}, bf16[2,2,96,1024]{3,2,1,0:T(8,128)(2,1)S(1)}, u32[]{:S(2)}, u32[]{:S(2)}) collective-permute-start(bf16[2,2,96,1024]{3,2,1,0:T(8,128)(2,1)S(1)} %copy-done.62), channel_id=1, source_target_pairs={{0,2},{1,3},{2,0},{3,1},{4,6},{5,7},{6,4},{7,5},{8,10},{9,11},{10,... | collective-permute-start | bytes 2359304 | tf_op jit(solution)/shard_map/ppermute | solution.py:39
  1282.2 121.7 %collective-permute-start.71 = (bf16[2,2,96,1024]{3,2,1,0:T(8,128)(2,1)}, bf16[2,2,96,1024]{3,2,1,0:T(8,128)(2,1)}, u32[]{:S(2)}, u32[]{:S(2)}) collective-permute-start(bf16[2,2,96,1024]{3,2,1,0:T(8,128)(2,1)} %get-tuple-element.132), channel_id=1, source_target_pairs={{0,3},{1,0},{2,1},{3,2},{4,7},{5,4},{6,5},{7,6},{8,11},{9,8},{10,9... | collective-permute-start | bytes 2359304 | tf_op jit(solution)/shard_map/ppermute | solution.py:39
  1310.3 95.7 %collective-permute-start.94 = (bf16[128,1024]{1,0:T(8,128)(2,1)S(1)}, bf16[128,1024]{1,0:T(8,128)(2,1)}, u32[]{:S(2)}, u32[]{:S(2)}) collective-permute-start(bf16[128,1024]{1,0:T(8,128)(2,1)S(1)} %fusion.171), channel_id=1, source_target_pairs={{0,1},{1,2},{2,3},{3,0},{4,5},{5,6},{6,7},{7,4},{8,9},{9,10},{10,1... | collective-permute-start | bytes 786440 | tf_op jit(solution)/shard_map/ppermute | solution.py:39
  1315.9 91.3 %collective-permute-start.86 = (bf16[128,1024]{1,0:T(8,128)(2,1)}, bf16[128,1024]{1,0:T(8,128)(2,1)}, u32[]{:S(2)}, u32[]{:S(2)}) collective-permute-start(bf16[128,1024]{1,0:T(8,128)(2,1)} %fusion.173), channel_id=1, source_target_pairs={{0,1},{1,2},{2,3},{3,0},{4,5},{5,6},{6,7},{7,4},{8,9},{9,10},{10,1... | collective-permute-start | bytes 786440 | tf_op jit(solution)/shard_map/ppermute | solution.py:39
  1335.1 47.7 %collective-permute-start.73 = (bf16[2,2,256,1024]{3,2,1,0:T(8,128)(2,1)}, bf16[2,2,256,1024]{3,2,1,0:T(8,128)(2,1)}, u32[]{:S(2)}, u32[]{:S(2)}) collective-permute-start(bf16[2,2,256,1024]{3,2,1,0:T(8,128)(2,1)} %dynamic-slice_bitcast_fusion.3), channel_id=1, source_target_pairs={{0,8},{4,12},{8,0},{12,4},{16,24},{20,28},{24,16},{28,20},{1,9},{5... | collective-permute-start | bytes 6291464 | tf_op jit(solution)/shard_map/ppermute | solution.py:52
  1402.5 62.3 %collective-permute-start.103 = (bf16[2,6272,128]{2,1,0:T(8,128)(2,1)S(1)}, bf16[2,6272,128]{2,1,0:T(8,128)(2,1)S(1)}, u32[]{:S(2)}, u32[]{:S(2)}) collective-permute-start(bf16[2,6272,128]{2,1,0:T(8,128)(2,1)S(1)} %dynamic-slice_bitcast_fusion.1), channel_id=1, source_target_pairs={{0,8},{4,12},{8,0},{12,4},{16,24},{20,28},{24,16},{28,20},{1,9},{5... | collective-permute-start | bytes 9633800 | tf_op jit(solution)/shard_map/ppermute | solution.py:52
  1421.1 72.5 %collective-permute-start.105 = (bf16[2,6272,128]{2,1,0:T(8,128)(2,1)S(1)}, bf16[2,6272,128]{2,1,0:T(8,128)(2,1)S(1)}, u32[]{:S(2)}, u32[]{:S(2)}) collective-permute-start(bf16[2,6272,128]{2,1,0:T(8,128)(2,1)S(1)} %dynamic-slice_bitcast_fusion), channel_id=1, source_target_pairs={{0,16},{4,20},{8,24},{12,28},{16,0},{20,4},{24,8},{28,12},{1,17},{... | collective-permute-start | bytes 9633800 | tf_op jit(solution)/shard_map/ppermute | solution.py:52
  1437.4 59.0 %collective-permute-start.79 = (bf16[256,1024]{1,0:T(8,128)(2,1)S(1)}, bf16[256,1024]{1,0:T(8,128)(2,1)S(1)}, u32[]{:S(2)}, u32[]{:S(2)}) collective-permute-start(bf16[256,1024]{1,0:T(8,128)(2,1)S(1)} %fusion.148), channel_id=1, source_target_pairs={{0,1},{1,2},{2,3},{3,0},{4,5},{5,6},{6,7},{7,4},{8,9},{9,10},{10,1... | collective-permute-start | bytes 1572872 | tf_op jit(solution)/shard_map/ppermute | solution.py:39
  1465.8 48.1 %collective-permute-start.104 = (bf16[6272,128]{1,0:T(8,128)(2,1)S(1)}, bf16[6272,128]{1,0:T(8,128)(2,1)S(1)}, u32[]{:S(2)}, u32[]{:S(2)}) collective-permute-start(bf16[6272,128]{1,0:T(8,128)(2,1)S(1)} %dynamic-slice_bitcast_fusion.5), channel_id=1, source_target_pairs={{0,16},{4,20},{8,24},{12,28},{16,0},{20,4},{24,8},{28,12},{1,17},{... | collective-permute-start | bytes 4816904 | tf_op jit(solution)/shard_map/ppermute | solution.py:52
  (235 other events, 6174.0 us)

commit v2 on v1

--- a/solution.py
+++ b/solution.py
@@ -1,6 +1,10 @@
+import functools
+
 import jax
 import jax.numpy as jnp
 from jax import lax
+from jax.experimental import pallas as pl
+from jax.experimental.pallas import tpu as pltpu
 from jax.sharding import PartitionSpec as P
 
 HEADS = 16
@@ -11,19 +15,6 @@
 mask_fill = -1e30
 root_half = 0.7071067811865476
 inv_root_tau = 0.3989422804014327
-
-
-def merged(value, axis, join):
-    size = lax.axis_size(axis)
-    packed = jnp.stack(value)
-    me = lax.axis_index(axis)
-    parts = jnp.stack([packed] + [shifted(packed, axis, step) for step in range(1, size)])
-    parts = parts[(me - jnp.arange(size)) % size]
-    pieces = tuple(parts[:, i] for i in range(len(value)))
-    head = jax.tree.map(lambda part: part[0], pieces)
-    tail = jax.tree.map(lambda part: part[1:], pieces)
-    running, _ = lax.scan(lambda running, section: (join(running, section), None), head, tail)
-    return running
 
 
 def grid_of(n_pb):
@@ -239,6 +230,371 @@
     return (grad_queries, grad_keys, grad_values)
 
 
+PIECE = 128
+CHUNK = 256
+
+
+def vocab_tile(share):
+    return max(d for d in range(16, 901, 16) if share % d == 0)
+
+
+def each_count(live, chunks, run):
+    for taken in range(1, chunks + 1):
+        low = (taken - 1) * (CHUNK // PIECE)
+        high = taken * (CHUNK // PIECE)
+        upper = live <= high if taken < chunks else live >= 0
+
+        @pl.when(jnp.logical_and(live > low, upper))
+        def _():
+            run(taken)
+
+
+def rows_kernel(info, own_ids, mate_ids, own, mate, table, expo, sums, stats, acc, top, total):
+    tile = pl.program_id(0)
+    wide = table.shape[0]
+    group = own.shape[0]
+    chunks = group // CHUNK
+
+    @pl.when(tile == 0)
+    def _():
+        acc[...] = jnp.zeros_like(acc)
+        top[...] = jnp.full_like(top, mask_fill)
+        total[...] = jnp.zeros_like(total)
+        stats[...] = jnp.zeros_like(stats)
+
+    lane = lax.broadcasted_iota(jnp.int32, (CHUNK, 128), 1)
+    column = lax.broadcasted_iota(jnp.int32, (CHUNK, wide), 1)
+
+    for side, (rows, ids) in enumerate(((own, own_ids), (mate, mate_ids))):
+
+        def scores(chunk):
+            return lax.dot_general(
+                rows[chunk * CHUNK : (chunk + 1) * CHUNK, :],
+                table[...],
+                (((1,), (1,)), ((), ())),
+                preferred_element_type=jnp.float32,
+            )
+
+        def soften(chunk, logits):
+            here = slice(side * group + chunk * CHUNK, side * group + (chunk + 1) * CHUNK)
+            target = ids[chunk * CHUNK : (chunk + 1) * CHUNK, :] - tile * wide
+            logits = jnp.where(column == target, mask_fill, logits)
+            before = top[here, 0:1]
+            now = jnp.maximum(before, jnp.max(logits, axis=1, keepdims=True))
+            fade = jnp.exp(before - now)
+            grown = jnp.exp(logits - now)
+            total[here, :] = jnp.broadcast_to(
+                total[here, 0:1] * fade + jnp.sum(grown, axis=1, keepdims=True), (CHUNK, 128)
+            )
+            top[here, :] = jnp.broadcast_to(now, (CHUNK, 128))
+            stats[here, :] = jnp.where(lane == tile, now, stats[here, :])
+            grown = grown.astype(jnp.bfloat16)
+            expo[0, here, :] = grown
+            return here, grown, fade
+
+        def gather(here, grown, fade):
+            acc[here, :] = acc[here, :] * fade + jnp.dot(
+                grown, table[...], preferred_element_type=jnp.float32
+            )
+
+        def run(taken):
+            logits = [scores(0)]
+            late = None
+            for chunk in range(taken):
+                if chunk + 1 < taken:
+                    logits.append(scores(chunk + 1))
+                ready = soften(chunk, logits[chunk])
+                if late is not None:
+                    gather(*late)
+                late = ready
+            gather(*late)
+
+        each_count(info[1 + side], chunks, run)
+
+    @pl.when(tile == pl.num_programs(0) - 1)
+    def _():
+        for chunk in range(2 * chunks):
+            here = slice(chunk * CHUNK, (chunk + 1) * CHUNK)
+            mass = total[here, :]
+            share = jnp.where(mass[:, 0:1] > 0.0, 1.0 / jnp.maximum(mass[:, 0:1], 1e-30), 0.0)
+            sums[here, :] = (acc[here, :] * share).astype(jnp.bfloat16)
+            stats[here, :] = jnp.where(
+                lane == 127, top[here, :] + jnp.log(jnp.maximum(mass, 1e-30)), stats[here, :]
+            )
+
+
+def rows_pass(info, own_ids, mate_ids, own, mate, table, cores):
+    group, width = own.shape
+    share = table.shape[0] // cores
+    wide = vocab_tile(share)
+    tiles = share // wide
+    rows = 2 * group
+    whole = lambda i, s: (0, 0)
+    return pl.pallas_call(
+        rows_kernel,
+        grid_spec=pltpu.PrefetchScalarGridSpec(
+            num_scalar_prefetch=1,
+            grid=(tiles,),
+            in_specs=[
+                pl.BlockSpec((group, 1), whole),
+                pl.BlockSpec((group, 1), whole),
+                pl.BlockSpec((group, width), whole),
+                pl.BlockSpec((group, width), whole),
+                pl.BlockSpec((wide, width), lambda i, s: (s[0] * tiles + i, 0)),
+            ],
+            out_specs=[
+                pl.BlockSpec((1, rows, wide), lambda i, s: (i, 0, 0)),
+                pl.BlockSpec((rows, width), whole),
+                pl.BlockSpec((rows, 128), whole),
+            ],
+            scratch_shapes=[
+                pltpu.VMEM((rows, width), jnp.float32),
+                pltpu.VMEM((rows, 128), jnp.float32),
+                pltpu.VMEM((rows, 128), jnp.float32),
+            ],
+        ),
+        out_shape=[
+            jax.ShapeDtypeStruct((tiles, rows, wide), jnp.bfloat16),
+            jax.ShapeDtypeStruct((rows, width), jnp.bfloat16),
+            jax.ShapeDtypeStruct((rows, 128), jnp.float32),
+        ],
+        compiler_params=pltpu.CompilerParams(vmem_limit_bytes=56 << 20),
+        cost_estimate=pl.CostEstimate(
+            flops=4 * rows * share * width, bytes_accessed=4 * share * width, transcendentals=0
+        ),
+        name="rows_pass",
+    )(info, own_ids, mate_ids, own, mate, table)
+
+
+def table_kernel(first, sources, info, ids, scales, *refs):
+    rows, expos, (out, acc) = refs[: 2 * sources], refs[2 * sources : 3 * sources], refs[3 * sources :]
+    tile = pl.program_id(0) + first
+    wide = expos[0].shape[2]
+    group = rows[0].shape[0]
+    acc[...] = jnp.zeros_like(acc)
+    for part in range(2 * sources):
+        low = part % 2 * group
+
+        def run(taken):
+            count = taken * CHUNK
+            here = slice(part * group, part * group + count)
+            scale = scales[here, :]
+            lane = lax.broadcasted_iota(jnp.int32, (count, 128), 1)
+            column = lax.broadcasted_iota(jnp.int32, (count, wide), 1)
+            spread = jnp.sum(jnp.where(lane == tile, scale, 0.0), axis=1, keepdims=True)
+            hit = jnp.sum(jnp.where(lane == 127, scale, 0.0), axis=1, keepdims=True)
+            grad = expos[part // 2][0, low : low + count, :].astype(jnp.float32) * spread
+            grad = jnp.where(column == ids[here, :] - tile * wide, hit, grad).astype(jnp.bfloat16)
+            acc[...] += lax.dot_general(
+                grad,
+                rows[part][0:count, :],
+                (((0,), (0,)), ((), ())),
+                preferred_element_type=jnp.float32,
+            )
+
+        each_count(info[part], group // CHUNK, run)
+    for place in range(out.shape[0]):
+        size = out.shape[3]
+        out[place, 0] = acc[:, place * size : (place + 1) * size].astype(jnp.bfloat16)
+
+
+def table_pass(info, ids, scales, rows, expos, first, tiles, n_pb):
+    sources = len(expos)
+    _, both, wide = expos[0].shape
+    group, width = rows[0].shape
+    own = width // n_pb
+    whole = lambda i, s: (0, 0)
+    once = pl.Buffered(1)
+    return pl.pallas_call(
+        functools.partial(table_kernel, first, sources),
+        grid_spec=pltpu.PrefetchScalarGridSpec(
+            num_scalar_prefetch=1,
+            grid=(tiles,),
+            in_specs=[
+                pl.BlockSpec((sources * both, 1), whole, pipeline_mode=once),
+                pl.BlockSpec((sources * both, 128), whole, pipeline_mode=once),
+            ]
+            + [pl.BlockSpec((group, width), whole, pipeline_mode=once)] * (2 * sources)
+            + [pl.BlockSpec((1, both, wide), lambda i, s: (i + first, 0, 0))] * sources,
+            out_specs=pl.BlockSpec((n_pb, 1, wide, own), lambda i, s: (0, i, 0, 0)),
+            scratch_shapes=[pltpu.VMEM((wide, width), jnp.float32)],
+        ),
+        out_shape=jax.ShapeDtypeStruct((n_pb, tiles, wide, own), jnp.bfloat16),
+        compiler_params=pltpu.CompilerParams(vmem_limit_bytes=60 << 20),
+        cost_estimate=pl.CostEstimate(
+            flops=2 * sources * both * tiles * wide * width,
+            bytes_accessed=4 * sources * both * tiles * wide,
+            transcendentals=0,
+        ),
+        name=f"table_pass_{first}",
+    )(info, ids, scales, *rows, *expos)
+
+
+def gather_kernel(*refs):
+    mats, rows = refs[:3], refs[3:5]
+    full, laid = refs[5:8], refs[8:10]
+    send, recv, near = refs[10:]
+    slots = full[0].shape[1]
+    pb, place = lax.axis_index("pb"), lax.axis_index("slot")
+    mate = pb // 2 * 2 + (pb + 1) % 2
+    side_x = pb // 4 * 4 + (pb + 2) % 4
+    side_y = (pb + 4) % 8
+    corner = (side_x + 4) % 8
+    barrier = pltpu.get_barrier_semaphore()
+    partners = [(mate, place), (side_x, place), (side_y, place)]
+    partners += [(pb, (place + step) % slots) for step in range(1, slots)]
+    for partner in partners:
+        pl.semaphore_signal(barrier, inc=1, device_id=partner, device_id_type=pl.DeviceIdType.MESH)
+    pl.semaphore_wait(barrier, len(partners))
+
+    sent, unread, stays, ready = [], {}, [], {}
+
+    def push(source, target, device):
+        copy = pltpu.make_async_remote_copy(
+            src_ref=source,
+            dst_ref=target,
+            send_sem=send.at[len(sent)],
+            recv_sem=recv.at[len(sent)],
+            device_id=device,
+            device_id_type=pl.DeviceIdType.MESH,
+        )
+        copy.start()
+        unread[len(sent)] = copy
+        sent.append(copy)
+        return len(sent) - 1
+
+    def read(number):
+        unread.pop(number).wait_recv()
+
+    def put(source, target):
+        copy = pltpu.make_async_copy(source, target, near.at[len(stays)])
+        copy.start()
+        stays.append(copy)
+
+    def move_rows(step):
+        goal = (place + step) % slots
+        for source, target in zip(rows, laid):
+            own = target.shape[0]
+            block = source.at[pl.ds(goal * own, own)]
+            spot = target.at[:, :, place]
+            if step:
+                push(block, spot, (pb, goal))
+            else:
+                put(block, spot)
+
+    def part(mat, at_pb, origin, half):
+        size = full[mat].shape[2] // 2
+        return full[mat].at[at_pb, origin, pl.ds(half * size, size)]
+
+    def own_moves(step, mat, origin, source):
+        size = full[mat].shape[2] // 2
+        first, second = (source.at[pl.ds(half * size, size)] for half in range(2))
+        first_at, second_at = (part(mat, pb, origin, half) for half in range(2))
+        ready[step, mat] = [
+            push(first, first_at, (side_x, place)),
+            push(second, second_at, (side_y, place)),
+            push(first, first_at, (side_y, place)),
+            push(second, second_at, (side_x, place)),
+        ]
+        push(source, full[mat].at[pb, origin], (mate, place))
+
+    def onward(step, mat, origin):
+        over_x, over_y, _, _ = ready[step, mat]
+        read(over_x)
+        block = part(mat, side_x, origin, 0)
+        ready[step, mat].append(push(block, block, (side_y, place)))
+        push(block, block, (mate, place))
+        read(over_y)
+        block = part(mat, side_y, origin, 1)
+        ready[step, mat].append(push(block, block, (side_x, place)))
+        push(block, block, (mate, place))
+
+    def finish(step, mat, origin):
+        _, _, over_y, over_x, first, second = ready[step, mat]
+        for number, at_pb, half in (
+            (over_y, side_y, 0),
+            (over_x, side_x, 1),
+            (first, corner, 0),
+            (second, corner, 1),
+        ):
+            read(number)
+            block = part(mat, at_pb, origin, half)
+            push(block, block, (mate, place))
+
+    count = len(mats)
+    following = (pb, (place + 1) % slots)
+    ring = [push(mats[mat], full[mat].at[pb, place], following) for mat in range(count)]
+    for mat in range(count):
+        own_moves(0, mat, place, mats[mat])
+        put(mats[mat], full[mat].at[pb, place])
+    move_rows(1)
+    move_rows(0)
+    for step in range(1, slots + 1):
+        origin = (place + slots - step) % slots
+        before = (place + slots - step + 1) % slots
+        if step < slots:
+            for mat in range(count):
+                read(ring[mat])
+                block = full[mat].at[pb, origin]
+                if step < slots - 1:
+                    ring[mat] = push(block, block, following)
+                own_moves(step, mat, origin, block)
+        if step == 1:
+            move_rows(slots - 1)
+        if step == 2:
+            for other in range(2, slots - 1):
+                move_rows(other)
+        for mat in range(count):
+            onward(step - 1, mat, before)
+        for mat in range(count):
+            finish(step - 1, mat, before)
+    for number in sorted(unread):
+        read(number)
+    for copy in sent:
+        copy.wait_send()
+    for copy in stays:
+        copy.wait()
+
+
+def gather_inputs(x_in, memory, attn_w, ffn_in, ffn_out):
+    n_pb, slots = lax.axis_size("pb"), lax.axis_size("slot")
+    mats, rows = (attn_w, ffn_in, ffn_out), (x_in, memory)
+    width = attn_w.shape[1]
+    if (n_pb, slots) != (8, 4):
+        return (
+            to_slots(x_in),
+            to_slots(memory),
+            *(gather_all(mat).reshape(-1, width) for mat in mats),
+        )
+    shapes = [jax.ShapeDtypeStruct((n_pb, slots) + mat.shape, mat.dtype) for mat in mats]
+    for row in rows:
+        every, questions, steps, _ = row.shape
+        shapes.append(
+            jax.ShapeDtypeStruct((every // slots, questions, slots, steps, width), row.dtype)
+        )
+    copies = 13 * len(mats) * slots + (slots - 1) * (len(mats) + len(rows))
+    anywhere = pl.BlockSpec(memory_space=pl.ANY)
+    *full, x_here, mem_here = pl.pallas_call(
+        gather_kernel,
+        in_specs=[anywhere] * 5,
+        out_specs=[anywhere] * 5,
+        out_shape=shapes,
+        scratch_shapes=[
+            pltpu.SemaphoreType.DMA((copies,)),
+            pltpu.SemaphoreType.DMA((copies,)),
+            pltpu.SemaphoreType.DMA((len(mats) + len(rows),)),
+        ],
+        compiler_params=pltpu.CompilerParams(collective_id=0, has_side_effects=True),
+        name="gather_inputs",
+    )(*mats, *rows)
+    own, questions, _, _, _ = x_here.shape
+    return (
+        x_here.reshape(own, questions, -1, width),
+        mem_here.reshape(own, questions, -1, width),
+        *(mat.reshape(-1, width) for mat in full),
+    )
+
+
 def body(
     x_in,
     memory,
@@ -254,20 +610,14 @@
     norms,
     embedding,
 ):
-    x_here, mem_here = (
-        to_slots(x_in),
-        to_slots(memory),
+    x_here, mem_here, attn_full, in_full, out_full = gather_inputs(
+        x_in, memory, attn_w, ffn_in, ffn_out
     )
     slots_here, questions, tgt_steps, model_width = x_here.shape
     mem_steps = mem_here.shape[2]
     seq_count = slots_here * questions
     head_dim = model_width // HEADS
     scaling = head_dim ** (-0.5)
-    attn_full, in_full, out_full = (
-        gather_all(attn_w).reshape(-1, model_width),
-        gather_all(ffn_in).reshape(-1, model_width),
-        gather_all(ffn_out).reshape(-1, model_width),
-    )
     blocks = [
         attn_full[block_index * model_width : (block_index + 1) * model_width]
         for block_index in range(8)
@@ -322,40 +672,112 @@
     three_low = hidden_three.astype(jnp.bfloat16).reshape(
         slots_here, questions, tgt_steps, model_width
     )
+    place, slot_count = place_of("slot")
+    core, cores = place_of("core")
     vocab_here = embedding.shape[0]
-    vocab_start = lax.axis_index("slot") * vocab_here
-    local_ids = target_ids - vocab_start
-    slot_count = lax.axis_size("slot")
-    piece = jnp.zeros((slot_count,) + three_low.shape, three_low.dtype)
-    for index, block in ring_gather(three_low, "slot"):
-        piece = lax.dynamic_update_index_in_dim(piece, block, index, 0)
-    piece = piece.reshape((-1,) + three_low.shape[1:])
-    flat_rows = piece.reshape(-1, model_width)
-    logits = contract_cols(flat_rows, embedding).reshape(
-        piece.shape[0], questions, tgt_steps, vocab_here
-    )
-    rows_all = piece
-    onehot = jnp.arange(vocab_here)[None, None, None, :] == local_ids[None, :, :, None]
-    row_max = jnp.max(logits, axis=-1)
-    row_sum = jnp.sum(jnp.exp(logits - row_max[..., None]), axis=-1)
-    target_logit = jnp.sum(jnp.where(onehot, logits, 0.0), axis=-1)
-
-    def merge_stats(first, second):
-        joint_max = jnp.maximum(first[0], second[0])
-        joint_sum = first[1] * jnp.exp(first[0] - joint_max) + second[1] * jnp.exp(
-            second[0] - joint_max
+    share = vocab_here // cores
+    pieces = slots_here * questions
+
+    def both_cores(value):
+        return jnp.stack([value, shifted(value, "core", 1)]) if cores > 1 else value[None]
+
+    tokens = jnp.concatenate([target_ids, valid_count[:, None], target_len[:, None]], axis=1)
+    tokens = both_cores(tokens)
+    ids_all, valid_all, len_all = tokens[:, :, :tgt_steps], tokens[:, :, -2], tokens[:, :, -1]
+
+    local = target_ids - place * vocab_here
+    held = jnp.logical_and(local >= 0, local < vocab_here)
+    target_rows = jnp.take(embedding, jnp.clip(local, 0, vocab_here - 1), axis=0)
+    target_rows = jnp.where(held[..., None], target_rows, jnp.zeros_like(target_rows))
+    found = [shifted(target_rows, "slot", step) for step in range(1, slot_count)]
+    target_rows = sum([f.astype(jnp.float32) for f in found], target_rows.astype(jnp.float32))
+
+    slot_ids = jnp.arange(slot_count * slots_here).reshape(slot_count, 1, slots_here, 1)
+    live_piece = (slot_ids < valid_all[None, :, None, :]).reshape(slot_count, -1, pieces)
+    order_all = jnp.argsort(jnp.logical_not(live_piece), axis=-1, stable=True).astype(jnp.int32)
+    live_all = jnp.sum(live_piece, axis=-1).astype(jnp.int32)
+    piece_ids = jnp.broadcast_to(
+        ids_all[None, :, None], (slot_count, cores, slots_here, questions, tgt_steps)
+    ).reshape(slot_count, cores, pieces, tgt_steps)
+    piece_ids = piece_ids - (place * vocab_here + core * share)
+    sorted_ids = jnp.take_along_axis(piece_ids, order_all[..., None], axis=2)
+    ring = (place - jnp.arange(slot_count)) % slot_count
+    order_ring, live_ring, ids_ring = order_all[ring], live_all[ring], sorted_ids[ring]
+
+    own_order = order_ring[0, 0]
+    group = pieces * tgt_steps
+    three_pieces = three_low.reshape(pieces, tgt_steps, model_width)
+    moving = jnp.concatenate(
+        [lax.dynamic_index_in_dim(three_pieces, own_order[i], 0) for i in range(pieces)], axis=0
+    ).reshape(group, model_width)
+
+    def join(first, second):
+        rows_a, log_a = first
+        rows_b, log_b = second
+        log = jnp.logaddexp(log_a, log_b)
+        rows = rows_a.astype(jnp.float32) * jnp.exp(log_a - log)[:, None]
+        rows = rows + rows_b.astype(jnp.float32) * jnp.exp(log_b - log)[:, None]
+        return rows, log
+
+    def lower(part):
+        return part[0].astype(jnp.bfloat16), part[1]
+
+    row_list, expo_list, stat_list = [], [], []
+    partial, own_part = None, None
+    for step in range(slot_count):
+        if step:
+            moving, _ = lax.optimization_barrier((moving, expo_list[-1]))
+        other = shifted(moving, "core", 1)
+        following = shifted(moving, "slot", 1) if step + 1 < slot_count else None
+        info = jnp.concatenate([core[None].astype(jnp.int32), live_ring[step]])
+        expo, sums, stats = rows_pass(
+            info,
+            ids_ring[step, 0].reshape(group, 1),
+            ids_ring[step, 1].reshape(group, 1),
+            moving,
+            other,
+            embedding,
+            cores,
         )
-        return (joint_max, joint_sum, first[2] + second[2])
-
-    row_max, row_sum, target_logit = merged((row_max, row_sum, target_logit), "slot", merge_stats)
-    log_norm = row_max + jnp.log(row_sum)
-    live = positions[None, :] < target_len[:, None]
-    lengths = target_len.astype(jnp.float32)
-    per_slot = (
-        jnp.sum(jnp.where(live[None], target_logit - log_norm, 0.0), axis=2) / lengths[None, :]
-    )
-    valid = jnp.arange(per_slot.shape[0])[:, None] < valid_count[None, :]
-    scores_t = doc_scores.T
+        row_list += [moving, other]
+        expo_list.append(expo)
+        stat_list.append(stats)
+        logs = stats[:, 127]
+        arrived = (shifted(sums[group:], "core", 1), shifted(logs[group:], "core", 1))
+        part = lower(join((sums[:group], logs[:group]), arrived))
+        if step == 0:
+            own_part = part
+        else:
+            if partial is not None:
+                part = lower(join(part, partial))
+            partial = tuple(shifted(value, "slot", 1) for value in part)
+        moving = following
+    mean_rows, log_rest = join(own_part, partial)
+    back = jnp.argsort(own_order)
+
+    def natural(value):
+        value = value.reshape((pieces, tgt_steps) + value.shape[1:])
+        return jnp.concatenate(
+            [lax.dynamic_index_in_dim(value, back[i], 0) for i in range(pieces)], axis=0
+        ).reshape((slots_here, questions, tgt_steps) + value.shape[2:])
+
+    mean_rows, log_rest = natural(mean_rows), natural(log_rest)
+    target_logit = jnp.sum(three_low.astype(jnp.float32) * target_rows[None], axis=-1)
+
+    packed = jnp.stack([log_rest, target_logit])
+    spread = [packed] + [shifted(packed, "slot", step) for step in range(1, slot_count)]
+    spread = jnp.stack(spread)[ring]
+    spread = both_cores(spread)
+    spread = spread.transpose(2, 1, 3, 0, 4, 5).reshape(
+        2, slot_count * slots_here, cores, questions, tgt_steps
+    )
+    rest_all, hit_all = spread[0], spread[1]
+    log_norm = jnp.logaddexp(rest_all, hit_all)
+    live = positions < len_all[..., None]
+    lengths = len_all.astype(jnp.float32)
+    per_slot = jnp.sum(jnp.where(live[None], hit_all - log_norm, 0.0), axis=3) / lengths[None]
+    valid = jnp.arange(per_slot.shape[0])[:, None, None] < valid_all[None]
+    scores_t = both_cores(doc_scores).transpose(2, 0, 1)
     joint = jnp.where(valid, scores_t + per_slot, mask_fill)
     prior = jnp.where(valid, scores_t, mask_fill)
     joint_total = jax.nn.logsumexp(joint, axis=0)
@@ -363,34 +785,61 @@
     log_post = joint - joint_total
     posterior = jnp.exp(log_post)
     entropy_q = -jnp.sum(posterior * log_post, axis=0)
-    objective_part = jnp.sum(lengths * (neg_marginal + entropy_weight * entropy_q))
-    sum_objective, sum_lengths, sum_entropy = lax.psum(
-        (objective_part, jnp.sum(lengths), jnp.sum(entropy_q)), "pb"
-    )
-    loss = sum_objective / sum_lengths
-    entropy = sum_entropy / (questions * lax.axis_size("pb"))
-    slot_weight = -posterior * (1.0 + entropy_weight * (log_post + entropy_q[None, :]))
-    token_weight = jnp.where(live[None], slot_weight[:, :, None], 0.0)
-    soft_probs = jnp.exp(logits - log_norm[..., None])
-    grad_logits = (token_weight[..., None] * (onehot.astype(jnp.float32) - soft_probs)).astype(
-        jnp.bfloat16
-    )
-    grad_embed = contract_rows(
-        grad_logits.reshape(-1, vocab_here), rows_all.reshape(-1, model_width)
-    )
-    grad_embed = scatter_pb(
-        grad_embed.astype(jnp.bfloat16)
-        .reshape(vocab_here, lax.axis_size("pb"), -1)
-        .transpose(1, 0, 2)
-    )
-    piece = grad_logits
-    grad_three = ring_scatter(
-        product(piece.reshape(-1, vocab_here), embedding)
-        .astype(jnp.bfloat16)
-        .reshape(slot_count, -1, model_width),
-        "slot",
-        0,
-    )
+    objective_part = jnp.sum((lengths * (neg_marginal + entropy_weight * entropy_q))[0])
+    slot_weight = -posterior * (1.0 + entropy_weight * (log_post + entropy_q[None]))
+    token_weight = jnp.where(live[None], slot_weight[..., None], 0.0)
+    hit_weight = token_weight * jax.nn.sigmoid(rest_all - hit_all)
+
+    def own_slots(value):
+        value = value[:, 0].reshape(slot_count, slots_here, questions, tgt_steps)
+        return pick(value, place, 0)
+
+    grad_three = own_slots(hit_weight)[..., None] * (target_rows[None] - mean_rows)
+    grad_three = grad_three.reshape(-1, model_width)
+
+    def ring_rows(value):
+        value = value.reshape(slot_count, slots_here, cores, questions, tgt_steps)
+        value = value.transpose(0, 2, 1, 3, 4).reshape(slot_count, cores, pieces, tgt_steps)
+        value = jnp.take_along_axis(value, order_all[..., None], axis=2)
+        return value[ring].reshape(-1, 1)
+
+    weight_rows, norm_rows, hit_rows = (
+        ring_rows(token_weight),
+        ring_rows(log_norm),
+        ring_rows(hit_weight),
+    )
+    tops = jnp.concatenate(stat_list, axis=0)
+    scales = jnp.where(weight_rows == 0.0, 0.0, -weight_rows * jnp.exp(tops - norm_rows))
+    scales = jnp.where(jnp.arange(128)[None, :] == 127, hit_rows, scales)
+    tiles = expo_list[0].shape[0]
+    cut = tiles // 2 + 1
+    n_pb = lax.axis_size("pb")
+    tall, wide, _ = grid_of(n_pb)
+    grad_pieces = []
+    for first, count in ((0, cut), (cut, tiles - cut)):
+        chunk = table_pass(
+            live_ring.reshape(-1),
+            ids_ring.reshape(-1, 1),
+            scales,
+            row_list,
+            expo_list,
+            first,
+            count,
+            n_pb,
+        )
+        chunk = chunk.reshape((tall, wide, cores, -1) + chunk.shape[3:])
+        half = chunk.shape[3] // 2
+        early = ring_scatter(chunk[:, :, :, :half], "x", 1).astype(jnp.bfloat16)
+        late = ring_scatter(chunk[:, :, :, half:], "y", 0).astype(jnp.bfloat16)
+        early = ring_scatter(early, "y", 0).astype(jnp.bfloat16)
+        late = ring_scatter(late, "x", 0).astype(jnp.bfloat16)
+        chunk = jnp.concatenate([early, late], axis=1)
+        kept = pick(chunk, core, 0)
+        given = shifted(pick(chunk, 1 - core, 0), "core", 1)
+        grad_pieces.append(jnp.stack([kept, given]))
+    grad_embed = jnp.concatenate(grad_pieces, axis=1)
+    grad_embed = jnp.where(core == 0, grad_embed, grad_embed[::-1])
+    grad_embed = grad_embed.reshape(vocab_here, -1).astype(jnp.float32)
     back_blocks, in_back, out_back = blocks, in_full, out_full
     grad_res_three, gain_three, shift_three = norm_backward(
         grad_three, normed_three, root_three, norms[4]
@@ -470,12 +919,17 @@
         [
             jnp.stack([gain_one, shift_one, gain_two, shift_two, gain_three, shift_three], axis=0),
             grad_bias.reshape(-1, model_width),
+            jnp.zeros((1, model_width), jnp.float32)
+            .at[0, :3]
+            .set(jnp.stack([objective_part, jnp.sum(lengths[0]), jnp.sum(entropy_q[0])])),
         ],
         axis=0,
     )
     small = sum_all(small, ("core", "x", "y", "slot"))
     grad_norms = small[:6]
-    grad_bias = small[6:].reshape(-1)
+    loss = small[-1, 0] / small[-1, 1]
+    entropy = small[-1, 2] / (questions * n_pb * slot_count)
+    grad_bias = small[6:-1].reshape(-1)
     own_bias = grad_bias.shape[0] // (lax.axis_size("pb") * slot_count)
     grad_bias = lax.dynamic_slice_in_dim(
         grad_bias,

time: 1530 us -> 1370 us (0.90)
  Pallas kernels: 0 us -> 430 us
  waiting for transfers between devices: 480 us -> 243 us
  matrix products: 404 us -> 188 us
  other arithmetic: 197 us -> 109 us
  local copies, waits for them, and re-layouts: 246 us -> 210 us
  blocking collectives: 27.1 us -> 0 us
    pallas_call x0 -> x7, Pallas kernels: none -> 430 us  [the longest x1 198 us: gather_inputs(): pl.pallas_call(gather_kernel, in_specs=[anywhere] * 5, out_specs=[anywher...]
    ppermute x65 -> x43, waiting for transfers between devices: 301 us -> 131 us  [shifted(): return lax.ppermute(value, 'pb', pairs)]
    dot_general x11 -> x10, matrix products: 117 us -> 33.4 us  [contract_rows(): lax.dot_general(left, right, (((0,), (0,)), ((), ())), preferred_element_...]
    dot_general x11 -> x10, matrix products: 107 us -> 36.8 us  [product(): return jnp.dot(left, right, preferred_element_type=jnp.float32)]
    ppermute x42 -> x33, waiting for transfers between devices: 179 us -> 111 us  [shifted(): lax.ppermute(value, 'slot', [(i, (i + step) % size) for i in range(size)])]
    dot_general x11 -> x10, matrix products: 139 us -> 71.9 us  [contract_cols(): lax.dot_general(left, right, (((1,), (1,)), ((), ())), preferred_element_...]
    convert_element_type x4 -> x13, other arithmetic: 60.8 us -> 14.4 us  [the longest x3 7.51 us: lower(): return (part[0].astype(jnp.bfloat16), part[1])]
    reduce_sum x4 -> x8, other arithmetic: 49.4 us -> 3.61 us  [the longest x1 0.72 us: body(): jnp.sum(three_low.astype(jnp.float32) * target_rows[None], axis=-1)]
  transfers between devices with their start and end apart: 107 -> 76, of which waited for: 48 -> 26; matrix products, arithmetic and copies ran while one was open for 30% -> 26% of each run, Pallas kernels for 0% -> 32%
where the time goes in v2:
time: 1370 us; the launch traced here: 1350 us
  Pallas kernels  430 us (31%)
  waiting for transfers between devices  243 us (18%)
  local copies, waits for them, and re-layouts  210 us (15%)
  matrix products  188 us (14%)
  starting transfers between devices  150 us (11%)
  other arithmetic  109 us (8%)
  between operations  24 us (2%)
    pallas_call x1, Pallas kernels, gather_inputs(): pl.pallas_call(gather_kernel, in_specs=[anywhere] * 5, out_specs=[anywher...  198 us
    pallas_call x4, Pallas kernels, rows_pass(): pl.pallas_call(rows_kernel, grid_spec=pltpu.PrefetchScalarGridSpec(num_sc...  143 us
    ppermute x43, waiting for transfers between devices, shifted(): return lax.ppermute(value, 'pb', pairs)  131 us
    ppermute x33, waiting for transfers between devices, shifted(): lax.ppermute(value, 'slot', [(i, (i + step) % size) for i in range(size)])  111 us
    ppermute x33, starting transfers between devices, shifted(): lax.ppermute(value, 'slot', [(i, (i + step) % size) for i in range(size)])  99.1 us
    pallas_call x2, Pallas kernels, table_pass(): pl.pallas_call(functools.partial(table_kernel, first, sources), grid_spec...  88.5 us
    dot_general x10, matrix products, contract_cols(): lax.dot_general(left, right, (((1,), (1,)), ((), ())), preferred_element_...  71.9 us
    reshape x16, local copies, waits for them, and re-layouts, split_heads(): return value.reshape(seq_count, steps, HEADS, head_dim)  62.5 us
  transfers between devices with their start and end apart: 76, of which 26 were waited for; matrix products, arithmetic and copies ran while one was open for 26% of the time, Pallas kernels for 32%

profile of v2, /device:TPU:0, one launch (start us, length us, event | category | flops | bytes accessed | tf_op | source)
XLA Modules:
  0.0 1353.6 jit_solution(4906611592976872427)
XLA Ops:
  2.1 13.2 gather_fusion.3
  28.7 198.4 %gather_inputs.1 = (bf16[8,4,256,1024]{3,2,1,0:T(8,128)(2,1)}, bf16[8,4,128,1024]{3,2,1,0:T(8,128)(2,1)}, bf16[8,4,128,1024]{3,2,1,0:T(8,128)(2,1)}, bf16[2,2,4,...) custom-call(bf16[256,1024]{1,0:T(8,128)(2,1)} %refs_0_.1, bf16[128,1024]{1,0:T(8,128)(2,1)} %refs_1_.1, ...), custom_call_target="tpu_custom_call" | custom-call | tf_op jit(solution)/shard_map/gather_inputs/pallas_call | solution.py:577
  227.1 11.3 fusion.188
  344.1 26.9 %fusion.4 = (bf16[512,4096]{1,0:T(8,128)(2,1)S(1)}, f32[512,4096]{1,0:T(8,128)}) fusion(f32[4096]{0:T(1024)S(1)} %copy-done.143, bf16[4096,1024]{1,0:T(8,128)(2,1)} %bitcast.707, f32[512,1024]{1,0:T(8,128)S(1)} %get-tuple-element.202, f32[1024]{0:T(1024)S(1)} %bitcast.698, f32[1024]{0:T(1024)S(1)} %bitcast.672, f32[512]{0:T(512)S(1)} %add_rsqrt_fusion.1, ...), kind=kOutput, calls=%fused_computation.30 | convolution fusion | flops 4436000768 | bytes 23097344 | tf_op jit(solution)/shard_map/dot_general | solution.py:173
  396.7 43.8 %rows_pass.4 = (bf16[7,1024,896]{2,1,0:T(8,128)(2,1)}, bf16[1024,1024]{1,0:T(8,128)(2,1)}, f32[1024,128]{1,0:T(8,128)}) custom-call(s32[3]{0:T(128)} %pad_add_fusion.2.info, s32[512,1]{1,0:T(8,128)} %copy.356.own_ids, s32[512,1]{1,0:T(8,128)} %copy.357.mate_ids, bf16[512,1024]{1,0:T(8,128)(2,1)} %bitcast.612, ...), custom_call_target="tpu_custom_call" | custom-call | flops 26306674688 | bytes 25690112 | tf_op jit(solution)/shard_map/rows_pass/pallas_call | solution.py:333
  447.1 14.6 %collective-permute-start.5 = (bf16[512,1024]{1,0:T(8,128)(2,1)}, bf16[512,1024]{1,0:T(8,128)(2,1)}, u32[]{:S(2)}, u32[]{:S(2)}) collective-permute-start(bf16[512,1024]{1,0:T(8,128)(2,1)} %collective-permute-done.4.own.refs_2_), channel_id=1, source_target_pairs={{0,1},{1,2},{2,3},{3,0},{4,5},{5,6},{6,7},{7,4},{8,9},{9,10},{10,1... | collective-permute-start | bytes 3145736 | tf_op jit(solution)/shard_map/ppermute | solution.py:30
  462.7 19.3 %rows_pass.5 = (bf16[7,1024,896]{2,1,0:T(8,128)(2,1)}, bf16[1024,1024]{1,0:T(8,128)(2,1)}, f32[1024,128]{1,0:T(8,128)}) custom-call(s32[3]{0:T(128)} %pad_add_fusion.4.info, s32[512,1]{1,0:T(8,128)} %copy.358.own_ids, s32[512,1]{1,0:T(8,128)} %copy.359.mate_ids, bf16[512,1024]{1,0:T(8,128)(2,1)} %collective-permute-done.4.own.refs_2_, ...), custom_call_target="tpu_custom_call" | custom-call | flops 26306674688 | bytes 25690112 | tf_op jit(solution)/shard_map/rows_pass/pallas_call | solution.py:333
  488.5 21.7 %collective-permute-start.7 = (bf16[512,1024]{1,0:T(8,128)(2,1)}, bf16[512,1024]{1,0:T(8,128)(2,1)}, u32[]{:S(2)}, u32[]{:S(2)}) collective-permute-start(bf16[512,1024]{1,0:T(8,128)(2,1)} %collective-permute-done.5.own.refs_4_), channel_id=1, source_target_pairs={{0,1},{1,2},{2,3},{3,0},{4,5},{5,6},{6,7},{7,4},{8,9},{9,10},{10,1... | collective-permute-start | bytes 3145736 | tf_op jit(solution)/shard_map/ppermute | solution.py:30
  511.2 36.5 %rows_pass.6 = (bf16[7,1024,896]{2,1,0:T(8,128)(2,1)}, bf16[1024,1024]{1,0:T(8,128)(2,1)}, f32[1024,128]{1,0:T(8,128)}) custom-call(s32[3]{0:T(128)} %pad_add_fusion.5.info, s32[512,1]{1,0:T(8,128)} %copy.360.own_ids, s32[512,1]{1,0:T(8,128)} %copy.361.mate_ids, bf16[512,1024]{1,0:T(8,128)(2,1)} %collective-permute-done.5.own.refs_4_, ...), custom_call_target="tpu_custom_call" | custom-call | flops 26306674688 | bytes 25690112 | tf_op jit(solution)/shard_map/rows_pass/pallas_call | solution.py:333
  557.4 43.8 %rows_pass.7 = (bf16[7,1024,896]{2,1,0:T(8,128)(2,1)}, bf16[1024,1024]{1,0:T(8,128)(2,1)}, f32[1024,128]{1,0:T(8,128)}) custom-call(s32[3]{0:T(128)} %pad_add_fusion.3.info, s32[512,1]{1,0:T(8,128)} %copy.362.own_ids, s32[512,1]{1,0:T(8,128)} %copy.363.mate_ids, bf16[512,1024]{1,0:T(8,128)(2,1)} %collective-permute-done.7.own.refs_6_, ...), custom_call_target="tpu_custom_call" | custom-call | flops 26306674688 | bytes 25690112 | tf_op jit(solution)/shard_map/rows_pass/pallas_call | solution.py:333
  614.8 17.4 %collective-permute-done.15 = f32[512]{0:T(512)S(1)} collective-permute-done((f32[512]{0:T(512)S(1)}, f32[512]{0:T(512)S(1)}, u32[]{:S(2)}, u32[]{:S(2)}) %collective-permute-start.15) | collective-permute-done | bytes 2080 | tf_op jit(solution)/shard_map/ppermute | solution.py:30
  662.7 39.5 %table_pass_4.1 = bf16[8,3,896,128]{3,2,1,0:T(8,128)(2,1)} custom-call(s32[8]{0:T(128)} %reshape.821.info, s32[4096,1]{1,0:T(8,128)} %copy.404.ids, f32[4096,128]{1,0:T(8,128)} %fusion.46.scales, bf16[512,1024]{1,0:T(8,128)(2,1)} %bitcast.613, bf16[512,1024]{1,0:T(8,128)(2,1)} %collective-permute-done.2.mate.refs_1_, ...), custom_call_target="tpu_custom_call" | custom-call | flops 22548578304 | bytes 44040192 | tf_op jit(solution)/shard_map/table_pass_4/pallas_call | solution.py:408
  714.4 48.9 %table_pass_0.1 = bf16[8,4,896,128]{3,2,1,0:T(8,128)(2,1)} custom-call(s32[8]{0:T(128)} %reshape.821.info, s32[4096,1]{1,0:T(8,128)} %copy.404.ids, f32[4096,128]{1,0:T(8,128)} %fusion.46.scales, bf16[512,1024]{1,0:T(8,128)(2,1)} %bitcast.614, bf16[512,1024]{1,0:T(8,128)(2,1)} %collective-permute-done.2.mate.refs_1_, ...), custom_call_target="tpu_custom_call" | custom-call | flops 30064771072 | bytes 58720256 | tf_op jit(solution)/shard_map/table_pass_0/pallas_call | solution.py:408
  778.3 31.4 %collective-permute-done.66 = bf16[2,2,1792,128]{3,2,1,0:T(8,128)(2,1)S(1)} collective-permute-done((bf16[2,2,1792,128]{3,2,1,0:T(8,128)(2,1)S(1)}, bf16[2,2,1792,128]{3,2,1,0:T(8,128)(2,1)S(1)}, u32[]{:S(2)}, u32[]{:S(2)}) %collective-permute-start.66) | collective-permute-done | bytes 1835040 | tf_op jit(solution)/shard_map/ppermute | solution.py:43
  813.6 12.9 collective-permute-done.72
  835.4 12.2 convert_reduce_fusion
  868.5 10.5 multiply_reduce_fusion
  998.5 9.7 add_convert_fusion
  1070.9 17.4 %collective-permute-done.69 = bf16[2,1792,128]{2,1,0:T(8,128)(2,1)S(1)} collective-permute-done((bf16[2,1792,128]{2,1,0:T(8,128)(2,1)}, bf16[2,1792,128]{2,1,0:T(8,128)(2,1)S(1)}, u32[]{:S(2)}, u32[]{:S(2)}) %collective-permute-start.69) | collective-permute-done | bytes 917536 | tf_op jit(solution)/shard_map/ppermute | solution.py:43
  1094.4 30.8 %collective-permute-done.40 = bf16[2,2,96,1024]{3,2,1,0:T(8,128)(2,1)S(1)} collective-permute-done((bf16[2,2,96,1024]{3,2,1,0:T(8,128)(2,1)S(1)}, bf16[2,2,96,1024]{3,2,1,0:T(8,128)(2,1)S(1)}, u32[]{:S(2)}, u32[]{:S(2)}) %collective-permute-start.40) | collective-permute-done | bytes 786464 | tf_op jit(solution)/shard_map/ppermute | solution.py:30
  1172.0 11.1 collective-permute-done.59
  1193.7 48.9 %collective-permute-done.52 = bf16[2,128,1024]{2,1,0:T(8,128)(2,1)S(1)} collective-permute-done((bf16[2,128,1024]{2,1,0:T(8,128)(2,1)S(1)}, bf16[2,128,1024]{2,1,0:T(8,128)(2,1)S(1)}, u32[]{:S(2)}, u32[]{:S(2)}) %collective-permute-start.52) | collective-permute-done | bytes 524320 | tf_op jit(solution)/shard_map/ppermute | solution.py:43
  1258.7 11.6 collective-permute-start.55
  1271.3 18.8 %collective-permute-start.63 = (bf16[128,1024]{1,0:T(8,128)(2,1)S(1)}, bf16[128,1024]{1,0:T(8,128)(2,1)S(1)}, u32[]{:S(2)}, u32[]{:S(2)}) collective-permute-start(bf16[128,1024]{1,0:T(8,128)(2,1)S(1)} %fusion.141), channel_id=1, source_target_pairs={{0,1},{1,2},{2,3},{3,0},{4,5},{5,6},{6,7},{7,4},{8,9},{9,10},{10,1... | collective-permute-start | bytes 786440 | tf_op jit(solution)/shard_map/ppermute | solution.py:30
  (792 shorter events, 579.0 us)
Async XLA Ops:
  16.3 372.4 %collective-permute-start.17 = (bf16[2,128,1024]{2,1,0:T(8,128)(2,1)}, bf16[2,128,1024]{2,1,0:T(8,128)(2,1)}, u32[]{:S(2)}, u32[]{:S(2)}) collective-permute-start(bf16[2,128,1024]{2,1,0:T(8,128)(2,1)} %select_select_fusion), channel_id=1, source_target_pairs={{0,2},{1,3},{2,0},{3,1},{4,6},{5,7},{6,4},{7,5},{8,10},{9,11},{10,... | collective-permute-start | bytes 1572872 | tf_op jit(solution)/shard_map/ppermute | solution.py:30
  20.3 368.4 %collective-permute-start.16 = (bf16[2,128,1024]{2,1,0:T(8,128)(2,1)}, bf16[2,128,1024]{2,1,0:T(8,128)(2,1)}, u32[]{:S(2)}, u32[]{:S(2)}) collective-permute-start(bf16[2,128,1024]{2,1,0:T(8,128)(2,1)} %select_select_fusion), channel_id=1, source_target_pairs={{0,1},{1,2},{2,3},{3,0},{4,5},{5,6},{6,7},{7,4},{8,9},{9,10},{10,1... | collective-permute-start | bytes 1572872 | tf_op jit(solution)/shard_map/ppermute | solution.py:30
  21.9 366.8 %collective-permute-start.18 = (bf16[2,128,1024]{2,1,0:T(8,128)(2,1)}, bf16[2,128,1024]{2,1,0:T(8,128)(2,1)}, u32[]{:S(2)}, u32[]{:S(2)}) collective-permute-start(bf16[2,128,1024]{2,1,0:T(8,128)(2,1)} %select_select_fusion), channel_id=1, source_target_pairs={{0,3},{1,0},{2,1},{3,2},{4,7},{5,4},{6,5},{7,6},{8,11},{9,8},{10,9... | collective-permute-start | bytes 1572872 | tf_op jit(solution)/shard_map/ppermute | solution.py:30
  24.1 463.4 %collective-permute-start.1 = (f32[2,8]{1,0:T(2,128)}, f32[2,8]{1,0:T(2,128)}, u32[]{:S(2)}, u32[]{:S(2)}) collective-permute-start(f32[2,8]{1,0:T(2,128)} %param.19), channel_id=1, source_target_pairs={{0,4},{4,0},{8,12},{12,8},{16,20},{20,16},{24,28},{28,24},{1,5},{5... | collective-permute-start | bytes 200 | tf_op jit(solution)/shard_map/ppermute | solution.py:43
  25.0 351.5 %collective-permute-start = (s32[2,130]{1,0:T(2,128)}, s32[2,130]{1,0:T(2,128)}, u32[]{:S(2)}, u32[]{:S(2)}) collective-permute-start(s32[2,130]{1,0:T(2,128)} %pad_add_fusion.1), channel_id=1, source_target_pairs={{0,4},{4,0},{8,12},{12,8},{16,20},{20,16},{24,28},{28,24},{1,5},{5... | collective-permute-start | bytes 3128 | tf_op jit(solution)/shard_map/ppermute | solution.py:43
  488.5 59.1 %collective-permute-start.7 = (bf16[512,1024]{1,0:T(8,128)(2,1)}, bf16[512,1024]{1,0:T(8,128)(2,1)}, u32[]{:S(2)}, u32[]{:S(2)}) collective-permute-start(bf16[512,1024]{1,0:T(8,128)(2,1)} %collective-permute-done.5.own.refs_4_), channel_id=1, source_target_pairs={{0,1},{1,2},{2,3},{3,0},{4,5},{5,6},{6,7},{7,4},{8,9},{9,10},{10,1... | collective-permute-start | bytes 3145736 | tf_op jit(solution)/shard_map/ppermute | solution.py:30
  553.8 61.0 %collective-permute-start.3 = (f32[512]{0:T(512)S(1)}, f32[512]{0:T(512)S(1)}, u32[]{:S(2)}, u32[]{:S(2)}) collective-permute-start(f32[512]{0:T(512)S(1)} %get-tuple-element.79), channel_id=1, source_target_pairs={{0,4},{4,0},{8,12},{12,8},{16,20},{20,16},{24,28},{28,24},{1,5},{5... | collective-permute-start | bytes 6152 | tf_op jit(solution)/shard_map/ppermute | solution.py:43
  641.3 186.9 %collective-permute-start.23 = (bf16[512,1024]{1,0:T(8,128)(2,1)}, bf16[512,1024]{1,0:T(8,128)(2,1)}, u32[]{:S(2)}, u32[]{:S(2)}) collective-permute-start(bf16[512,1024]{1,0:T(8,128)(2,1)} %slice.384), channel_id=1, source_target_pairs={{0,4},{4,0},{8,12},{12,8},{16,20},{20,16},{24,28},{28,24},{1,5},{5... | collective-permute-start | bytes 3145736 | tf_op jit(solution)/shard_map/ppermute | solution.py:43
  646.2 121.2 %collective-permute-start.28 = (bf16[512,1024]{1,0:T(8,128)(2,1)}, bf16[512,1024]{1,0:T(8,128)(2,1)}, u32[]{:S(2)}, u32[]{:S(2)}) collective-permute-start(bf16[512,1024]{1,0:T(8,128)(2,1)} %add_convert_fusion.3), channel_id=1, source_target_pairs={{0,1},{1,2},{2,3},{3,0},{4,5},{5,6},{6,7},{7,4},{8,9},{9,10},{10,1... | collective-permute-start | bytes 3145736 | tf_op jit(solution)/shard_map/ppermute | solution.py:30
  647.7 119.8 %collective-permute-start.24 = (bf16[512,1024]{1,0:T(8,128)(2,1)}, bf16[512,1024]{1,0:T(8,128)(2,1)}, u32[]{:S(2)}, u32[]{:S(2)}) collective-permute-start(bf16[512,1024]{1,0:T(8,128)(2,1)} %slice.386), channel_id=1, source_target_pairs={{0,4},{4,0},{8,12},{12,8},{16,20},{20,16},{24,28},{28,24},{1,5},{5... | collective-permute-start | bytes 3145736 | tf_op jit(solution)/shard_map/ppermute | solution.py:43
  706.6 67.1 %collective-permute-start.71 = (bf16[2,2,1344,128]{3,2,1,0:T(8,128)(2,1)}, bf16[2,2,1344,128]{3,2,1,0:T(8,128)(2,1)}, u32[]{:S(2)}, u32[]{:S(2)}) collective-permute-start(bf16[2,2,1344,128]{3,2,1,0:T(8,128)(2,1)} %dynamic-slice_bitcast_fusion.5), channel_id=1, source_target_pairs={{0,8},{4,12},{8,0},{12,4},{16,24},{20,28},{24,16},{28,20},{1,9},{5... | collective-permute-start | bytes 4128776 | tf_op jit(solution)/shard_map/ppermute | solution.py:43
  707.8 68.8 %collective-permute-start.73 = (bf16[2,2,1344,128]{3,2,1,0:T(8,128)(2,1)}, bf16[2,2,1344,128]{3,2,1,0:T(8,128)(2,1)S(1)}, u32[]{:S(2)}, u32[]{:S(2)}) collective-permute-start(bf16[2,2,1344,128]{3,2,1,0:T(8,128)(2,1)} %dynamic-slice_bitcast_fusion.4), channel_id=1, source_target_pairs={{0,16},{4,20},{8,24},{12,28},{16,0},{20,4},{24,8},{28,12},{1,17},{... | collective-permute-start | bytes 4128776 | tf_op jit(solution)/shard_map/ppermute | solution.py:43
  773.7 54.5 %collective-permute-start.29 = (bf16[512,1024]{1,0:T(8,128)(2,1)S(1)}, bf16[512,1024]{1,0:T(8,128)(2,1)S(1)}, u32[]{:S(2)}, u32[]{:S(2)}) collective-permute-start(bf16[512,1024]{1,0:T(8,128)(2,1)S(1)} %add_convert_fusion.2), channel_id=1, source_target_pairs={{0,1},{1,2},{2,3},{3,0},{4,5},{5,6},{6,7},{7,4},{8,9},{9,10},{10,1... | collective-permute-start | bytes 3145736 | tf_op jit(solution)/shard_map/ppermute | solution.py:30
  776.6 50.0 %collective-permute-start.72 = (bf16[2,1344,128]{2,1,0:T(8,128)(2,1)S(1)}, bf16[2,1344,128]{2,1,0:T(8,128)(2,1)S(1)}, u32[]{:S(2)}, u32[]{:S(2)}) collective-permute-start(bf16[2,1344,128]{2,1,0:T(8,128)(2,1)S(1)} %dynamic-slice_bitcast_fusion.18), channel_id=1, source_target_pairs={{0,16},{4,20},{8,24},{12,28},{16,0},{20,4},{24,8},{28,12},{1,17},{... | collective-permute-start | bytes 2064392 | tf_op jit(solution)/shard_map/ppermute | solution.py:43
  936.9 85.2 %collective-permute-start.30 = (f32[11,1024]{1,0:T(8,128)S(1)}, f32[11,1024]{1,0:T(8,128)S(1)}, u32[]{:S(2)}, u32[]{:S(2)}) collective-permute-start(f32[11,1024]{1,0:T(8,128)S(1)} %concatenate.69), channel_id=1, source_target_pairs={{0,4},{4,0},{8,12},{12,8},{16,20},{20,16},{24,28},{28,24},{1,5},{5... | collective-permute-start | bytes 135176 | tf_op jit(solution)/shard_map/ppermute | solution.py:43
  952.3 95.5 %collective-permute-start.38 = (bf16[2,2,32,1024]{3,2,1,0:T(8,128)(2,1)}, bf16[2,2,32,1024]{3,2,1,0:T(8,128)(2,1)}, u32[]{:S(2)}, u32[]{:S(2)}) collective-permute-start(bf16[2,2,32,1024]{3,2,1,0:T(8,128)(2,1)} %get-tuple-element.127), channel_id=1, source_target_pairs={{0,3},{1,0},{2,1},{3,2},{4,7},{5,4},{6,5},{7,6},{8,11},{9,8},{10,9... | collective-permute-start | bytes 786440 | tf_op jit(solution)/shard_map/ppermute | solution.py:30
  998.5 154.2 %collective-permute-start.42 = (bf16[4,4,256,1024]{3,2,1,0:T(8,128)(2,1)}, bf16[4,4,256,1024]{3,2,1,0:T(8,128)(2,1)}, u32[]{:S(2)}, u32[]{:S(2)}) collective-permute-start(bf16[4,4,256,1024]{3,2,1,0:T(8,128)(2,1)} %fusion.10), channel_id=1, source_target_pairs={{0,4},{4,0},{8,12},{12,8},{16,20},{20,16},{24,28},{28,24},{1,5},{5... | collective-permute-start | bytes 25165832 | tf_op jit(solution)/shard_map/ppermute | solution.py:43
  1021.6 104.9 %collective-permute-start.50 = (bf16[4,4,128,1024]{3,2,1,0:T(8,128)(2,1)}, bf16[4,4,128,1024]{3,2,1,0:T(8,128)(2,1)}, u32[]{:S(2)}, u32[]{:S(2)}) collective-permute-start(bf16[4,4,128,1024]{3,2,1,0:T(8,128)(2,1)} %fusion.27), channel_id=1, source_target_pairs={{0,4},{4,0},{8,12},{12,8},{16,20},{20,16},{24,28},{28,24},{1,5},{5... | collective-permute-start | bytes 12582920 | tf_op jit(solution)/shard_map/ppermute | solution.py:43
  1047.8 96.5 %collective-permute-start.58 = (bf16[4,4,128,1024]{3,2,1,0:T(8,128)(2,1)}, bf16[4,4,128,1024]{3,2,1,0:T(8,128)(2,1)}, u32[]{:S(2)}, u32[]{:S(2)}) collective-permute-start(bf16[4,4,128,1024]{3,2,1,0:T(8,128)(2,1)} %fusion.28), channel_id=1, source_target_pairs={{0,4},{4,0},{8,12},{12,8},{16,20},{20,16},{24,28},{28,24},{1,5},{5... | collective-permute-start | bytes 12582920 | tf_op jit(solution)/shard_map/ppermute | solution.py:43
  1163.3 80.5 %collective-permute-start.43 = (bf16[2,2,256,1024]{3,2,1,0:T(8,128)(2,1)S(1)}, bf16[2,2,256,1024]{3,2,1,0:T(8,128)(2,1)S(1)}, u32[]{:S(2)}, u32[]{:S(2)}) collective-permute-start(bf16[2,2,256,1024]{3,2,1,0:T(8,128)(2,1)S(1)} %dynamic-slice_bitcast_fusion.1), channel_id=1, source_target_pairs={{0,8},{4,12},{8,0},{12,4},{16,24},{20,28},{24,16},{28,20},{1,9},{5... | collective-permute-start | bytes 6291464 | tf_op jit(solution)/shard_map/ppermute | solution.py:43
  1164.2 82.2 %collective-permute-start.45 = (bf16[2,2,256,1024]{3,2,1,0:T(8,128)(2,1)S(1)}, bf16[2,2,256,1024]{3,2,1,0:T(8,128)(2,1)S(1)}, u32[]{:S(2)}, u32[]{:S(2)}) collective-permute-start(bf16[2,2,256,1024]{3,2,1,0:T(8,128)(2,1)S(1)} %dynamic-slice_bitcast_fusion), channel_id=1, source_target_pairs={{0,16},{4,20},{8,24},{12,28},{16,0},{20,4},{24,8},{28,12},{1,17},{... | collective-permute-start | bytes 6291464 | tf_op jit(solution)/shard_map/ppermute | solution.py:43
  1171.5 119.7 %collective-permute-start.75 = (bf16[2688,128]{1,0:T(8,128)(2,1)S(1)}, bf16[2688,128]{1,0:T(8,128)(2,1)S(1)}, u32[]{:S(2)}, u32[]{:S(2)}) collective-permute-start(bf16[2688,128]{1,0:T(8,128)(2,1)S(1)} %copy-done.85), channel_id=1, source_target_pairs={{0,4},{4,0},{8,12},{12,8},{16,20},{20,16},{24,28},{28,24},{1,5},{5... | collective-permute-start | bytes 2064392 | tf_op jit(solution)/shard_map/ppermute | solution.py:43
  1183.2 59.4 %collective-permute-start.52 = (bf16[2,128,1024]{2,1,0:T(8,128)(2,1)S(1)}, bf16[2,128,1024]{2,1,0:T(8,128)(2,1)S(1)}, u32[]{:S(2)}, u32[]{:S(2)}) collective-permute-start(bf16[2,128,1024]{2,1,0:T(8,128)(2,1)S(1)} %dynamic-slice_bitcast_fusion.22), channel_id=1, source_target_pairs={{0,16},{4,20},{8,24},{12,28},{16,0},{20,4},{24,8},{28,12},{1,17},{... | collective-permute-start | bytes 1572872 | tf_op jit(solution)/shard_map/ppermute | solution.py:43
  1192.6 56.0 %collective-permute-start.54 = (bf16[2,128,1024]{2,1,0:T(8,128)(2,1)S(1)}, bf16[2,128,1024]{2,1,0:T(8,128)(2,1)S(1)}, u32[]{:S(2)}, u32[]{:S(2)}) collective-permute-start(bf16[2,128,1024]{2,1,0:T(8,128)(2,1)S(1)} %dynamic-slice_bitcast_fusion.21), channel_id=1, source_target_pairs={{0,8},{4,12},{8,0},{12,4},{16,24},{20,28},{24,16},{28,20},{1,9},{5... | collective-permute-start | bytes 1572872 | tf_op jit(solution)/shard_map/ppermute | solution.py:43
  (211 other events, 4733.3 us)

commit v3 on v2

v3 whole, which is shorter than its diff:
```python
import functools

import jax
import jax.numpy as jnp
from jax import lax
from jax.experimental import pallas as pl
from jax.experimental.pallas import tpu as pltpu
from jax.sharding import PartitionSpec as P

HEADS = 16


eps_norm = 1e-05
entropy_weight = 0.25
mask_fill = -1e30
root_half = 0.7071067811865476
inv_root_tau = 0.3989422804014327


def grid_of(n_pb):
    cores = 2 if n_pb % 2 == 0 else 1
    chips = n_pb // cores
    wide = max(d for d in range(1, chips + 1) if chips % d == 0 and d * d <= chips)
    return chips // wide, wide, cores


def shifted(value, axis, step):
    if axis == "slot":
        size = lax.axis_size("slot")
        return lax.ppermute(value, "slot", [(i, (i + step) % size) for i in range(size)])
    n_pb = lax.axis_size("pb")
    tall, wide, cores = grid_of(n_pb)
    pairs = []
    for i in range(n_pb):
        y, x, c = i // (wide * cores), i // cores % wide, i % cores
        if axis == "y":
            y = (y + step) % tall
        elif axis == "x":
            x = (x + step) % wide
        else:
            c = (c + step) % cores
        pairs.append((i, (y * wide + x) * cores + c))
    return lax.ppermute(value, "pb", pairs)


def place_of(axis):
    if axis == "slot":
        return lax.axis_index("slot"), lax.axis_size("slot")
    tall, wide, cores = grid_of(lax.axis_size("pb"))
    i = lax.axis_index("pb")
    if axis == "y":
        return i // (wide * cores), tall
    if axis == "x":
        return i // cores % wide, wide
    return i % cores, cores


def after(value, *tokens):
    for token in tokens:
        first = token[(0,) * token.ndim].astype(jnp.float32)
        value = jnp.where(first == first, value, jnp.zeros_like(value))
    return value


def pick(value, index, dim):
    return lax.dynamic_index_in_dim(value, index, dim, keepdims=False)


def ring_gather(value, axis):
    me, size = place_of(axis)
    found = [(me, value)]
    for step in range(1, size):
        value = shifted(value, axis, 1)
        found.append(((me - step) % size, value))
    return found


def ring_scatter(value, axis, dim, late=None):
    me, size = place_of(axis)
    total = pick(value, (me - 1) % size, dim).astype(jnp.bfloat16)
    for step in range(1, size):
        part = pick(value, (me - 1 - step) % size, dim)
        total = shifted(total, axis, 1)
        if late is not None:
            total = after(total, late)
        total = total.astype(jnp.float32) + part.astype(jnp.float32)
        if step < size - 1:
            total = total.astype(jnp.bfloat16)
    return total


def ring_first(value, axis, dim):
    me, size = place_of(axis)
    return pick(value, (me - 1) % size, dim).astype(jnp.bfloat16)


def gather_all(shard):
    tall, wide, cores = grid_of(lax.axis_size("pb"))
    rows, width = shard.shape
    slots = lax.axis_size("slot")
    column = jnp.zeros((slots, rows, width), shard.dtype)
    for index, block in ring_gather(shard, "slot"):
        column = lax.dynamic_update_index_in_dim(column, block, index, 0)
    column = column.reshape(slots * rows, width)
    half = slots * rows // 2
    core, _ = place_of("core")
    whole = jnp.zeros((tall * wide, cores, 2, half, width), shard.dtype)
    for side, (first, second) in enumerate((("x", "y"), ("y", "x"))):
        part = column[side * half : (side + 1) * half]
        for at_first, block in ring_gather(part, first):
            for at_second, block in ring_gather(block, second):
                x, y = (at_first, at_second) if first == "x" else (at_second, at_first)
                for at_core, block in ring_gather(block, "core"):
                    whole = lax.dynamic_update_slice(
                        whole, block[None, None, None], (y * wide + x, at_core, side, 0, 0)
                    )
    return whole.reshape(tall * wide * cores, slots * rows, width)


def scatter_pb(value, lates=(None, None, None)):
    tall, wide, cores = grid_of(lax.axis_size("pb"))
    rest = value.shape[1:]
    value = value.reshape((tall * wide, cores) + rest)
    value = ring_scatter(value, "core", 1, lates[0]).astype(jnp.bfloat16)
    value = value.reshape((tall, wide) + rest)
    half = rest[0] // 2
    first = ring_scatter(value[:, :, :half], "x", 1, lates[1])
    second = ring_scatter(value[:, :, half:], "y", 0, lates[1])
    first = ring_scatter(first.astype(jnp.bfloat16), "y", 0, lates[2])
    second = ring_scatter(second.astype(jnp.bfloat16), "x", 0, lates[2])
    return jnp.concatenate([first, second], axis=0)


def scatter_all(value):
    n_pb, slots = lax.axis_size("pb"), lax.axis_size("slot")
    rows = value.shape[0] // (n_pb * slots)
    value = value.reshape((n_pb, slots, rows) + value.shape[1:])
    column = scatter_pb(value)
    return ring_scatter(column.astype(jnp.bfloat16), "slot", 0)


def scatter_slot(value, late):
    me, size = place_of("slot")
    parts = [
        after(shifted(pick(value, (me + step) % size, 0), "slot", step), late)
        for step in range(1, size)
    ]
    return sum([part.astype(jnp.float32) for part in parts], pick(value, me, 0).astype(jnp.float32))


def sum_all(value, axes):
    for axis in axes:
        me, size = place_of(axis)
        parts = [value] + [shifted(value, axis, step) for step in range(1, size)]
        placed = jnp.stack(parts)
        value = jnp.sum(placed[(me - jnp.arange(size)) % size], axis=0)
    return value


def to_slots(value):
    me, size = place_of("slot")
    every, questions, steps, width = value.shape
    chunks = value.reshape(every // size, size, questions, steps, width)
    result = jnp.zeros((every // size, questions, size, steps, width), value.dtype)
    for step in range(size):
        block = pick(chunks, (me + step) % size, 1)
        if step:
            block = shifted(block, "slot", step)
        result = lax.dynamic_update_index_in_dim(result, block, (me - step) % size, 2)
    return result.reshape(every // size, questions, size * steps, width)


def leave_slots(value):
    me, size = place_of("slot")
    own, questions, steps, width = value.shape
    chunks = value.reshape(own, questions, size, steps // size, width)
    return [pick(chunks, (me + step) % size, 2) for step in range(size)]


def to_positions(blocks, late=None):
    me, size = place_of("slot")
    own, questions, steps, width = blocks[0].shape
    result = jnp.zeros((own, size, questions, steps, width), blocks[0].dtype)
    for step, block in enumerate(blocks):
        if step:
            block = shifted(block, "slot", step)
            block = block if late is None else after(block, late)
        result = lax.dynamic_update_index_in_dim(result, block, (me - step) % size, 1)
    return result.reshape(size * own, questions, steps, width)


def product(left, right):
    return jnp.dot(left, right, preferred_element_type=jnp.float32)


def contract_rows(left, right):
    return lax.dot_general(
        left, right, (((0,), (0,)), ((), ())), preferred_element_type=jnp.float32
    )


def contract_cols(left, right):
    return lax.dot_general(
        left, right, (((1,), (1,)), ((), ())), preferred_element_type=jnp.float32
    )


def norm_forward(resid, gain, shift):
    row_mean = jnp.mean(resid, axis=-1, keepdims=True)
    centered = resid - row_mean
    inv_root = lax.rsqrt(jnp.mean(centered * centered, axis=-1, keepdims=True) + eps_norm)
    normed = centered * inv_root
    return (normed * gain + shift, normed, inv_root)


def norm_backward(grad_out, normed, inv_root, gain):
    scaled = grad_out * gain
    grad_in = inv_root * (
        scaled
        - jnp.mean(scaled, axis=-1, keepdims=True)
        - normed * jnp.mean(scaled * normed, axis=-1, keepdims=True)
    )
    return (grad_in, jnp.sum(grad_out * normed, axis=0), jnp.sum(grad_out, axis=0))


def two_heads(value):
    left = lax.broadcasted_iota(jnp.int32, value.shape, 1) < value.shape[1] // 2
    none = jnp.zeros_like(value)
    return jnp.concatenate([jnp.where(left, value, none), jnp.where(left, none, value)], axis=0)


def one_pair(value):
    rows = value.shape[0] // 2
    left = lax.broadcasted_iota(jnp.int32, (rows, value.shape[1]), 1) < value.shape[1] // 2
    return jnp.where(left, value[:rows], value[rows:])


def pair_scores(info, causal, queries, key_rows):
    scores = lax.dot_general(
        queries, key_rows, (((1,), (1,)), ((), ())), preferred_element_type=jnp.float32
    )
    column = lax.broadcasted_iota(jnp.int32, scores.shape, 1)
    if causal:
        row = lax.broadcasted_iota(jnp.int32, scores.shape, 0)
        allowed = column <= jnp.where(row < scores.shape[0] // 2, row, row - scores.shape[0] // 2)
    else:
        allowed = column < info[pl.program_id(0)]
    return jnp.where(allowed, scores, mask_fill)


def attend_kernel(causal, info, queries, keys, values, out, logs):
    steps, width = queries.shape
    lane = lax.broadcasted_iota(jnp.int32, (steps, 128), 1)
    kept = jnp.zeros((steps, 128), jnp.float32)
    for pair in range(width // 128):
        here = slice(pair * 128, (pair + 1) * 128)
        scores = pair_scores(info, causal, two_heads(queries[:, here]), keys[:, here])
        row_max = jnp.max(scores, axis=1, keepdims=True)
        expos = jnp.exp(scores - row_max)
        row_sum = jnp.sum(expos, axis=1, keepdims=True)
        probs = (expos * (1.0 / row_sum)).astype(jnp.bfloat16)
        out[:, here] = one_pair(
            jnp.dot(probs, values[:, here], preferred_element_type=jnp.float32)
        ).astype(jnp.bfloat16)
        log = row_max + jnp.log(row_sum)
        kept = jnp.where(lane == 2 * pair, log[:steps], kept)
        kept = jnp.where(lane == 2 * pair + 1, log[steps:], kept)
    logs[...] = kept


def attend_back_kernel(causal, info, queries, keys, values, logs, grads, *refs):
    d_queries, d_keys, d_values = refs[-3:]
    steps, width = queries.shape
    rows_first = (((0,), (0,)), ((), ()))
    for pair in range(width // 128):
        here = slice(pair * 128, (pair + 1) * 128)
        both = two_heads(queries[:, here])
        both_grads = two_heads(grads[:, here])
        log = jnp.concatenate(
            [logs[:, 2 * pair : 2 * pair + 1], logs[:, 2 * pair + 1 : 2 * pair + 2]], axis=0
        )
        probs = jnp.exp(pair_scores(info, causal, both, keys[:, here]) - log)
        d_probs = lax.dot_general(
            both_grads, values[:, here], (((1,), (1,)), ((), ())), preferred_element_type=jnp.float32
        )
        d_values[:, here] = lax.dot_general(
            probs.astype(jnp.bfloat16), both_grads, rows_first, preferred_element_type=jnp.float32
        ).astype(jnp.bfloat16)
        delta = jnp.sum(d_probs * probs, axis=1, keepdims=True)
        d_scores = (probs * (d_probs - delta)).astype(jnp.bfloat16)
        d_queries[:, here] = one_pair(
            jnp.dot(d_scores, keys[:, here], preferred_element_type=jnp.float32)
        ).astype(jnp.bfloat16)
        d_keys[:, here] = lax.dot_general(
            d_scores, both, rows_first, preferred_element_type=jnp.float32
        ).astype(jnp.bfloat16)


def attend(causal, lengths, queries, keys, values, logs=None, grads=None, earlier=()):
    count = lengths.shape[0]
    width = queries.shape[1]
    steps, spans = queries.shape[0] // count, keys.shape[0] // count
    short = pl.BlockSpec((steps, width), lambda i, s: (i, 0))
    long = pl.BlockSpec((spans, width), lambda i, s: (i, 0))
    thin = pl.BlockSpec((steps, 128), lambda i, s: (i, 0))
    like = lambda value: jax.ShapeDtypeStruct(value.shape, jnp.bfloat16)
    if grads is None:
        kernel, operands = attend_kernel, (queries, keys, values)
        in_specs, out_specs = [short, long, long], [short, thin]
        out_shape = [like(queries), jax.ShapeDtypeStruct((queries.shape[0], 128), jnp.float32)]
    else:
        kernel, operands = attend_back_kernel, (queries, keys, values, logs, grads, *earlier)
        in_specs, out_specs = [short, long, long, thin, short], [short, long, long]
        in_specs += [pl.BlockSpec(memory_space=pl.ANY)] * len(earlier)
        out_shape = [like(queries), like(keys), like(values)]
    flops = (4 if grads is None else 10) * queries.shape[0] * spans * width
    return pl.pallas_call(
        functools.partial(kernel, causal),
        grid_spec=pltpu.PrefetchScalarGridSpec(
            num_scalar_prefetch=1, grid=(count,), in_specs=in_specs, out_specs=out_specs
        ),
        out_shape=out_shape,
        compiler_params=pltpu.CompilerParams(vmem_limit_bytes=48 << 20),
        cost_estimate=pl.CostEstimate(
            flops=4 * flops, bytes_accessed=8 * keys.shape[0] * width, transcendentals=0
        ),
        name=("self" if causal else "cross") + ("_attend" if grads is None else "_attend_back"),
    )(lengths, *operands)


def gelu_parts(value):
    place = 1.0 / (1.0 + 0.3275911 * root_half * jnp.abs(value))
    bell = jnp.exp(-0.5 * value * value)
    series = 1.061405429
    for factor in (-1.453152027, 1.421413741, -0.284496736, 0.254829592):
        series = series * place + factor
    tail = 0.5 * series * place * bell
    share = jnp.where(value > 0.0, 1.0 - tail, tail)
    return value * share, share + value * (inv_root_tau * bell)


PIECE = 128
CHUNK = 256


def vocab_tile(share):
    return max(d for d in range(16, 901, 16) if share % d == 0)


def columns(block):
    return jnp.concatenate([block] * 16, axis=0).T


def each_count(live, chunks, run):
    for taken in range(1, chunks + 1):
        above = live > (taken - 1) * CHUNK
        upto = live <= taken * CHUNK if taken < chunks else live >= 0

        @pl.when(jnp.logical_and(above, upto))
        def _():
            run(taken)


def piece_places(info, step, count):
    base = 1 + step * (count + 1)
    return [pl.multiple_of(info[base + i], 16) for i in range(count)], info[base + count]


def rows_kernel(step, info, ids, own, mate, table, *refs):
    expo, packed, tops, own_sums, mate_sums, own_logs, mate_logs, acc, top, total, marks = refs[-11:]
    expo, packed, tops = expo.at[0], packed.at[0], tops.at[0]
    tile = pl.program_id(0)
    wide = table.shape[0]
    pieces = own.shape[0] // PIECE
    count = 2 * pieces
    places, live = piece_places(info, step, count)

    @pl.when(tile == 0)
    def _():
        acc[...] = jnp.zeros_like(acc)
        top[...] = jnp.full_like(top, mask_fill)
        total[...] = jnp.zeros_like(total)
        tops[...] = jnp.zeros_like(tops)
        packed[...] = jnp.zeros_like(packed)
        marks[...] = jnp.full_like(marks, -1.0)
        for piece in range(count):
            side = own if piece < pieces else mate
            low = piece % pieces * PIECE
            packed[pl.ds(places[piece], PIECE), :] = side[low : low + PIECE, :]
            marks[pl.ds(places[piece], PIECE), :] = columns(ids[piece])

    lane = lax.broadcasted_iota(jnp.int32, (CHUNK, 128), 1)
    column = lax.broadcasted_iota(jnp.int32, (CHUNK, wide), 1)

    def scores(chunk):
        return lax.dot_general(
            packed[chunk * CHUNK : (chunk + 1) * CHUNK, :],
            table[...],
            (((1,), (1,)), ((), ())),
            preferred_element_type=jnp.float32,
        )

    def soften(chunk, logits):
        here = slice(chunk * CHUNK, (chunk + 1) * CHUNK)
        target = marks[here, 0:1].astype(jnp.int32) - tile * wide
        logits = jnp.where(column == target, mask_fill, logits)
        before = top[here, 0:1]
        now = jnp.maximum(before, jnp.max(logits, axis=1, keepdims=True))
        fade = jnp.exp(before - now)
        grown = jnp.exp(logits - now)
        total[here, :] = jnp.broadcast_to(
            total[here, 0:1] * fade + jnp.sum(grown, axis=1, keepdims=True), (CHUNK, 128)
        )
        top[here, :] = jnp.broadcast_to(now, (CHUNK, 128))
        tops[here, :] = jnp.where(lane == tile, now, tops[here, :])
        grown = grown.astype(jnp.bfloat16)
        expo[0, here, :] = grown
        return here, grown, fade

    def gather(here, grown, fade):
        acc[here, :] = acc[here, :] * fade + jnp.dot(
            grown, table[...], preferred_element_type=jnp.float32
        )

    def run(taken):
        logits = [scores(0)]
        late = None
        for chunk in range(taken):
            if chunk + 1 < taken:
                logits.append(scores(chunk + 1))
            ready = soften(chunk, logits[chunk])
            if late is not None:
                gather(*late)
            late = ready
        gather(*late)

    each_count(live, count * PIECE // CHUNK, run)

    @pl.when(tile == pl.num_programs(0) - 1)
    def _():
        for piece in range(count):
            here = pl.ds(places[piece], PIECE)
            mass = total[here, :]
            share = jnp.where(mass > 0.0, 1.0 / jnp.maximum(mass, 1e-30), 0.0)[:, 0:1]
            sums, logs = (own_sums, own_logs) if piece < pieces else (mate_sums, mate_logs)
            low = piece % pieces * PIECE
            sums[low : low + PIECE, :] = (acc[here, :] * share).astype(jnp.bfloat16)
            logs[piece % pieces] = (top[here, :] + jnp.log(jnp.maximum(mass, 1e-30))).T[0:8]


def rows_pass(step, steps, info, ids, own, mate, table, cores, kept, earlier):
    group, width = own.shape
    share = table.shape[0] // cores
    wide = vocab_tile(share)
    tiles = share // wide
    rows = 2 * group
    count = rows // PIECE
    room = rows + PIECE
    whole = lambda i, s: (0, 0)
    cube = lambda i, s: (0, 0, 0)
    return pl.pallas_call(
        functools.partial(rows_kernel, step),
        grid_spec=pltpu.PrefetchScalarGridSpec(
            num_scalar_prefetch=1,
            grid=(tiles,),
            in_specs=[
                pl.BlockSpec((count, 8, 128), lambda i, s: (step, 0, 0)),
                pl.BlockSpec((group, width), whole),
                pl.BlockSpec((group, width), whole),
                pl.BlockSpec((wide, width), lambda i, s: (s[0] * tiles + i, 0)),
            ]
            + [pl.BlockSpec(memory_space=pl.ANY)] * (len(kept) + len(earlier)),
            out_specs=[
                pl.BlockSpec((1, 1, rows, wide), lambda i, s: (step, i, 0, 0)),
                pl.BlockSpec((1, room, width), lambda i, s: (step, 0, 0)),
                pl.BlockSpec((1, room, 128), lambda i, s: (step, 0, 0)),
                pl.BlockSpec((group, width), whole),
                pl.BlockSpec((group, width), whole),
                pl.BlockSpec((count // 2, 8, 128), cube),
                pl.BlockSpec((count // 2, 8, 128), cube),
            ],
            scratch_shapes=[
                pltpu.VMEM((room, width), jnp.float32),
                pltpu.VMEM((room, 128), jnp.float32),
                pltpu.VMEM((room, 128), jnp.float32),
                pltpu.VMEM((room, 128), jnp.float32),
            ],
        ),
        out_shape=[
            jax.ShapeDtypeStruct((steps, tiles, rows, wide), jnp.bfloat16),
            jax.ShapeDtypeStruct((steps, room, width), jnp.bfloat16),
            jax.ShapeDtypeStruct((steps, room, 128), jnp.float32),
            jax.ShapeDtypeStruct((group, width), jnp.bfloat16),
            jax.ShapeDtypeStruct((group, width), jnp.bfloat16),
            jax.ShapeDtypeStruct((count // 2, 8, 128), jnp.float32),
            jax.ShapeDtypeStruct((count // 2, 8, 128), jnp.float32),
        ],
        input_output_aliases={5 + place: place for place in range(len(kept))},
        compiler_params=pltpu.CompilerParams(vmem_limit_bytes=60 << 20),
        cost_estimate=pl.CostEstimate(
            flops=4 * rows * share * width, bytes_accessed=4 * share * width, transcendentals=0
        ),
        name=f"rows_pass_{step}",
    )(info, ids, own, mate, table, *kept, *earlier)


def join_kernel(own, other, own_log, other_log, out):
    for piece in range(own_log.shape[0]):
        here = slice(piece * PIECE, (piece + 1) * PIECE)
        log = jnp.logaddexp(own_log[piece], other_log[piece])
        left = columns(jnp.exp(own_log[piece] - log))[:, 0:1]
        right = columns(jnp.exp(other_log[piece] - log))[:, 0:1]
        out[here, :] = (
            own[here, :].astype(jnp.float32) * left + other[here, :].astype(jnp.float32) * right
        ).astype(jnp.bfloat16)


def join_pass(own, other, own_log, other_log):
    rows, width = own.shape
    flat = pl.BlockSpec((CHUNK, width), lambda i: (i, 0))
    cube = pl.BlockSpec((CHUNK // PIECE, 8, 128), lambda i: (i, 0, 0))
    return pl.pallas_call(
        join_kernel,
        grid=(rows // CHUNK,),
        in_specs=[flat, flat, cube, cube],
        out_specs=flat,
        out_shape=jax.ShapeDtypeStruct((rows, width), jnp.bfloat16),
        name="join_pass",
    )(own, other, own_log, other_log)


def home_kernel(count, logs, weight, targets, *refs):
    parts, out = refs[:count], refs[-1]
    log = logs[0]
    share = jnp.exp(log - jnp.max(log, axis=0, keepdims=True))
    share = columns(share / jnp.sum(share, axis=0, keepdims=True))
    mean = parts[0][...].astype(jnp.float32) * share[:, 0:1]
    for place in range(1, count):
        mean = mean + parts[place][...].astype(jnp.float32) * share[:, place : place + 1]
    out[...] = columns(weight[0])[:, 0:1] * (targets[0] - mean)


def home_pass(logs, weight, targets, parts, earlier):
    rows, width = parts[0].shape
    questions = targets.shape[0]
    flat = pl.BlockSpec((PIECE, width), lambda i: (i, 0))
    cube = pl.BlockSpec((1, 8, 128), lambda i: (i, 0, 0))
    return pl.pallas_call(
        functools.partial(home_kernel, len(parts)),
        grid=(rows // PIECE,),
        in_specs=[cube, cube, pl.BlockSpec((1, PIECE, width), lambda i: (i % questions, 0, 0))]
        + [flat] * len(parts)
        + [pl.BlockSpec(memory_space=pl.ANY)] * len(earlier),
        out_specs=flat,
        out_shape=jax.ShapeDtypeStruct((rows, width), jnp.float32),
        name="home_pass",
    )(logs, weight, targets, *parts, *earlier)


def table_kernel(first, info, facts, tops, rows, expos, *refs):
    outs, acc, scales = refs[-4:-2], refs[-2], refs[-1]
    tile = pl.program_id(0) + first
    sources, _, both, wide = expos.shape
    count = both // PIECE

    @pl.when(pl.program_id(0) == 0)
    def _():
        def ready(source, _):
            places, _ = piece_places(info, source, count)
            scales[source] = jnp.zeros(scales.shape[1:], jnp.float32)
            for piece in range(count):
                scales[source, pl.ds(places[piece], PIECE), :] = columns(facts[source * count + piece])
            raw = scales[source]
            lane = lax.broadcasted_iota(jnp.int32, raw.shape, 1)
            weight = raw[:, 0:1]
            spread = jnp.where(weight == 0.0, 0.0, -weight * jnp.exp(tops[source] - raw[:, 1:2]))
            spread = jnp.where(lane == 127, raw[:, 2:3], spread)
            scales[source] = jnp.where(lane == 126, raw[:, 3:4], spread)
            return 0

        lax.fori_loop(0, sources, ready, 0)

    acc[...] = jnp.zeros_like(acc)

    def add(source, begin, size):
        here = pl.ds(pl.multiple_of(begin, CHUNK), size)
        scale = scales[source, here, :]
        lane = lax.broadcasted_iota(jnp.int32, (size, 128), 1)
        column = lax.broadcasted_iota(jnp.int32, (size, wide), 1)
        spread = jnp.sum(jnp.where(lane == tile, scale, 0.0), axis=1, keepdims=True)
        target = scale[:, 126:127].astype(jnp.int32) - tile * wide
        grad = expos[source, 0, here, :].astype(jnp.float32) * spread
        grad = jnp.where(column == target, scale[:, 127:128], grad).astype(jnp.bfloat16)
        acc[...] += lax.dot_general(
            grad,
            rows[source, here, :],
            (((0,), (0,)), ((), ())),
            preferred_element_type=jnp.float32,
        )

    def add_source(source, _):
        live = info[1 + source * (count + 1) + count]
        chunks = (live + CHUNK - 1) // CHUNK

        def add_two(pair, _):
            add(source, pair * (2 * CHUNK), 2 * CHUNK)
            return 0

        lax.fori_loop(0, chunks // 2, add_two, 0)

        @pl.when(chunks % 2 == 1)
        def _():
            add(source, (chunks - 1) * CHUNK, CHUNK)

        return 0

    lax.fori_loop(0, sources, add_source, 0)
    half = wide // 2
    for side, out in enumerate(outs):
        for place in range(out.shape[0]):
            size = out.shape[3]
            out[place, 0] = acc[
                side * half : (side + 1) * half, place * size : (place + 1) * size
            ].astype(jnp.bfloat16)


def table_pass(info, facts, tops, rows, expos, first, tiles, n_pb, earlier):
    sources, _, both, wide = expos.shape
    _, room, width = rows.shape
    own = width // n_pb
    once = pl.Buffered(1)
    cube = lambda i, s: (0, 0, 0)
    return pl.pallas_call(
        functools.partial(table_kernel, first),
        grid_spec=pltpu.PrefetchScalarGridSpec(
            num_scalar_prefetch=1,
            grid=(tiles,),
            in_specs=[
                pl.BlockSpec(facts.shape, cube, pipeline_mode=once),
                pl.BlockSpec(tops.shape, cube, pipeline_mode=once),
                pl.BlockSpec(rows.shape, cube, pipeline_mode=once),
                pl.BlockSpec((sources, 1, both, wide), lambda i, s: (0, i + first, 0, 0)),
            ]
            + [pl.BlockSpec(memory_space=pl.ANY)] * len(earlier),
            out_specs=[pl.BlockSpec((n_pb, 1, wide // 2, own), lambda i, s: (0, i, 0, 0))] * 2,
            scratch_shapes=[
                pltpu.VMEM((wide, width), jnp.float32),
                pltpu.VMEM((sources, room, 128), jnp.float32),
            ],
        ),
        out_shape=[jax.ShapeDtypeStruct((n_pb, tiles, wide // 2, own), jnp.bfloat16)] * 2,
        compiler_params=pltpu.CompilerParams(vmem_limit_bytes=60 << 20),
        cost_estimate=pl.CostEstimate(
            flops=2 * sources * both * tiles * wide * width,
            bytes_accessed=4 * sources * both * tiles * wide,
            transcendentals=0,
        ),
        name=f"table_pass_{first}",
    )(info, facts, tops, rows, expos, *earlier)


def gather_kernel(*refs):
    mats, rows = refs[:3], refs[3:5]
    full, laid = refs[5:8], refs[8:10]
    send, recv, near = refs[10:]
    slots = full[0].shape[1]
    pb, place = lax.axis_index("pb"), lax.axis_index("slot")
    mate = pb // 2 * 2 + (pb + 1) % 2
    side_x = pb // 4 * 4 + (pb + 2) % 4
    side_y = (pb + 4) % 8
    corner = (side_x + 4) % 8
    barrier = pltpu.get_barrier_semaphore()
    partners = [(mate, place), (side_x, place), (side_y, place)]
    partners += [(pb, (place + step) % slots) for step in range(1, slots)]
    for partner in partners:
        pl.semaphore_signal(barrier, inc=1, device_id=partner, device_id_type=pl.DeviceIdType.MESH)
    pl.semaphore_wait(barrier, len(partners))

    sent, unread, stays, ready = [], {}, [], {}

    def push(source, target, device):
        copy = pltpu.make_async_remote_copy(
            src_ref=source,
            dst_ref=target,
            send_sem=send.at[len(sent)],
            recv_sem=recv.at[len(sent)],
            device_id=device,
            device_id_type=pl.DeviceIdType.MESH,
        )
        copy.start()
        unread[len(sent)] = copy
        sent.append(copy)
        return len(sent) - 1

    def read(number):
        unread.pop(number).wait_recv()

    def put(source, target):
        copy = pltpu.make_async_copy(source, target, near.at[len(stays)])
        copy.start()
        stays.append(copy)

    def move_rows(step):
        goal = (place + step) % slots
        for source, target in zip(rows, laid):
            block = source.at[:, goal]
            spot = target.at[:, :, place]
            if step:
                push(block, spot, (pb, goal))
            else:
                put(block, spot)

    def part(mat, at_pb, origin, half):
        size = full[mat].shape[2] // 2
        return full[mat].at[at_pb, origin, pl.ds(half * size, size)]

    def own_moves(step, mat, origin, source):
        size = full[mat].shape[2] // 2
        first, second = (source.at[pl.ds(half * size, size)] for half in range(2))
        first_at, second_at = (part(mat, pb, origin, half) for half in range(2))
        ready[step, mat] = [
            push(first, first_at, (side_x, place)),
            push(second, second_at, (side_y, place)),
            push(first, first_at, (side_y, place)),
            push(second, second_at, (side_x, place)),
        ]
        push(source, full[mat].at[pb, origin], (mate, place))

    def onward(step, mat, origin):
        over_x, over_y, _, _ = ready[step, mat]
        read(over_x)
        block = part(mat, side_x, origin, 0)
        ready[step, mat].append(push(block, block, (side_y, place)))
        push(block, block, (mate, place))
        read(over_y)
        block = part(mat, side_y, origin, 1)
        ready[step, mat].append(push(block, block, (side_x, place)))
        push(block, block, (mate, place))

    def finish(step, mat, origin):
        _, _, over_y, over_x, first, second = ready[step, mat]
        for number, at_pb, half in (
            (over_y, side_y, 0),
            (over_x, side_x, 1),
            (first, corner, 0),
            (second, corner, 1),
        ):
            read(number)
            block = part(mat, at_pb, origin, half)
            push(block, block, (mate, place))

    count = len(mats)
    following = (pb, (place + 1) % slots)
    ring = [push(mats[mat], full[mat].at[pb, place], following) for mat in range(count)]
    for mat in range(count):
        own_moves(0, mat, place, mats[mat])
        put(mats[mat], full[mat].at[pb, place])
    move_rows(1)
    move_rows(0)
    for step in range(1, slots + 1):
        origin = (place + slots - step) % slots
        before = (place + slots - step + 1) % slots
        if step < slots:
            for mat in range(count):
                read(ring[mat])
                block = full[mat].at[pb, origin]
                if step < slots - 1:
                    ring[mat] = push(block, block, following)
                own_moves(step, mat, origin, block)
        if step == 1:
            move_rows(slots - 1)
        if step == 2:
            for other in range(2, slots - 1):
                move_rows(other)
        for mat in range(count):
            onward(step - 1, mat, before)
        for mat in range(count):
            finish(step - 1, mat, before)
    for number in sorted(unread):
        read(number)
    for copy in sent:
        copy.wait_send()
    for copy in stays:
        copy.wait()


def gather_inputs(x_in, memory, attn_w, ffn_in, ffn_out):
    n_pb, slots = lax.axis_size("pb"), lax.axis_size("slot")
    mats, rows = (attn_w, ffn_in, ffn_out), (x_in, memory)
    width = attn_w.shape[1]
    rows = [row.reshape((-1, slots) + row.shape[1:]) for row in rows]
    if (n_pb, slots) != (8, 4):
        return (
            to_slots(x_in),
            to_slots(memory),
            *(gather_all(mat).reshape(-1, width) for mat in mats),
        )
    shapes = [jax.ShapeDtypeStruct((n_pb, slots) + mat.shape, mat.dtype) for mat in mats]
    for row in rows:
        own, _, questions, steps, _ = row.shape
        shapes.append(jax.ShapeDtypeStruct((own, questions, slots, steps, width), row.dtype))
    copies = 13 * len(mats) * slots + (slots - 1) * (len(mats) + len(rows))
    anywhere = pl.BlockSpec(memory_space=pl.ANY)
    *full, x_here, mem_here = pl.pallas_call(
        gather_kernel,
        in_specs=[anywhere] * 5,
        out_specs=[anywhere] * 5,
        out_shape=shapes,
        scratch_shapes=[
            pltpu.SemaphoreType.DMA((copies,)),
            pltpu.SemaphoreType.DMA((copies,)),
            pltpu.SemaphoreType.DMA((len(mats) + len(rows),)),
        ],
        compiler_params=pltpu.CompilerParams(collective_id=0, has_side_effects=True),
        name="gather_inputs",
    )(*mats, *rows)
    own, questions, _, _, _ = x_here.shape
    return (
        x_here.reshape(own, questions, -1, width),
        mem_here.reshape(own, questions, -1, width),
        *(mat.reshape(-1, width) for mat in full),
    )


UNIT = 64


def scatter_kernel(*refs):
    mats, rows, few = refs[:3], refs[3], refs[4]
    outs, laid, few_out = refs[5:8], refs[8], refs[9]
    (from_core, kept, wide_x, wide_y, narrow_x, narrow_y, from_slot, few_here, few_there, few_slot) = refs[10:20]
    send, recv, near = refs[20:]
    depth = kept.shape[0]
    slots = mats[0].shape[2]
    pb, place = lax.axis_index("pb"), lax.axis_index("slot")
    core, at_x, at_y = pb % 2, pb // 2 % 2, pb // 4
    mate = (pb // 2 * 2 + (pb + 1) % 2, place)
    side_x = (pb // 4 * 4 + (pb + 2) % 4, place)
    side_y = ((pb + 4) % 8, place)
    barrier = pltpu.get_barrier_semaphore()
    partners = [mate, side_x, side_y]
    partners += [(pb, (place + step) % slots) for step in range(1, slots)]
    for partner in partners:
        pl.semaphore_signal(barrier, inc=1, device_id=partner, device_id_type=pl.DeviceIdType.MESH)
    pl.semaphore_wait(barrier, len(partners))

    sent = []

    def push(source, target, device):
        copy = pltpu.make_async_remote_copy(
            src_ref=source,
            dst_ref=target,
            send_sem=send.at[len(sent)],
            recv_sem=recv.at[len(sent)],
            device_id=device,
            device_id_type=pl.DeviceIdType.MESH,
        )
        copy.start()
        sent.append(copy)
        return copy

    stays = []

    def put(source, target):
        copy = pltpu.make_async_copy(source, target, near.at[len(stays)])
        copy.start()
        stays.append(copy)
        return copy

    units = [
        (mat, unit)
        for mat in (1, 2, 0)
        for unit in range(mats[mat].shape[3] // UNIT)
    ]

    def block(number, which):
        mat, unit = units[number]
        return mats[mat].at[:, which, :, pl.ds(unit * UNIT, UNIT)]

    half = UNIT // 2
    first, second = pl.ds(0, half), pl.ds(half, half)
    by_core = [push(block(n, 1 - core), from_core.at[n], mate) for n in range(len(units))]
    loads = {n: put(block(n, core), kept.at[n % depth]) for n in range(min(depth, len(units)))}
    by_rows = []
    for step in range(1, slots):
        goal = (place + step) % slots
        by_rows.append(push(rows.at[:, :, goal], laid.at[:, place], (pb, goal)))
    at_home = put(rows.at[:, :, place], laid.at[:, place])
    by_few = push(few, few_there.at[0], mate)

    def total(left, right):
        return (left.astype(jnp.float32) + right.astype(jnp.float32)).astype(jnp.bfloat16)

    over, across, along = {}, {}, {}

    def from_cores(n):
        slot = n % depth
        by_core[n].wait_recv()
        loads[n].wait()

        def step(i, _):
            y, x, z = i // (2 * slots), i // slots % 2, i % slots
            kept[slot, 2 * y + x, z] = total(kept[slot, 2 * y + x, z], from_core[n, 2 * y + x, z])
            return 0

        lax.fori_loop(0, 4 * slots, step, 0)
        over[n] = [
            push(kept.at[slot, 1 - at_x, :, first], wide_x.at[n, 0], side_x),
            push(kept.at[slot, 2 + 1 - at_x, :, first], wide_x.at[n, 1], side_x),
            push(kept.at[slot, pl.ds(2 * (1 - at_y), 2), :, second], wide_y.at[n], side_y),
        ]

    def over_first(n):
        slot = n % depth
        for copy in over[n]:
            copy.wait_recv()

        def step(i, _):
            side, z = i // slots, i % slots
            spot = 2 * side + at_x
            kept[slot, spot, z, 0:half] = total(kept[slot, spot, z, 0:half], wide_x[n, side, z])
            spot = 2 * at_y + side
            kept[slot, spot, z, half:UNIT] = total(kept[slot, spot, z, half:UNIT], wide_y[n, side, z])
            return 0

        lax.fori_loop(0, 2 * slots, step, 0)
        across[n] = [
            push(kept.at[slot, 2 * (1 - at_y) + at_x, :, first], narrow_y.at[n], side_y),
            push(kept.at[slot, 2 * at_y + 1 - at_x, :, second], narrow_x.at[n], side_x),
        ]

    def over_second(n):
        slot = n % depth
        for copy in across[n]:
            copy.wait_recv()
        spot = 2 * at_y + at_x

        def step(z, _):
            kept[slot, spot, z, 0:half] = total(kept[slot, spot, z, 0:half], narrow_y[n, z])
            kept[slot, spot, z, half:UNIT] = total(kept[slot, spot, z, half:UNIT], narrow_x[n, z])
            return 0

        lax.fori_loop(0, slots, step, 0)
        along[n] = []
        for step_on in range(1, slots):
            goal = (place + step_on) % slots
            along[n].append(push(kept.at[slot, spot, goal], from_slot.at[n, step_on - 1], (pb, goal)))

    def over_slots(n):
        slot = n % depth
        mat, unit = units[n]
        for copy in along[n]:
            copy.wait_recv()
        here = kept[slot, 2 * at_y + at_x, place].astype(jnp.float32)
        for step_on in range(1, slots):
            here = here + from_slot[n, step_on - 1].astype(jnp.float32)
        outs[mat][unit * UNIT : (unit + 1) * UNIT, :] = here
        if n + depth < len(units):
            for copy in over[n] + across[n] + along[n]:
                copy.wait_send()
            loads[n + depth] = put(block(n + depth, core), kept.at[slot])

    stages = (from_cores, over_first, over_second, over_slots)
    for turn in range(len(units) + len(stages) - 1):
        for lag, stage in enumerate(stages):
            if 0 <= turn - lag < len(units):
                stage(turn - lag)
        if turn == 0:
            by_few.wait_recv()
            few_here[0] = few[...] + few_there[0]
            by_few = push(few_here.at[0], few_there.at[1], side_x)
        if turn == 1:
            by_few.wait_recv()
            few_here[1] = few_here[0] + few_there[1]
            by_few = push(few_here.at[1], few_there.at[2], side_y)
        if turn == 2:
            by_few.wait_recv()
            few_here[2] = few_here[1] + few_there[2]
            few_slot[place] = few_here[2]
            by_few = [
                push(few_here.at[2], few_slot.at[place], (pb, (place + step) % slots))
                for step in range(1, slots)
            ]
    for copy in by_few:
        copy.wait_recv()
    every = few_slot[0]
    for step in range(1, slots):
        every = every + few_slot[step]
    few_out[...] = every
    for copy in by_rows:
        copy.wait_recv()
    at_home.wait()
    freed = set()
    for n in range(len(units) - depth):
        freed.update(id(copy) for copy in over[n] + across[n] + along[n])
    for copy in sent:
        if id(copy) not in freed:
            copy.wait_send()


def scatter_outputs(grad_attn, grad_in_w, grad_out_w, grad_inputs, small):
    n_pb, slots = lax.axis_size("pb"), lax.axis_size("slot")
    if (n_pb, slots) != (8, 4):
        return (
            scatter_all(grad_attn),
            scatter_all(grad_in_w),
            scatter_all(grad_out_w),
            to_positions(leave_slots(grad_inputs)),
            sum_all(small, ("core", "x", "y", "slot")),
        )
    width = grad_attn.shape[1]
    mats = [
        mat.reshape(n_pb // 2, 2, slots, -1, width)
        for mat in (grad_attn, grad_in_w, grad_out_w)
    ]
    own, questions, steps, _ = grad_inputs.shape
    rows = grad_inputs.reshape(own, questions, slots, steps // slots, width)
    laid = jax.ShapeDtypeStruct((own, slots, questions, steps // slots, width), rows.dtype)
    units = sum(mat.shape[3] for mat in mats) // UNIT
    depth = 5
    copies = units * (1 + 3 + 2 + slots - 1) + (slots - 1) + 3 + slots - 1
    anywhere, inside = pl.BlockSpec(memory_space=pl.ANY), pl.BlockSpec(memory_space=pltpu.VMEM)
    half = UNIT // 2
    low, high = jnp.bfloat16, jnp.float32
    *shards, laid, small = pl.pallas_call(
        scatter_kernel,
        in_specs=[anywhere] * 4 + [inside],
        out_specs=[inside] * 3 + [anywhere, inside],
        out_shape=[jax.ShapeDtypeStruct(mat.shape[3:], high) for mat in mats]
        + [laid, jax.ShapeDtypeStruct(small.shape, high)],
        scratch_shapes=[
            pltpu.VMEM((units, 4, slots, UNIT, width), low),
            pltpu.VMEM((depth, 4, slots, UNIT, width), low),
            pltpu.VMEM((units, 2, slots, half, width), low),
            pltpu.VMEM((units, 2, slots, half, width), low),
            pltpu.VMEM((units, slots, half, width), low),
            pltpu.VMEM((units, slots, half, width), low),
            pltpu.VMEM((units, slots - 1, UNIT, width), low),
            pltpu.VMEM((3,) + small.shape, high),
            pltpu.VMEM((3,) + small.shape, high),
            pltpu.VMEM((slots,) + small.shape, high),
            pltpu.SemaphoreType.DMA((copies,)),
            pltpu.SemaphoreType.DMA((copies,)),
            pltpu.SemaphoreType.DMA((units + 1,)),
        ],
        compiler_params=pltpu.CompilerParams(
            collective_id=1, has_side_effects=True, vmem_limit_bytes=60 << 20
        ),
        name="scatter_outputs",
    )(*mats, rows, small)
    return (*shards, laid.reshape((-1,) + laid.shape[2:]), small)


def body(
    x_in,
    memory,
    doc_scores,
    valid_count,
    target_ids,
    target_len,
    mem_len,
    attn_w,
    ffn_in,
    ffn_out,
    ffn_bias,
    norms,
    embedding,
):
    x_here, mem_here, attn_full, in_full, out_full = gather_inputs(
        x_in, memory, attn_w, ffn_in, ffn_out
    )
    slots_here, questions, tgt_steps, model_width = x_here.shape
    mem_steps = mem_here.shape[2]
    seq_count = slots_here * questions
    head_dim = model_width // HEADS
    scaling = head_dim ** (-0.5)
    blocks = [
        attn_full[block_index * model_width : (block_index + 1) * model_width]
        for block_index in range(8)
    ]

    inputs = x_here.reshape(seq_count * tgt_steps, model_width)
    memory_rows = mem_here.reshape(seq_count * mem_steps, model_width)
    positions = jnp.arange(tgt_steps)
    place, slot_count = place_of("slot")
    core, cores = place_of("core")
    ring = (place - jnp.arange(slot_count)) % slot_count
    lengths_here = [mem_len] + [shifted(mem_len, "slot", step) for step in range(1, slot_count)]
    lengths_here = jnp.stack(lengths_here)[ring].reshape(slots_here, slot_count, questions)
    mem_lengths = pick(lengths_here, place, 1).reshape(seq_count)
    tgt_lengths = jnp.full_like(mem_lengths, tgt_steps)
    queries = (product(inputs, blocks[0]) * scaling).astype(jnp.bfloat16)
    key_rows = product(inputs, blocks[1]).astype(jnp.bfloat16)
    value_rows = product(inputs, blocks[2]).astype(jnp.bfloat16)
    self_out, self_lse = attend(True, tgt_lengths, queries, key_rows, value_rows)
    hidden_one, normed_one, root_one = norm_forward(
        inputs.astype(jnp.float32) + product(self_out, blocks[3]), norms[0], norms[1]
    )
    one_low = hidden_one.astype(jnp.bfloat16)
    cross_queries = (product(one_low, blocks[4]) * scaling).astype(jnp.bfloat16)
    cross_keys = product(memory_rows, blocks[5]).astype(jnp.bfloat16)
    cross_values = product(memory_rows, blocks[6]).astype(jnp.bfloat16)
    cross_out, cross_lse = attend(False, mem_lengths, cross_queries, cross_keys, cross_values)
    hidden_two, normed_two, root_two = norm_forward(
        hidden_one + product(cross_out, blocks[7]), norms[2], norms[3]
    )
    two_low = hidden_two.astype(jnp.bfloat16)
    pre_act = contract_cols(two_low, in_full) + ffn_bias
    act, slope = gelu_parts(pre_act)
    act_low, slope = act.astype(jnp.bfloat16), slope.astype(jnp.bfloat16)
    hidden_three, normed_three, root_three = norm_forward(
        hidden_two + product(act_low, out_full), norms[4], norms[5]
    )
    three_low = hidden_three.astype(jnp.bfloat16).reshape(
        slots_here, questions, tgt_steps, model_width
    )
    vocab_here = embedding.shape[0]
    share = vocab_here // cores
    pieces = slots_here * questions

    def both_cores(value):
        return jnp.stack([value, shifted(value, "core", 1)]) if cores > 1 else value[None]

    tokens = jnp.concatenate([target_ids, valid_count[:, None], target_len[:, None]], axis=1)
    tokens = both_cores(tokens)
    ids_all, valid_all, len_all = tokens[:, :, :tgt_steps], tokens[:, :, -2], tokens[:, :, -1]

    local = target_ids - place * vocab_here
    held = jnp.logical_and(local >= 0, local < vocab_here)
    target_rows = jnp.take(embedding, jnp.clip(local, 0, vocab_here - 1), axis=0)
    target_rows = jnp.where(held[..., None], target_rows, jnp.zeros_like(target_rows))
    target_rows = after(target_rows, x_here)
    found = [shifted(target_rows, "slot", step) for step in range(1, slot_count)]
    target_rows = sum([f.astype(jnp.float32) for f in found], target_rows.astype(jnp.float32))

    slot_ids = jnp.arange(slot_count)[:, None] + slot_count * jnp.arange(slots_here)[None]
    live_piece = slot_ids[:, None, :, None] < valid_all[None, :, None, :]
    long_piece = (len_all + 15) // 16 * 16
    long_piece = jnp.where(live_piece, long_piece[None, :, None, :], 0).reshape(slot_count, -1)
    ends = jnp.cumsum(long_piece, axis=1)
    packing = jnp.concatenate([ends - long_piece, ends[:, -1:]], axis=1)[ring]
    info = jnp.concatenate([core[None], packing.reshape(-1)]).astype(jnp.int32)
    piece_ids = (ids_all - (place * vocab_here + core * share)).astype(jnp.float32)
    piece_ids = jnp.broadcast_to(
        piece_ids[None, :, None], (slot_count, cores, slots_here, questions, tgt_steps)
    ).reshape(-1, 1, tgt_steps)
    ids_rows = jnp.broadcast_to(piece_ids, (piece_ids.shape[0], 8, tgt_steps))

    group = pieces * tgt_steps
    moving = three_low.reshape(group, model_width)
    arriving = [moving] + [shifted(moving, "slot", step) for step in range(1, slot_count)]
    kept, log_list, homes = (), [], []
    for step in range(slot_count):
        moving = arriving[step] if not step else after(arriving[step], own_logs)
        other = shifted(moving, "core", 1)
        earlier = (own_logs,) if step else ()
        *kept, own_sums, mate_sums, own_logs, mate_logs = rows_pass(
            step, slot_count, info, ids_rows, moving, other, embedding, cores, kept, earlier
        )
        log_list += [own_logs[:, 0], mate_logs[:, 0]]
        homes.append(
            join_pass(
                own_sums, shifted(mate_sums, "core", 1), own_logs, shifted(mate_logs, "core", 1)
            )
        )

    def by_slot(value):
        parts = [value] + [shifted(value, "slot", step) for step in range(1, slot_count)]
        return jnp.stack(parts)[ring]

    target_logit = jnp.sum(three_low.astype(jnp.float32) * target_rows[None], axis=-1)
    told = jnp.concatenate(log_list + [target_logit.reshape(-1, tgt_steps)], axis=0)
    told = both_cores(by_slot(told))
    hit_all = told[:, :, -pieces:].reshape(cores, slot_count, slots_here, questions, tgt_steps)
    hit_all = hit_all.transpose(2, 1, 0, 3, 4).reshape(-1, cores, questions, tgt_steps)
    logs = told[:, :, :-pieces].reshape(
        cores, slot_count, slot_count, cores, slots_here, questions, tgt_steps
    )
    logs = jnp.stack([logs[0], logs[1][:, :, ::-1]]) if cores > 1 else logs
    logs = jax.nn.logsumexp(logs, axis=0)
    turns = (jnp.arange(slot_count)[:, None] - jnp.arange(slot_count)[None]) % slot_count
    logs = jnp.take_along_axis(
        logs, turns.reshape((slot_count, slot_count) + (1,) * (logs.ndim - 2)), axis=1
    )
    rest_all = jax.nn.logsumexp(logs, axis=0)
    rest_all = rest_all.transpose(2, 0, 1, 3, 4).reshape(hit_all.shape)
    log_norm = jnp.logaddexp(rest_all, hit_all)
    live = positions < len_all[..., None]
    lengths = len_all.astype(jnp.float32)
    per_slot = jnp.sum(jnp.where(live[None], hit_all - log_norm, 0.0), axis=3) / lengths[None]
    valid = jnp.arange(per_slot.shape[0])[:, None, None] < valid_all[None]
    scores_t = both_cores(doc_scores).transpose(2, 0, 1)
    joint = jnp.where(valid, scores_t + per_slot, mask_fill)
    prior = jnp.where(valid, scores_t, mask_fill)
    joint_total = jax.nn.logsumexp(joint, axis=0)
    neg_marginal = jax.nn.logsumexp(prior, axis=0) - joint_total
    log_post = joint - joint_total
    posterior = jnp.exp(log_post)
    entropy_q = -jnp.sum(posterior * log_post, axis=0)
    objective_part = jnp.sum((lengths * (neg_marginal + entropy_weight * entropy_q))[0])
    slot_weight = -posterior * (1.0 + entropy_weight * (log_post + entropy_q[None]))
    token_weight = jnp.where(live[None], slot_weight[..., None], 0.0)
    hit_weight = token_weight * jax.nn.sigmoid(rest_all - hit_all)

    def own_slots(value):
        value = value[:, 0].reshape(slots_here, slot_count, questions, tgt_steps)
        return pick(value, place, 1)

    def ring_rows(value):
        value = value.reshape(slots_here, slot_count, cores, questions, tgt_steps)
        return value.transpose(1, 2, 0, 3, 4)[ring].reshape(-1, tgt_steps)

    facts = [ring_rows(value) for value in (token_weight, log_norm, hit_weight)]
    facts = jnp.stack(facts + [ids_rows[:, 0]] + [jnp.zeros_like(facts[0])] * 4, axis=1)
    expos, packed, tops = kept
    tiles = expos.shape[1]
    cut = tiles // 2 + 1
    n_pb = lax.axis_size("pb")
    tall, wide, _ = grid_of(n_pb)
    sends = tuple(homes[1:])
    homes[1:] = [
        shifted(homes[step], "slot", slot_count - step) for step in range(1, slot_count)
    ]
    table_grads = []
    for first, count in ((0, cut), (cut, tiles - cut)):
        sides = [
            side.reshape((tall, wide, cores) + side.shape[1:])
            for side in table_pass(
                info, facts, tops, packed, expos, first, count, n_pb, sends
            )
        ]
        sends = (ring_first(sides[0], "x", 1), ring_first(sides[1], "y", 0))
        table_grads.append(sides)

    def over_first(sides, late):
        return (
            ring_scatter(sides[0], "x", 1, late).astype(jnp.bfloat16),
            ring_scatter(sides[1], "y", 0, late).astype(jnp.bfloat16),
        )

    def over_second(sides, late):
        return (
            ring_scatter(sides[0], "y", 0, late).astype(jnp.bfloat16),
            ring_scatter(sides[1], "x", 0, late).astype(jnp.bfloat16),
        )

    def second_sends(sides):
        return ring_first(sides[0], "y", 0), ring_first(sides[1], "x", 0)

    home_logs = pick(logs, place, 1)[:, 0][(place + jnp.arange(slot_count)) % slot_count]
    home_logs = home_logs.reshape(slot_count, pieces, tgt_steps).transpose(1, 0, 2)
    home_logs = jnp.pad(
        home_logs, ((0, 0), (0, 8 - slot_count), (0, 0)), constant_values=mask_fill
    )
    own_weight = own_slots(hit_weight).reshape(pieces, 1, tgt_steps)
    own_weight = jnp.broadcast_to(own_weight, (pieces, 8, tgt_steps))
    grad_three = home_pass(home_logs, own_weight, target_rows, homes, sends)
    back_blocks, in_back, out_back = blocks, in_full, out_full
    grad_res_three, gain_three, shift_three = norm_backward(
        grad_three, normed_three, root_three, norms[4]
    )
    grad_ffn = grad_res_three.astype(jnp.bfloat16)
    grad_out_w = contract_rows(act_low, grad_ffn)
    grad_act = contract_cols(grad_ffn, out_back)
    grad_pre = (grad_act * slope.astype(jnp.float32)).astype(jnp.bfloat16)
    grad_in_w = contract_rows(grad_pre, two_low)
    grad_bias = jnp.sum(lax.optimization_barrier(grad_pre).astype(jnp.float32), axis=0)
    grad_two = grad_res_three + product(grad_pre, in_back)
    grad_res_two, gain_two, shift_two = norm_backward(grad_two, normed_two, root_two, norms[2])
    grad_cross = grad_res_two.astype(jnp.bfloat16)
    grad_w7 = contract_rows(cross_out, grad_cross)
    grad_cross_out = contract_cols(grad_cross, back_blocks[7]).astype(jnp.bfloat16)
    cq_grad, ck_grad, cv_grad = attend(
        False, mem_lengths, cross_queries, cross_keys, cross_values, cross_lse, grad_cross_out
    )
    grad_w4 = contract_rows(one_low, cq_grad) * scaling
    grad_w5 = contract_rows(memory_rows, ck_grad)
    grad_w6 = contract_rows(memory_rows, cv_grad)
    grad_memory = (
        contract_cols(ck_grad, back_blocks[5]) + contract_cols(cv_grad, back_blocks[6])
    ).astype(jnp.bfloat16)
    grad_memory = leave_slots(
        grad_memory.reshape(slots_here, questions, mem_steps, model_width)
    )
    table_sum = [over_first(sides, cq_grad) for sides in table_grads]
    earlier = grad_memory[1:] + [*second_sends(table_sum[0]), *second_sends(table_sum[1])]
    grad_one = grad_res_two + contract_cols(cq_grad, back_blocks[4]) * scaling
    grad_res_one, gain_one, shift_one = norm_backward(grad_one, normed_one, root_one, norms[0])
    grad_attn_out = grad_res_one.astype(jnp.bfloat16)
    grad_w3 = contract_rows(self_out, grad_attn_out)
    grad_self_out = contract_cols(grad_attn_out, back_blocks[3]).astype(jnp.bfloat16)
    sq_grad, sk_grad, sv_grad = attend(
        True, tgt_lengths, queries, key_rows, value_rows, self_lse, grad_self_out, earlier
    )
    grad_w0 = contract_rows(inputs, sq_grad) * scaling
    grad_w1 = contract_rows(inputs, sk_grad)
    grad_w2 = contract_rows(inputs, sv_grad)
    grad_inputs = (
        grad_res_one
        + contract_cols(sq_grad, back_blocks[0]) * scaling
        + contract_cols(sk_grad, back_blocks[1])
        + contract_cols(sv_grad, back_blocks[2])
    )
    grad_inputs = grad_inputs.astype(jnp.bfloat16).reshape(
        slots_here, questions, tgt_steps, model_width
    )
    grad_attn = jnp.concatenate(
        [
            grad.astype(jnp.bfloat16)
            for grad in (grad_w0, grad_w1, grad_w2, grad_w3, grad_w4, grad_w5, grad_w6, grad_w7)
        ],
        axis=0,
    )
    small = jnp.concatenate(
        [
            jnp.stack([gain_one, shift_one, gain_two, shift_two, gain_three, shift_three], axis=0),
            grad_bias.reshape(-1, model_width),
            jnp.zeros((6, model_width), jnp.float32)
            .at[0, :3]
            .set(jnp.stack([objective_part, jnp.sum(lengths[0]), jnp.sum(entropy_q[0])])),
        ],
        axis=0,
    )
    table_sum = [over_second(sides, grad_inputs) for sides in table_sum]
    table_sum = [jnp.stack(sides, axis=2) for sides in table_sum]
    table_sum = jnp.concatenate(table_sum, axis=1).reshape(cores, share, -1)
    table_send = pick(table_sum, 1 - core, 0)
    grad_attn, grad_in_w, grad_out_w, grad_inputs, small = scatter_outputs(
        grad_attn,
        grad_in_w.astype(jnp.bfloat16),
        grad_out_w.astype(jnp.bfloat16),
        grad_inputs,
        after(small, table_send),
    )
    grad_memory = to_positions(grad_memory, small)
    kept = pick(table_sum, core, 0)
    given = after(shifted(table_send, "core", 1), small)
    grad_embed = jnp.stack([kept, given])
    grad_embed = jnp.where(core == 0, grad_embed, grad_embed[::-1])
    grad_embed = grad_embed.reshape(vocab_here, -1).astype(jnp.float32)
    grad_norms = small[:6]
    scalars = small[-6]
    loss = scalars[0] / scalars[1]
    entropy = scalars[2] / (questions * n_pb * slot_count)
    grad_bias = small[6:-6].reshape(-1)
    own_bias = grad_bias.shape[0] // (lax.axis_size("pb") * slot_count)
    grad_bias = lax.dynamic_slice_in_dim(
        grad_bias,
        (lax.axis_index("pb") * slot_count + lax.axis_index("slot")) * own_bias,
        own_bias,
    )
    return (
        loss,
        entropy,
        grad_inputs,
        grad_memory,
        grad_attn,
        grad_in_w,
        grad_out_w,
        grad_bias,
        grad_norms,
        grad_embed,
    )


def solution(mesh):
    placed = (
        P(None, "pb", "slot", None),
        P(None, "pb", "slot", None),
        P("pb", None),
        P("pb"),
        P("pb", None),
        P("pb"),
        P("slot", "pb"),
        P(("pb", "slot"), None),
        P(("pb", "slot"), None),
        P(("pb", "slot"), None),
        P(),
        P(),
        P("slot", None),
    )
    return jax.shard_map(
        body,
        mesh=mesh,
        in_specs=placed,
        out_specs=(
            P(),
            P(),
            P(None, "pb", "slot", None),
            P(None, "pb", "slot", None),
            P(("pb", "slot"), None),
            P(("pb", "slot"), None),
            P(("pb", "slot"), None),
            P(("pb", "slot")),
            P(),
            P("slot", "pb"),
        ),
        check_vma=False,
    )
```

time: 1370 us -> 977 us (0.71)
  waiting for transfers between devices: 243 us -> 26.6 us
  Pallas kernels: 430 us -> 621 us
  local copies, waits for them, and re-layouts: 210 us -> 86.6 us
  starting transfers between devices: 150 us -> 36 us
  matrix products: 188 us -> 125 us
  other arithmetic: 109 us -> 49.3 us
    pallas_call x6 -> x16, Pallas kernels: 232 us -> 456 us  [the longest x1 165 us: scatter_outputs(): pl.pallas_call(scatter_kernel, in_specs=[anywhere] * 4 + [inside], out_sp...]
    ppermute x43 -> x24, waiting for transfers between devices: 131 us -> 2.89 us  [shifted(): return lax.ppermute(value, 'pb', pairs)]
    ppermute x33 -> x18, waiting for transfers between devices: 111 us -> 23.7 us  [shifted(): lax.ppermute(value, 'slot', [(i, (i + step) % size) for i in range(size)])]
    ppermute x33 -> x18, starting transfers between devices: 99.1 us -> 25.7 us  [shifted(): lax.ppermute(value, 'slot', [(i, (i + step) % size) for i in range(size)])]
    reshape x20 -> x2, local copies, waits for them, and re-layouts: 65.2 us -> 0.17 us  [the longest x1 0.08 us: body(): info = jnp.concatenate([core[None], packing.reshape(-1)]).astype(jnp.int32)]
    dot_general x12 -> x0, matrix products: 45.7 us -> none  [the longest x2 12.3 us: attend_backward(): jnp.einsum('nhqk,nqhe->nkhe', attn_probs.astype(jnp.bfloat16), grad_out,...]
    convert_element_type x28 -> x5, other arithmetic: 48.7 us -> 8.17 us  [the longest x2 4.14 us: over_first(): ring_scatter(sides[1], 'y', 0, late).astype(jnp.bfloat16)]
    ppermute x43 -> x24, starting transfers between devices: 50.6 us -> 10.3 us  [shifted(): return lax.ppermute(value, 'pb', pairs)]
  transfers between devices with their start and end apart: 76 -> 42, of which waited for: 26 -> 6; matrix products, arithmetic and copies ran while one was open for 26% -> 24% of each run, Pallas kernels for 32% -> 65%
where the time goes in v3:
time: 977 us; the launch traced here: 962 us
  Pallas kernels  621 us (64%)
  matrix products  125 us (13%)
  local copies, waits for them, and re-layouts  86.6 us (9%)
  other arithmetic  49.3 us (5%)
  starting transfers between devices  36 us (4%)
  waiting for transfers between devices  26.6 us (3%)
  between operations  17.8 us (2%)
    pallas_call x1, Pallas kernels, scatter_outputs(): pl.pallas_call(scatter_kernel, in_specs=[anywhere] * 4 + [inside], out_sp...  165 us
    pallas_call x1, Pallas kernels, gather_inputs(): pl.pallas_call(gather_kernel, in_specs=[anywhere] * 5, out_specs=[anywher...  165 us
    pallas_call x4, Pallas kernels, rows_pass(): pl.pallas_call(functools.partial(rows_kernel, step), grid_spec=pltpu.Pref...  129 us
    pallas_call x2, Pallas kernels, table_pass(): pl.pallas_call(functools.partial(table_kernel, first), grid_spec=pltpu.Pr...  92 us
    dot_general x10, matrix products, contract_cols(): lax.dot_general(left, right, (((1,), (1,)), ((), ())), preferred_element_...  55.3 us
    pallas_call x4, Pallas kernels, attend(): pl.pallas_call(functools.partial(kernel, causal), grid_spec=pltpu.Prefetc...  53.2 us
    dot_general x10, matrix products, product(): return jnp.dot(left, right, preferred_element_type=jnp.float32)  35.2 us
    dot_general x10, matrix products, contract_rows(): lax.dot_general(left, right, (((0,), (0,)), ((), ())), preferred_element_...  34 us
  transfers between devices with their start and end apart: 42, of which 6 were waited for; matrix products, arithmetic and copies ran while one was open for 24% of the time, Pallas kernels for 65%

profile of v3, /device:TPU:0, one launch (start us, length us, event | category | flops | bytes accessed | tf_op | source)
XLA Modules:
  0.0 961.9 jit_solution(15687214710624741143)
XLA Ops:
  9.0 164.6 %gather_inputs.1 = (bf16[8,4,256,1024]{3,2,1,0:T(8,128)(2,1)}, bf16[8,4,128,1024]{3,2,1,0:T(8,128)(2,1)}, bf16[8,4,128,1024]{3,2,1,0:T(8,128)(2,1)}, bf16[2,2,4,...) custom-call(bf16[256,1024]{1,0:T(8,128)(2,1)} %refs_0_.1, bf16[128,1024]{1,0:T(8,128)(2,1)} %refs_1_.1, ...), custom_call_target="tpu_custom_call" | custom-call | tf_op jit(solution)/shard_map/gather_inputs/pallas_call | solution.py:804
  176.1 13.2 %gather_fusion.2 = bf16[256,1024]{1,0:T(8,128)(2,1)S(1)} fusion(bf16[12544,1024]{1,0:T(8,128)(2,1)} %table.7, s32[1024]{0:T(1024)S(1)} %pad_clamp_fusion.1), kind=kCustom, calls=%fused_computation.2 | custom fusion | bytes 1049600 | tf_op jit(solution)/shard_map/jit(_take)/gather | solution.py:1130
  191.9 10.1 %fusion.66 = (bf16[1,4,256,1024]{3,2,1,0:T(8,128)(2,1)}, bf16[1,4,256,1024]{3,2,1,0:T(8,128)(2,1)}, bf16[1,4,256,1024]{3,2,1,0:T(8,128)(2,1)}, bf16[1,4,256,1024...) fusion(bf16[8,4,256,1024]{3,2,1,0:T(8,128)(2,1)} %get-tuple-ele, ...), kind=kLoop, calls=%fused_computation.264 | loop fusion | bytes 33554432 | tf_op jit(solution)/shard_map/slice | solution.py:1078
  215.1 7.8 convolution_convert_fusion.2.values
  237.2 15.7 %cross_attend.1 = (bf16[512,1024]{1,0:T(8,128)(2,1)S(1)}, f32[512,128]{1,0:T(8,128)S(1)}) custom-call(s32[4]{0:T(128)S(1)} %reshape.553.info, bf16[512,1024]{1,0:T(8,128)(2,1)S(1)} %multiply_convert_fusion.4.queries, bf16[1536,1024]{1,0:T(8,128)(2,1)S(1)} %copy-done.9, bf16[1536,1024]{1,0:T(8,128)(2,1)} %convolution_convert_fusion.2.values), custom_call_target="tpu_custom_call" | custom-call | flops 3221225472 | bytes 12582912 | tf_op jit(solution)/shard_map/cross_attend/pallas_call | solution.py:317
  255.6 15.1 %multiply_convert_fusion.1 = (bf16[512,4096]{1,0:T(8,128)(2,1)S(1)}, f32[512,4096]{1,0:T(8,128)}) fusion(f32[4096]{0:T(1024)S(1)} %copy-done.109, bf16[4096,1024]{1,0:T(8,128)(2,1)} %bitcast.422, f32[512,1024]{1,0:T(8,128)S(1)} %get-tuple-element.186, f32[1024]{0:T(1024)S(1)} %bitcast.407, f32[1024]{0:T(1024)S(1)} %bitcast.392, ...), kind=kOutput, calls=%fused_computation.15 | convolution fusion | flops 4345823232 | bytes 23097344 | tf_op jit(solution)/shard_map/dot_general | solution.py:203
  283.3 34.2 %rows_pass_0.1 = (bf16[4,7,1024,896]{3,2,1,0:T(8,128)(2,1)}, bf16[4,1152,1024]{2,1,0:T(8,128)(2,1)}, f32[4,1152,128]{2,1,0:T(8,128)}, bf16[512,1024]{1,0:T(8,128...) custom-call(s32[37]{0:T(128)} %pad_add_fusion.4.info, ...), custom_call_target="tpu_custom_call" | custom-call | flops 26306674688 | bytes 25690112 | tf_op jit(solution)/shard_map/rows_pass_0/pallas_call | solution.py:461
  324.0 26.4 %rows_pass_1.1 = (bf16[4,7,1024,896]{3,2,1,0:T(8,128)(2,1)}, bf16[4,1152,1024]{2,1,0:T(8,128)(2,1)}, f32[4,1152,128]{2,1,0:T(8,128)}, bf16[512,1024]{1,0:T(8,128...) custom-call(s32[37]{0:T(128)} %pad_add_fusion.4.info, ...), custom_call_target="tpu_custom_call", output_to_operand_aliasing={{0}: (5, {}), {1}: (6, {}), {2}: (7, {})} | custom-call | flops 26306674688 | bytes 25690112 | tf_op jit(solution)/shard_map/rows_pass_1/pallas_call | solution.py:461
  352.9 16.6 %collective-permute-done.7 = bf16[512,1024]{1,0:T(8,128)(2,1)S(1)} collective-permute-done((bf16[512,1024]{1,0:T(8,128)(2,1)}, bf16[512,1024]{1,0:T(8,128)(2,1)S(1)}, u32[]{:S(2)}, u32[]{:S(2)}) %collective-permute-start.7) | collective-permute-done | bytes 1048608 | tf_op jit(solution)/shard_map/ppermute | solution.py:30
  373.6 34.2 %rows_pass_2.1 = (bf16[4,7,1024,896]{3,2,1,0:T(8,128)(2,1)}, bf16[4,1152,1024]{2,1,0:T(8,128)(2,1)}, f32[4,1152,128]{2,1,0:T(8,128)}, bf16[512,1024]{1,0:T(8,128...) custom-call(s32[37]{0:T(128)} %pad_add_fusion.4.info, ...), custom_call_target="tpu_custom_call", output_to_operand_aliasing={{0}: (5, {}), {1}: (6, {}), {2}: (7, {})} | custom-call | flops 26306674688 | bytes 25690112 | tf_op jit(solution)/shard_map/rows_pass_2/pallas_call | solution.py:461
  416.4 34.6 %rows_pass_3.1 = (bf16[4,7,1024,896]{3,2,1,0:T(8,128)(2,1)}, bf16[4,1152,1024]{2,1,0:T(8,128)(2,1)}, f32[4,1152,128]{2,1,0:T(8,128)}, bf16[512,1024]{1,0:T(8,128...) custom-call(s32[37]{0:T(128)} %pad_add_fusion.4.info, ...), custom_call_target="tpu_custom_call", output_to_operand_aliasing={{0}: (5, {}), {1}: (6, {}), {2}: (7, {})} | custom-call | flops 26306674688 | bytes 25690112 | tf_op jit(solution)/shard_map/rows_pass_3/pallas_call | solution.py:461
  489.2 50.7 %table_pass_0.1 = (bf16[8,4,448,128]{3,2,1,0:T(8,128)(2,1)}, bf16[8,4,448,128]{3,2,1,0:T(8,128)(2,1)}) custom-call(s32[37]{0:T(128)} %pad_add_fusion.4.info, f32[32,8,128]{2,1,0:T(8,128)} %stack.146.facts, f32[4,1152,128]{2,1,0:T(8,128)} %get-tuple-element.107.tops, bf16[4,1152,1024]{2,1,0:T(8,128)(2,1)} %get-tuple-element.108.rows, ...), custom_call_target="tpu_custom_call" | custom-call | flops 30064771072 | bytes 58720256 | tf_op jit(solution)/shard_map/table_pass_0/pallas_call | solution.py:633
  544.2 41.3 %table_pass_4.1 = (bf16[8,3,448,128]{3,2,1,0:T(8,128)(2,1)}, bf16[8,3,448,128]{3,2,1,0:T(8,128)(2,1)}) custom-call(s32[37]{0:T(128)} %pad_add_fusion.4.info, f32[32,8,128]{2,1,0:T(8,128)} %stack.146.facts, f32[4,1152,128]{2,1,0:T(8,128)} %get-tuple-element.107.tops, bf16[4,1152,1024]{2,1,0:T(8,128)(2,1)} %get-tuple-element.108.rows, ...), custom_call_target="tpu_custom_call" | custom-call | flops 22548578304 | bytes 44040192 | tf_op jit(solution)/shard_map/table_pass_4/pallas_call | solution.py:633
  602.0 15.0 %multiply_convert_fusion = bf16[512,4096]{1,0:T(8,128)(2,1)S(1)} fusion(bf16[4096,1024]{1,0:T(8,128)(2,1)} %bitcast.424, f32[512,4096]{1,0:T(8,128)} %get-tuple-element.188, f32[4096]{0:T(1024)S(1)} %copy-done.110, f32[512,1024]{1,0:T(8,128)S(1)} %subtract_multiply_fusion.2), kind=kOutput, calls=%fused_computation.13 | convolution fusion | flops 4354211840 | bytes 23085056 | tf_op jit(solution)/shard_map/dot_general | solution.py:203
  617.1 7.7 multiply_reduce_fusion.1
  624.8 7.3 convolution_convert_fusion.1
  632.1 7.2 convolution_convert_fusion
  642.3 18.6 %cross_attend_back.1 = (bf16[512,1024]{1,0:T(8,128)(2,1)S(1)}, bf16[1536,1024]{1,0:T(8,128)(2,1)}, bf16[1536,1024]{1,0:T(8,128)(2,1)}) custom-call(s32[4]{0:T(128)S(1)} %reshape.553.info, bf16[512,1024]{1,0:T(8,128)(2,1)S(1)} %multiply_convert_fusion.4.queries, bf16[1536,1024]{1,0:T(8,128)(2,1)} %convolution_convert_fusion.3.keys, ...), custom_call_target="tpu_custom_call" | custom-call | flops 8053063680 | bytes 12582912 | tf_op jit(solution)/shard_map/cross_attend_back/pallas_call | solution.py:317
  660.9 5.9 fusion.73
  701.7 13.7 %self_attend_back.1 = (bf16[512,1024]{1,0:T(8,128)(2,1)}, bf16[512,1024]{1,0:T(8,128)(2,1)}, bf16[512,1024]{1,0:T(8,128)(2,1)}) custom-call(s32[4]{0:T(128)S(1)} %copy-done.4, bf16[512,1024]{1,0:T(8,128)(2,1)} %copy-done.2, bf16[512,1024]{1,0:T(8,128)(2,1)} %copy-done.1, bf16[512,1024]{1,0:T(8,128)(2,1)} %copy-done, f32[512,128]{1,0:T(8,128)S(1)} %get-tuple-element.76.logs, ...), custom_call_target="tpu_custom_call" | custom-call | flops 2684354560 | bytes 4194304 | tf_op jit(solution)/shard_map/self_attend_back/pallas_call | solution.py:317
  727.2 5.6 convert_dynamic-update-slice_fusion.2
  732.8 5.9 convert_dynamic-update-slice_fusion.1
  759.1 5.8 copy-done.15
  768.0 165.1 %scatter_outputs.1 = (f32[256,1024]{1,0:T(8,128)}, f32[128,1024]{1,0:T(8,128)}, f32[128,1024]{1,0:T(8,128)}, bf16[2,4,2,32,1024]{4,3,2,1,0:T(8,128)(2,1)}, f32[16,1024]{1,0:T(8,128)}) custom-call(bf16[4,2,4,256,1024]{4,3,2,1,0:T(8,128)(2,1)} %bitcast.319, bf16[4,2,4,128,1024]{4,3,2,1,0:T(8,128)(2,1)} %bitcast.323, bf16[4,2,4,128,1024]{4,3,2,1,0:T(8,128)(2,1)} %bitcast.324, ...), custom_call_target="tpu_custom_call" | custom-call | tf_op jit(solution)/shard_map/scatter_outputs/pallas_call | solution.py:1025
  (526 shorter events, 221.7 us)
Async XLA Ops:
  0.6 231.0 %collective-permute-start = (s32[2,2]{1,0:T(2,128)}, s32[2,2]{1,0:T(2,128)S(1)}, u32[]{:S(2)}, u32[]{:S(2)}) collective-permute-start(s32[2,2]{1,0:T(2,128)} %param.21), channel_id=1, source_target_pairs={{0,1},{1,2},{2,3},{3,0},{4,5},{5,6},{6,7},{7,4},{8,9},{9,10},{10,1... | collective-permute-start | bytes 56 | tf_op jit(solution)/shard_map/ppermute | solution.py:30
  3.7 230.9 %collective-permute-start.1 = (s32[2,2]{1,0:T(2,128)}, s32[2,2]{1,0:T(2,128)S(1)}, u32[]{:S(2)}, u32[]{:S(2)}) collective-permute-start(s32[2,2]{1,0:T(2,128)} %param.21), channel_id=1, source_target_pairs={{0,2},{1,3},{2,0},{3,1},{4,6},{5,7},{6,4},{7,5},{8,10},{9,11},{10,... | collective-permute-start | bytes 56 | tf_op jit(solution)/shard_map/ppermute | solution.py:30
  6.3 228.3 %collective-permute-start.2 = (s32[2,2]{1,0:T(2,128)}, s32[2,2]{1,0:T(2,128)S(1)}, u32[]{:S(2)}, u32[]{:S(2)}) collective-permute-start(s32[2,2]{1,0:T(2,128)} %param.21), channel_id=1, source_target_pairs={{0,3},{1,0},{2,1},{3,2},{4,7},{5,4},{6,5},{7,6},{8,11},{9,8},{10,9... | collective-permute-start | bytes 56 | tf_op jit(solution)/shard_map/ppermute | solution.py:30
  190.2 85.7 %collective-permute-start.11 = (bf16[2,128,1024]{2,1,0:T(8,128)(2,1)}, bf16[2,128,1024]{2,1,0:T(8,128)(2,1)S(1)}, u32[]{:S(2)}, u32[]{:S(2)}) collective-permute-start(bf16[2,128,1024]{2,1,0:T(8,128)(2,1)} %select_select_fusion), channel_id=1, source_target_pairs={{0,1},{1,2},{2,3},{3,0},{4,5},{5,6},{6,7},{7,4},{8,9},{9,10},{10,1... | collective-permute-start | bytes 1572872 | tf_op jit(solution)/shard_map/ppermute | solution.py:30
  190.4 85.6 %collective-permute-start.12 = (bf16[2,128,1024]{2,1,0:T(8,128)(2,1)}, bf16[2,128,1024]{2,1,0:T(8,128)(2,1)S(1)}, u32[]{:S(2)}, u32[]{:S(2)}) collective-permute-start(bf16[2,128,1024]{2,1,0:T(8,128)(2,1)} %select_select_fusion), channel_id=1, source_target_pairs={{0,2},{1,3},{2,0},{3,1},{4,6},{5,7},{6,4},{7,5},{8,10},{9,11},{10,... | collective-permute-start | bytes 1572872 | tf_op jit(solution)/shard_map/ppermute | solution.py:30
  370.6 82.0 %collective-permute-start.18 = (f32[2,8]{1,0:T(2,128)S(1)}, f32[2,8]{1,0:T(2,128)S(1)}, u32[]{:S(2)}, u32[]{:S(2)}) collective-permute-start(f32[2,8]{1,0:T(2,128)S(1)} %copy-done.98), channel_id=1, source_target_pairs={{0,4},{4,0},{8,12},{12,8},{16,20},{20,16},{24,28},{28,24},{1,5},{5... | collective-permute-start | bytes 200 | tf_op jit(solution)/shard_map/ppermute | solution.py:43
  373.0 90.2 %collective-permute-start.19 = (bf16[512,1024]{1,0:T(8,128)(2,1)}, bf16[512,1024]{1,0:T(8,128)(2,1)S(1)}, u32[]{:S(2)}, u32[]{:S(2)}) collective-permute-start(bf16[512,1024]{1,0:T(8,128)(2,1)} %get-tuple-element.100), channel_id=1, source_target_pairs={{0,4},{4,0},{8,12},{12,8},{16,20},{20,16},{24,28},{28,24},{1,5},{5... | collective-permute-start | bytes 3145736 | tf_op jit(solution)/shard_map/ppermute | solution.py:43
  412.9 54.1 %collective-permute-start.21 = (bf16[512,1024]{1,0:T(8,128)(2,1)}, bf16[512,1024]{1,0:T(8,128)(2,1)}, u32[]{:S(2)}, u32[]{:S(2)}) collective-permute-start(bf16[512,1024]{1,0:T(8,128)(2,1)} %get-tuple-element.102), channel_id=1, source_target_pairs={{0,4},{4,0},{8,12},{12,8},{16,20},{20,16},{24,28},{28,24},{1,5},{5... | collective-permute-start | bytes 3145736 | tf_op jit(solution)/shard_map/ppermute | solution.py:43
  413.3 59.3 %collective-permute-start.24 = (bf16[512,1024]{1,0:T(8,128)(2,1)}, bf16[512,1024]{1,0:T(8,128)(2,1)}, u32[]{:S(2)}, u32[]{:S(2)}) collective-permute-start(bf16[512,1024]{1,0:T(8,128)(2,1)} %get-tuple-element.104), channel_id=1, source_target_pairs={{0,4},{4,0},{8,12},{12,8},{16,20},{20,16},{24,28},{28,24},{1,5},{5... | collective-permute-start | bytes 3145736 | tf_op jit(solution)/shard_map/ppermute | solution.py:43
  470.3 120.5 %collective-permute-start.23 = (bf16[512,1024]{1,0:T(8,128)(2,1)}, bf16[512,1024]{1,0:T(8,128)(2,1)S(1)}, u32[]{:S(2)}, u32[]{:S(2)}) collective-permute-start(bf16[512,1024]{1,0:T(8,128)(2,1)} %join_pass.5.refs_0_), channel_id=1, source_target_pairs={{0,3},{1,0},{2,1},{3,2},{4,7},{5,4},{6,5},{7,6},{8,11},{9,8},{10,9... | collective-permute-start | bytes 3145736 | tf_op jit(solution)/shard_map/ppermute | solution.py:30
  475.5 115.3 %collective-permute-start.26 = (bf16[512,1024]{1,0:T(8,128)(2,1)}, bf16[512,1024]{1,0:T(8,128)(2,1)}, u32[]{:S(2)}, u32[]{:S(2)}) collective-permute-start(bf16[512,1024]{1,0:T(8,128)(2,1)} %join_pass.6.refs_1_), channel_id=1, source_target_pairs={{0,2},{1,3},{2,0},{3,1},{4,6},{5,7},{6,4},{7,5},{8,10},{9,11},{10,... | collective-permute-start | bytes 3145736 | tf_op jit(solution)/shard_map/ppermute | solution.py:30
  488.3 103.2 %collective-permute-start.29 = (bf16[512,1024]{1,0:T(8,128)(2,1)}, bf16[512,1024]{1,0:T(8,128)(2,1)}, u32[]{:S(2)}, u32[]{:S(2)}) collective-permute-start(bf16[512,1024]{1,0:T(8,128)(2,1)} %join_pass.7.refs_2_), channel_id=1, source_target_pairs={{0,1},{1,2},{2,3},{3,0},{4,5},{5,6},{6,7},{7,4},{8,9},{9,10},{10,1... | collective-permute-start | bytes 3145736 | tf_op jit(solution)/shard_map/ppermute | solution.py:30
  542.9 153.0 %collective-permute-start.31 = (bf16[2,2,4,448,128]{4,3,2,1,0:T(8,128)(2,1)}, bf16[2,2,4,448,128]{4,3,2,1,0:T(8,128)(2,1)}, u32[]{:S(2)}, u32[]{:S(2)}) collective-permute-start(bf16[2,2,4,448,128]{4,3,2,1,0:T(8,128)(2,1)} %dynamic-slice_bitcast_fusion.refs_1_), channel_id=1, source_target_pairs={{0,16},{4,20},{8,24},{12,28},{16,0},{20,4},{24,8},{28,12},{1,17},{... | collective-permute-start | bytes 5505032 | tf_op jit(solution)/shard_map/ppermute | solution.py:43
  585.5 112.7 %collective-permute-start.30 = (bf16[2,2,4,448,128]{4,3,2,1,0:T(8,128)(2,1)}, bf16[2,2,4,448,128]{4,3,2,1,0:T(8,128)(2,1)}, u32[]{:S(2)}, u32[]{:S(2)}) collective-permute-start(bf16[2,2,4,448,128]{4,3,2,1,0:T(8,128)(2,1)} %dynamic-slice_bitcast_fusion.1.refs_0_), channel_id=1, source_target_pairs={{0,8},{4,12},{8,0},{12,4},{16,24},{20,28},{24,16},{28,20},{1,9},{5... | collective-permute-start | bytes 5505032 | tf_op jit(solution)/shard_map/ppermute | solution.py:43
  590.8 101.7 %collective-permute-start.33 = (bf16[2,2,3,448,128]{4,3,2,1,0:T(8,128)(2,1)}, bf16[2,2,3,448,128]{4,3,2,1,0:T(8,128)(2,1)}, u32[]{:S(2)}, u32[]{:S(2)}) collective-permute-start(bf16[2,2,3,448,128]{4,3,2,1,0:T(8,128)(2,1)} %dynamic-slice_bitcast_fusion.3.refs_5_), channel_id=1, source_target_pairs={{0,16},{4,20},{8,24},{12,28},{16,0},{20,4},{24,8},{28,12},{1,17},{... | collective-permute-start | bytes 4128776 | tf_op jit(solution)/shard_map/ppermute | solution.py:43
  590.8 96.7 %collective-permute-start.32 = (bf16[2,2,3,448,128]{4,3,2,1,0:T(8,128)(2,1)}, bf16[2,2,3,448,128]{4,3,2,1,0:T(8,128)(2,1)}, u32[]{:S(2)}, u32[]{:S(2)}) collective-permute-start(bf16[2,2,3,448,128]{4,3,2,1,0:T(8,128)(2,1)} %dynamic-slice_bitcast_fusion.4.refs_4_), channel_id=1, source_target_pairs={{0,8},{4,12},{8,0},{12,4},{16,24},{20,28},{24,16},{28,20},{1,9},{5... | collective-permute-start | bytes 4128776 | tf_op jit(solution)/shard_map/ppermute | solution.py:43
  675.2 261.9 %collective-permute-start.38 = (bf16[2,2,96,1024]{3,2,1,0:T(8,128)(2,1)S(1)}, bf16[2,2,96,1024]{3,2,1,0:T(8,128)(2,1)}, u32[]{:S(2)}, u32[]{:S(2)}) collective-permute-start(bf16[2,2,96,1024]{3,2,1,0:T(8,128)(2,1)S(1)} %get-tuple-element.158.refs_0_), channel_id=1, source_target_pairs={{0,1},{1,2},{2,3},{3,0},{4,5},{5,6},{6,7},{7,4},{8,9},{9,10},{10,1... | collective-permute-start | bytes 2359304 | tf_op jit(solution)/shard_map/ppermute | solution.py:30
  690.5 56.0 %collective-permute-start.36 = (bf16[2,3,448,128]{3,2,1,0:T(8,128)(2,1)S(1)}, bf16[2,3,448,128]{3,2,1,0:T(8,128)(2,1)S(1)}, u32[]{:S(2)}, u32[]{:S(2)}) collective-permute-start(bf16[2,3,448,128]{3,2,1,0:T(8,128)(2,1)S(1)} %dynamic-slice_bitcast_fusion.11.refs_5_), channel_id=1, source_target_pairs={{0,16},{4,20},{8,24},{12,28},{16,0},{20,4},{24,8},{28,12},{1,17},{... | collective-permute-start | bytes 2064392 | tf_op jit(solution)/shard_map/ppermute | solution.py:43
  694.5 53.3 %collective-permute-start.37 = (bf16[2,3,448,128]{3,2,1,0:T(8,128)(2,1)S(1)}, bf16[2,3,448,128]{3,2,1,0:T(8,128)(2,1)}, u32[]{:S(2)}, u32[]{:S(2)}) collective-permute-start(bf16[2,3,448,128]{3,2,1,0:T(8,128)(2,1)S(1)} %dynamic-slice_bitcast_fusion.10.refs_6_), channel_id=1, source_target_pairs={{0,8},{4,12},{8,0},{12,4},{16,24},{20,28},{24,16},{28,20},{1,9},{5... | collective-permute-start | bytes 2064392 | tf_op jit(solution)/shard_map/ppermute | solution.py:43
  700.6 50.3 %collective-permute-start.34 = (bf16[2,4,448,128]{3,2,1,0:T(8,128)(2,1)S(1)}, bf16[2,4,448,128]{3,2,1,0:T(8,128)(2,1)}, u32[]{:S(2)}, u32[]{:S(2)}) collective-permute-start(bf16[2,4,448,128]{3,2,1,0:T(8,128)(2,1)S(1)} %dynamic-slice_bitcast_fusion.6.refs_3_), channel_id=1, source_target_pairs={{0,16},{4,20},{8,24},{12,28},{16,0},{20,4},{24,8},{28,12},{1,17},{... | collective-permute-start | bytes 2752520 | tf_op jit(solution)/shard_map/ppermute | solution.py:43
  700.9 51.5 %collective-permute-start.35 = (bf16[2,4,448,128]{3,2,1,0:T(8,128)(2,1)S(1)}, bf16[2,4,448,128]{3,2,1,0:T(8,128)(2,1)}, u32[]{:S(2)}, u32[]{:S(2)}) collective-permute-start(bf16[2,4,448,128]{3,2,1,0:T(8,128)(2,1)S(1)} %dynamic-slice_bitcast_fusion.5.refs_4_), channel_id=1, source_target_pairs={{0,8},{4,12},{8,0},{12,4},{16,24},{20,28},{24,16},{28,20},{1,9},{5... | collective-permute-start | bytes 2752520 | tf_op jit(solution)/shard_map/ppermute | solution.py:43
  746.5 192.8 %collective-permute-start.39 = (bf16[2,2,96,1024]{3,2,1,0:T(8,128)(2,1)S(1)}, bf16[2,2,96,1024]{3,2,1,0:T(8,128)(2,1)}, u32[]{:S(2)}, u32[]{:S(2)}) collective-permute-start(bf16[2,2,96,1024]{3,2,1,0:T(8,128)(2,1)S(1)} %get-tuple-element.157.refs_1_), channel_id=1, source_target_pairs={{0,2},{1,3},{2,0},{3,1},{4,6},{5,7},{6,4},{7,5},{8,10},{9,11},{10,... | collective-permute-start | bytes 2359304 | tf_op jit(solution)/shard_map/ppermute | solution.py:30
  747.8 199.4 %collective-permute-start.40 = (bf16[2,2,96,1024]{3,2,1,0:T(8,128)(2,1)S(1)}, bf16[2,2,96,1024]{3,2,1,0:T(8,128)(2,1)}, u32[]{:S(2)}, u32[]{:S(2)}) collective-permute-start(bf16[2,2,96,1024]{3,2,1,0:T(8,128)(2,1)S(1)} %get-tuple-element.156.refs_2_), channel_id=1, source_target_pairs={{0,3},{1,0},{2,1},{3,2},{4,7},{5,4},{6,5},{7,6},{8,11},{9,8},{10,9... | collective-permute-start | bytes 2359304 | tf_op jit(solution)/shard_map/ppermute | solution.py:30
  756.6 192.1 %collective-permute-start.41 = (bf16[6272,128]{1,0:T(8,128)(2,1)}, bf16[6272,128]{1,0:T(8,128)(2,1)}, u32[]{:S(2)}, u32[]{:S(2)}) collective-permute-start(bf16[6272,128]{1,0:T(8,128)(2,1)} %get-tuple-element.155), channel_id=1, source_target_pairs={{0,4},{4,0},{8,12},{12,8},{16,20},{20,16},{24,28},{28,24},{1,5},{5... | collective-permute-start | bytes 4816904 | tf_op jit(solution)/shard_map/ppermute | solution.py:43
  (136 other events, 1273.9 us)

commit v4 on v3

--- a/solution.py
+++ b/solution.py
@@ -252,9 +252,17 @@
     steps, width = queries.shape
     lane = lax.broadcasted_iota(jnp.int32, (steps, 128), 1)
     kept = jnp.zeros((steps, 128), jnp.float32)
+
+    def first(pair):
+        here = slice(pair * 128, (pair + 1) * 128)
+        return pair_scores(info, causal, two_heads(queries[:, here]), keys[:, here])
+
+    following = first(0)
     for pair in range(width // 128):
         here = slice(pair * 128, (pair + 1) * 128)
-        scores = pair_scores(info, causal, two_heads(queries[:, here]), keys[:, here])
+        scores = following
+        if pair + 1 < width // 128:
+            following = first(pair + 1)
         row_max = jnp.max(scores, axis=1, keepdims=True)
         expos = jnp.exp(scores - row_max)
         row_sum = jnp.sum(expos, axis=1, keepdims=True)
@@ -272,17 +280,27 @@
     d_queries, d_keys, d_values = refs[-3:]
     steps, width = queries.shape
     rows_first = (((0,), (0,)), ((), ()))
-    for pair in range(width // 128):
+
+    def first(pair):
         here = slice(pair * 128, (pair + 1) * 128)
         both = two_heads(queries[:, here])
         both_grads = two_heads(grads[:, here])
+        scores = pair_scores(info, causal, both, keys[:, here])
+        d_probs = lax.dot_general(
+            both_grads, values[:, here], (((1,), (1,)), ((), ())), preferred_element_type=jnp.float32
+        )
+        return both, both_grads, scores, d_probs
+
+    following = first(0)
+    for pair in range(width // 128):
+        here = slice(pair * 128, (pair + 1) * 128)
+        both, both_grads, scores, d_probs = following
+        if pair + 1 < width // 128:
+            following = first(pair + 1)
         log = jnp.concatenate(
             [logs[:, 2 * pair : 2 * pair + 1], logs[:, 2 * pair + 1 : 2 * pair + 2]], axis=0
         )
-        probs = jnp.exp(pair_scores(info, causal, both, keys[:, here]) - log)
-        d_probs = lax.dot_general(
-            both_grads, values[:, here], (((1,), (1,)), ((), ())), preferred_element_type=jnp.float32
-        )
+        probs = jnp.exp(scores - log)
         d_values[:, here] = lax.dot_general(
             probs.astype(jnp.bfloat16), both_grads, rows_first, preferred_element_type=jnp.float32
         ).astype(jnp.bfloat16)
@@ -339,6 +357,7 @@
     return value * share, share + value * (inv_root_tau * bell)
 
 
+SMALL = pl.CostEstimate(flops=1 << 20, bytes_accessed=1 << 16, transcendentals=0)
 PIECE = 128
 CHUNK = 256
 
@@ -497,9 +516,7 @@
         ],
         input_output_aliases={5 + place: place for place in range(len(kept))},
         compiler_params=pltpu.CompilerParams(vmem_limit_bytes=60 << 20),
-        cost_estimate=pl.CostEstimate(
-            flops=4 * rows * share * width, bytes_accessed=4 * share * width, transcendentals=0
-        ),
+        cost_estimate=SMALL,
         name=f"rows_pass_{step}",
     )(info, ids, own, mate, table, *kept, *earlier)
 
@@ -525,6 +542,7 @@
         in_specs=[flat, flat, cube, cube],
         out_specs=flat,
         out_shape=jax.ShapeDtypeStruct((rows, width), jnp.bfloat16),
+        cost_estimate=SMALL,
         name="join_pass",
     )(own, other, own_log, other_log)
 
@@ -553,6 +571,7 @@
         + [pl.BlockSpec(memory_space=pl.ANY)] * len(earlier),
         out_specs=flat,
         out_shape=jax.ShapeDtypeStruct((rows, width), jnp.float32),
+        cost_estimate=SMALL,
         name="home_pass",
     )(logs, weight, targets, *parts, *earlier)
 
@@ -602,11 +621,13 @@
         live = info[1 + source * (count + 1) + count]
         chunks = (live + CHUNK - 1) // CHUNK
 
-        def add_two(pair, _):
-            add(source, pair * (2 * CHUNK), 2 * CHUNK)
-            return 0
-
-        lax.fori_loop(0, chunks // 2, add_two, 0)
+        @pl.when(chunks == 4)
+        def _():
+            add(source, 0, 4 * CHUNK)
+
+        @pl.when(jnp.logical_or(chunks == 2, chunks == 3))
+        def _():
+            add(source, 0, 2 * CHUNK)
 
         @pl.when(chunks % 2 == 1)
         def _():
@@ -650,11 +671,7 @@
         ),
         out_shape=[jax.ShapeDtypeStruct((n_pb, tiles, wide // 2, own), jnp.bfloat16)] * 2,
         compiler_params=pltpu.CompilerParams(vmem_limit_bytes=60 << 20),
-        cost_estimate=pl.CostEstimate(
-            flops=2 * sources * both * tiles * wide * width,
-            bytes_accessed=4 * sources * both * tiles * wide,
-            transcendentals=0,
-        ),
+        cost_estimate=SMALL,
         name=f"table_pass_{first}",
     )(info, facts, tops, rows, expos, *earlier)
 
@@ -879,7 +896,8 @@
 
     half = UNIT // 2
     first, second = pl.ds(0, half), pl.ds(half, half)
-    by_core = [push(block(n, 1 - core), from_core.at[n], mate) for n in range(len(units))]
+    ahead = 2
+    by_core = [push(block(n, 1 - core), from_core.at[n], mate) for n in range(ahead)]
     loads = {n: put(block(n, core), kept.at[n % depth]) for n in range(min(depth, len(units)))}
     by_rows = []
     for step in range(1, slots):
@@ -896,6 +914,8 @@
     def from_cores(n):
         slot = n % depth
         by_core[n].wait_recv()
+        if n + ahead < len(units):
+            by_core.append(push(block(n + ahead, 1 - core), from_core.at[n + ahead], mate))
         loads[n].wait()
 
         def step(i, _):
@@ -1046,6 +1066,7 @@
         compiler_params=pltpu.CompilerParams(
             collective_id=1, has_side_effects=True, vmem_limit_bytes=60 << 20
         ),
+        cost_estimate=SMALL,
         name="scatter_outputs",
     )(*mats, rows, small)
     return (*shards, laid.reshape((-1,) + laid.shape[2:]), small)
@@ -1214,7 +1235,6 @@
     facts = jnp.stack(facts + [ids_rows[:, 0]] + [jnp.zeros_like(facts[0])] * 4, axis=1)
     expos, packed, tops = kept
     tiles = expos.shape[1]
-    cut = tiles // 2 + 1
     n_pb = lax.axis_size("pb")
     tall, wide, _ = grid_of(n_pb)
     sends = tuple(homes[1:])
@@ -1222,7 +1242,7 @@
         shifted(homes[step], "slot", slot_count - step) for step in range(1, slot_count)
     ]
     table_grads = []
-    for first, count in ((0, cut), (cut, tiles - cut)):
+    for first, count in ((0, tiles),):
         sides = [
             side.reshape((tall, wide, cores) + side.shape[1:])
             for side in table_pass(
@@ -1261,10 +1281,10 @@
     )
     grad_ffn = grad_res_three.astype(jnp.bfloat16)
     grad_out_w = contract_rows(act_low, grad_ffn)
-    grad_act = contract_cols(grad_ffn, out_back)
+    grad_act = lax.optimization_barrier(contract_cols(grad_ffn, out_back))
     grad_pre = (grad_act * slope.astype(jnp.float32)).astype(jnp.bfloat16)
     grad_in_w = contract_rows(grad_pre, two_low)
-    grad_bias = jnp.sum(lax.optimization_barrier(grad_pre).astype(jnp.float32), axis=0)
+    grad_bias = jnp.sum(grad_pre.astype(jnp.float32), axis=0)
     grad_two = grad_res_three + product(grad_pre, in_back)
     grad_res_two, gain_two, shift_two = norm_backward(grad_two, normed_two, root_two, norms[2])
     grad_cross = grad_res_two.astype(jnp.bfloat16)
@@ -1283,7 +1303,7 @@
         grad_memory.reshape(slots_here, questions, mem_steps, model_width)
     )
     table_sum = [over_first(sides, cq_grad) for sides in table_grads]
-    earlier = grad_memory[1:] + [*second_sends(table_sum[0]), *second_sends(table_sum[1])]
+    earlier = grad_memory[1:] + [send for sides in table_sum for send in second_sends(sides)]
     grad_one = grad_res_two + contract_cols(cq_grad, back_blocks[4]) * scaling
     grad_res_one, gain_one, shift_one = norm_backward(grad_one, normed_one, root_one, norms[0])
     grad_attn_out = grad_res_one.astype(jnp.bfloat16)

time: 977 us -> 958 us (0.981); the launches traced: 962 us -> 966 us
  starting transfers between devices: 36 us -> 97.9 us
  Pallas kernels: 621 us -> 561 us
  matrix products: 125 us -> 115 us
    ppermute x24 -> x20, starting transfers between devices: 10.3 us -> 57.2 us  [shifted(): return lax.ppermute(value, 'pb', pairs)]
    pallas_call x2 -> x1, Pallas kernels: 92 us -> 64.1 us  [table_pass(): pl.pallas_call(functools.partial(table_kernel, first), grid_spec=pltpu.Pr...]
    pallas_call x4, Pallas kernels: 129 us -> 110 us  [rows_pass(): pl.pallas_call(functools.partial(rows_kernel, step), grid_spec=pltpu.Pref...]
    ppermute x18, starting transfers between devices: 25.7 us -> 40.7 us  [shifted(): lax.ppermute(value, 'slot', [(i, (i + step) % size) for i in range(size)])]
    pallas_call x4, Pallas kernels: 53.2 us -> 41.1 us  [attend(): pl.pallas_call(functools.partial(kernel, causal), grid_spec=pltpu.Prefetc...]
    unnamed x242 -> x216, local copies, waits for them, and re-layouts: 27.2 us -> 28.6 us
  transfers between devices with their start and end apart: 42 -> 38, of which waited for: 6 -> 7; matrix products, arithmetic and copies ran while one was open for 24% -> 23% of each run, Pallas kernels for 65% -> 58%
where the time goes in v4:
time: 958 us; the launch traced here: 966 us
  Pallas kernels  561 us (59%)
  matrix products  115 us (12%)
  starting transfers between devices  97.9 us (10%)
  local copies, waits for them, and re-layouts  86.7 us (9%)
  other arithmetic  57.6 us (6%)
  waiting for transfers between devices  30.3 us (3%)
  between operations  17.7 us (2%)
    pallas_call x1, Pallas kernels, gather_inputs(): pl.pallas_call(gather_kernel, in_specs=[anywhere] * 5, out_specs=[anywher...  165 us
    pallas_call x1, Pallas kernels, scatter_outputs(): pl.pallas_call(scatter_kernel, in_specs=[anywhere] * 4 + [inside], out_sp...  164 us
    pallas_call x4, Pallas kernels, rows_pass(): pl.pallas_call(functools.partial(rows_kernel, step), grid_spec=pltpu.Pref...  110 us
    pallas_call x1, Pallas kernels, table_pass(): pl.pallas_call(functools.partial(table_kernel, first), grid_spec=pltpu.Pr...  64.1 us
    ppermute x20, starting transfers between devices, shifted(): return lax.ppermute(value, 'pb', pairs)  57.2 us
    dot_general x10, matrix products, contract_cols(): lax.dot_general(left, right, (((1,), (1,)), ((), ())), preferred_element_...  49.2 us
    pallas_call x4, Pallas kernels, attend(): pl.pallas_call(functools.partial(kernel, causal), grid_spec=pltpu.Prefetc...  41.1 us
    ppermute x18, starting transfers between devices, shifted(): lax.ppermute(value, 'slot', [(i, (i + step) % size) for i in range(size)])  40.7 us
  transfers between devices with their start and end apart: 38, of which 7 were waited for; matrix products, arithmetic and copies ran while one was open for 23% of the time, Pallas kernels for 58%

profile of v4, /device:TPU:0, one launch (start us, length us, event | category | flops | bytes accessed | tf_op | source)
XLA Modules:
  0.0 966.2 jit_solution(4487315754862107024)
XLA Ops:
  9.0 164.6 %gather_inputs.1 = (bf16[8,4,256,1024]{3,2,1,0:T(8,128)(2,1)}, bf16[8,4,128,1024]{3,2,1,0:T(8,128)(2,1)}, bf16[8,4,128,1024]{3,2,1,0:T(8,128)(2,1)}, bf16[2,2,4,...) custom-call(bf16[256,1024]{1,0:T(8,128)(2,1)} %refs_0_.1, bf16[128,1024]{1,0:T(8,128)(2,1)} %refs_1_.1, ...), custom_call_target="tpu_custom_call" | custom-call | tf_op jit(solution)/shard_map/gather_inputs/pallas_call | solution.py:821
  176.1 13.2 %gather_fusion.2 = bf16[256,1024]{1,0:T(8,128)(2,1)S(1)} fusion(bf16[12544,1024]{1,0:T(8,128)(2,1)} %table.7, s32[1024]{0:T(1024)S(1)} %pad_clamp_fusion.1), kind=kCustom, calls=%fused_computation.2 | custom fusion | bytes 1049600 | tf_op jit(solution)/shard_map/jit(_take)/gather | solution.py:1151
  192.0 10.0 %fusion.61 = (bf16[1,4,256,1024]{3,2,1,0:T(8,128)(2,1)}, bf16[1,4,256,1024]{3,2,1,0:T(8,128)(2,1)}, bf16[1,4,256,1024]{3,2,1,0:T(8,128)(2,1)}, bf16[1,4,256,1024...) fusion(bf16[8,4,256,1024]{3,2,1,0:T(8,128)(2,1)} %get-tuple-ele, ...), kind=kLoop, calls=%fused_computation.251 | loop fusion | bytes 33554432 | tf_op jit(solution)/shard_map/slice | solution.py:1099
  214.1 7.7 convolution_convert_fusion.2.values
  236.2 10.4 %cross_attend.1 = (bf16[512,1024]{1,0:T(8,128)(2,1)S(1)}, f32[512,128]{1,0:T(8,128)S(1)}) custom-call(s32[4]{0:T(128)S(1)} %reshape.539.info, bf16[512,1024]{1,0:T(8,128)(2,1)S(1)} %multiply_convert_fusion.4.queries, bf16[1536,1024]{1,0:T(8,128)(2,1)S(1)} %copy-done.9, bf16[1536,1024]{1,0:T(8,128)(2,1)} %convolution_convert_fusion.2.values), custom_call_target="tpu_custom_call" | custom-call | flops 3221225472 | bytes 12582912 | tf_op jit(solution)/shard_map/cross_attend/pallas_call | solution.py:335
  249.3 15.0 %multiply_convert_fusion.1 = (bf16[512,4096]{1,0:T(8,128)(2,1)S(1)}, f32[512,4096]{1,0:T(8,128)}) fusion(f32[4096]{0:T(1024)S(1)} %copy-done.68, bf16[4096,1024]{1,0:T(8,128)(2,1)} %bitcast.394, f32[512,1024]{1,0:T(8,128)S(1)} %get-tuple-element.184, f32[1024]{0:T(1024)S(1)} %bitcast.379, f32[1024]{0:T(1024)S(1)} %bitcast.364, f32[512]{0:T(512)S(1)} %add_rsqrt_fusion.1, ...), kind=kOutput, calls=%fused_computation.15 | convolution fusion | flops 4345823232 | bytes 23097344 | tf_op jit(solution)/shard_map/dot_general | solution.py:203
  278.8 34.3 %rows_pass_0.1 = (bf16[4,7,1024,896]{3,2,1,0:T(8,128)(2,1)}, bf16[4,1152,1024]{2,1,0:T(8,128)(2,1)}, f32[4,1152,128]{2,1,0:T(8,128)}, bf16[512,1024]{1,0:T(8,128...) custom-call(s32[37]{0:T(128)} %pad_add_fusion.4.info, ...), custom_call_target="tpu_custom_call" | custom-call | flops 1048576 | bytes 65536 | tf_op jit(solution)/shard_map/rows_pass_0/pallas_call | solution.py:480
  320.6 20.7 %rows_pass_1.1 = (bf16[4,7,1024,896]{3,2,1,0:T(8,128)(2,1)}, bf16[4,1152,1024]{2,1,0:T(8,128)(2,1)}, f32[4,1152,128]{2,1,0:T(8,128)}, bf16[512,1024]{1,0:T(8,128...) custom-call(s32[37]{0:T(128)} %pad_add_fusion.4.info, ...), custom_call_target="tpu_custom_call", output_to_operand_aliasing={{0}: (5, {}), {1}: (6, {}), {2}: (7, {})} | custom-call | flops 1048576 | bytes 65536 | tf_op jit(solution)/shard_map/rows_pass_1/pallas_call | solution.py:480
  344.0 22.3 %collective-permute-done.7 = bf16[512,1024]{1,0:T(8,128)(2,1)} collective-permute-done((bf16[512,1024]{1,0:T(8,128)(2,1)}, bf16[512,1024]{1,0:T(8,128)(2,1)}, u32[]{:S(2)}, u32[]{:S(2)}) %collective-permute-start.7) | collective-permute-done | bytes 1048608 | tf_op jit(solution)/shard_map/ppermute | solution.py:30
  370.4 20.4 %rows_pass_2.1 = (bf16[4,7,1024,896]{3,2,1,0:T(8,128)(2,1)}, bf16[4,1152,1024]{2,1,0:T(8,128)(2,1)}, f32[4,1152,128]{2,1,0:T(8,128)}, bf16[512,1024]{1,0:T(8,128...) custom-call(s32[37]{0:T(128)} %pad_add_fusion.4.info, ...), custom_call_target="tpu_custom_call", output_to_operand_aliasing={{0}: (5, {}), {1}: (6, {}), {2}: (7, {})} | custom-call | flops 1048576 | bytes 65536 | tf_op jit(solution)/shard_map/rows_pass_2/pallas_call | solution.py:480
  398.5 34.6 %rows_pass_3.1 = (bf16[4,7,1024,896]{3,2,1,0:T(8,128)(2,1)}, bf16[4,1152,1024]{2,1,0:T(8,128)(2,1)}, f32[4,1152,128]{2,1,0:T(8,128)}, bf16[512,1024]{1,0:T(8,128...) custom-call(s32[37]{0:T(128)} %pad_add_fusion.4.info, ...), custom_call_target="tpu_custom_call", output_to_operand_aliasing={{0}: (5, {}), {1}: (6, {}), {2}: (7, {})} | custom-call | flops 1048576 | bytes 65536 | tf_op jit(solution)/shard_map/rows_pass_3/pallas_call | solution.py:480
  434.9 15.5 %collective-permute-start.15 = (f32[36,128]{1,0:T(8,128)S(1)}, f32[36,128]{1,0:T(8,128)S(1)}, u32[]{:S(2)}, u32[]{:S(2)}) collective-permute-start(f32[36,128]{1,0:T(8,128)S(1)} %concatenate.23), channel_id=1, source_target_pairs={{0,2},{1,3},{2,0},{3,1},{4,6},{5,7},{6,4},{7,5},{8,10},{9,11},{10,... | collective-permute-start | bytes 55304 | tf_op jit(solution)/shard_map/ppermute | solution.py:30
  484.2 64.1 %table_pass_0.1 = (bf16[8,7,448,128]{3,2,1,0:T(8,128)(2,1)}, bf16[8,7,448,128]{3,2,1,0:T(8,128)(2,1)}) custom-call(s32[37]{0:T(128)} %pad_add_fusion.4.info, f32[32,8,128]{2,1,0:T(8,128)} %stack.137.facts, f32[4,1152,128]{2,1,0:T(8,128)} %get-tuple-element.105.tops, bf16[4,1152,1024]{2,1,0:T(8,128)(2,1)} %get-tuple-element.106.rows, ...), custom_call_target="tpu_custom_call" | custom-call | flops 1048576 | bytes 65536 | tf_op jit(solution)/shard_map/table_pass_0/pallas_call | solution.py:654
  552.4 50.8 %collective-permute-start.31 = (bf16[2,2,7,448,128]{4,3,2,1,0:T(8,128)(2,1)}, bf16[2,2,7,448,128]{4,3,2,1,0:T(8,128)(2,1)}, u32[]{:S(2)}, u32[]{:S(2)}) collective-permute-start(bf16[2,2,7,448,128]{4,3,2,1,0:T(8,128)(2,1)} %dynamic-slice_bitcast_fusion.refs_5_), channel_id=1, source_target_pairs={{0,16},{4,20},{8,24},{12,28},{16,0},{20,4},{24,8},{28,12},{1,17},{... | collective-permute-start | bytes 9633800 | tf_op jit(solution)/shard_map/ppermute | solution.py:43
  618.5 7.8 fusion.19
  626.3 8.1 convert_reduce_fusion
  634.4 9.2 multiply_reduce_fusion.1
  646.6 16.5 %cross_attend_back.1 = (bf16[512,1024]{1,0:T(8,128)(2,1)S(1)}, bf16[1536,1024]{1,0:T(8,128)(2,1)}, bf16[1536,1024]{1,0:T(8,128)(2,1)}) custom-call(s32[4]{0:T(128)S(1)} %reshape.539.info, bf16[512,1024]{1,0:T(8,128)(2,1)S(1)} %multiply_convert_fusion.4.queries, bf16[1536,1024]{1,0:T(8,128)(2,1)} %convolution_convert_fusion.3.keys, ...), custom_call_target="tpu_custom_call" | custom-call | flops 8053063680 | bytes 12582912 | tf_op jit(solution)/shard_map/cross_attend_back/pallas_call | solution.py:335
  663.2 5.9 fusion.68
  691.4 6.9 convolution_convert_fusion
  698.4 7.1 convolution_convert_fusion.1
  717.0 9.8 %self_attend_back.1 = (bf16[512,1024]{1,0:T(8,128)(2,1)S(1)}, bf16[512,1024]{1,0:T(8,128)(2,1)S(1)}, bf16[512,1024]{1,0:T(8,128)(2,1)S(1)}) custom-call(s32[4]{0:T(128)S(1)} %copy-done.4, bf16[512,1024]{1,0:T(8,128)(2,1)} %copy-done.2, bf16[512,1024]{1,0:T(8,128)(2,1)} %copy-done.1, bf16[512,1024]{1,0:T(8,128)(2,1)} %copy-done, ...), custom_call_target="tpu_custom_call" | custom-call | flops 2684354560 | bytes 4194304 | tf_op jit(solution)/shard_map/self_attend_back/pallas_call | solution.py:335
  763.9 5.8 copy-done.15
  772.9 164.3 %scatter_outputs.1 = (f32[256,1024]{1,0:T(8,128)}, f32[128,1024]{1,0:T(8,128)}, f32[128,1024]{1,0:T(8,128)}, bf16[2,4,2,32,1024]{4,3,2,1,0:T(8,128)(2,1)}, f32[16,1024]{1,0:T(8,128)}) custom-call(bf16[4,2,4,256,1024]{4,3,2,1,0:T(8,128)(2,1)} %bitcast.291, bf16[4,2,4,128,1024]{4,3,2,1,0:T(8,128)(2,1)} %bitcast.298, bf16[4,2,4,128,1024]{4,3,2,1,0:T(8,128)(2,1)} %bitcast.297, ...), custom_call_target="tpu_custom_call" | custom-call | flops 1048576 | bytes 65536 | tf_op jit(solution)/shard_map/scatter_outputs/pallas_call | solution.py:1045
  (485 shorter events, 223.7 us)
Async XLA Ops:
  0.6 229.9 %collective-permute-start = (s32[2,2]{1,0:T(2,128)}, s32[2,2]{1,0:T(2,128)S(1)}, u32[]{:S(2)}, u32[]{:S(2)}) collective-permute-start(s32[2,2]{1,0:T(2,128)} %param.21), channel_id=1, source_target_pairs={{0,1},{1,2},{2,3},{3,0},{4,5},{5,6},{6,7},{7,4},{8,9},{9,10},{10,1... | collective-permute-start | bytes 56 | tf_op jit(solution)/shard_map/ppermute | solution.py:30
  3.7 229.9 %collective-permute-start.1 = (s32[2,2]{1,0:T(2,128)}, s32[2,2]{1,0:T(2,128)S(1)}, u32[]{:S(2)}, u32[]{:S(2)}) collective-permute-start(s32[2,2]{1,0:T(2,128)} %param.21), channel_id=1, source_target_pairs={{0,2},{1,3},{2,0},{3,1},{4,6},{5,7},{6,4},{7,5},{8,10},{9,11},{10,... | collective-permute-start | bytes 56 | tf_op jit(solution)/shard_map/ppermute | solution.py:30
  6.3 227.3 %collective-permute-start.2 = (s32[2,2]{1,0:T(2,128)}, s32[2,2]{1,0:T(2,128)S(1)}, u32[]{:S(2)}, u32[]{:S(2)}) collective-permute-start(s32[2,2]{1,0:T(2,128)} %param.21), channel_id=1, source_target_pairs={{0,3},{1,0},{2,1},{3,2},{4,7},{5,4},{6,5},{7,6},{8,11},{9,8},{10,9... | collective-permute-start | bytes 56 | tf_op jit(solution)/shard_map/ppermute | solution.py:30
  190.2 79.2 %collective-permute-start.11 = (bf16[2,128,1024]{2,1,0:T(8,128)(2,1)}, bf16[2,128,1024]{2,1,0:T(8,128)(2,1)S(1)}, u32[]{:S(2)}, u32[]{:S(2)}) collective-permute-start(bf16[2,128,1024]{2,1,0:T(8,128)(2,1)} %select_select_fusion), channel_id=1, source_target_pairs={{0,1},{1,2},{2,3},{3,0},{4,5},{5,6},{6,7},{7,4},{8,9},{9,10},{10,1... | collective-permute-start | bytes 1572872 | tf_op jit(solution)/shard_map/ppermute | solution.py:30
  190.4 79.0 %collective-permute-start.12 = (bf16[2,128,1024]{2,1,0:T(8,128)(2,1)}, bf16[2,128,1024]{2,1,0:T(8,128)(2,1)S(1)}, u32[]{:S(2)}, u32[]{:S(2)}) collective-permute-start(bf16[2,128,1024]{2,1,0:T(8,128)(2,1)} %select_select_fusion), channel_id=1, source_target_pairs={{0,2},{1,3},{2,0},{3,1},{4,6},{5,7},{6,4},{7,5},{8,10},{9,11},{10,... | collective-permute-start | bytes 1572872 | tf_op jit(solution)/shard_map/ppermute | solution.py:30
  230.6 40.7 %collective-permute-start.13 = (bf16[2,128,1024]{2,1,0:T(8,128)(2,1)}, bf16[2,128,1024]{2,1,0:T(8,128)(2,1)}, u32[]{:S(2)}, u32[]{:S(2)}) collective-permute-start(bf16[2,128,1024]{2,1,0:T(8,128)(2,1)} %select_select_fusion), channel_id=1, source_target_pairs={{0,3},{1,0},{2,1},{3,2},{4,7},{5,4},{6,5},{7,6},{8,11},{9,8},{10,9... | collective-permute-start | bytes 1572872 | tf_op jit(solution)/shard_map/ppermute | solution.py:30
  233.6 42.2 %collective-permute-start.3 = (s32[2,130]{1,0:T(2,128)S(1)}, s32[2,130]{1,0:T(2,128)S(1)}, u32[]{:S(2)}, u32[]{:S(2)}) collective-permute-start(s32[2,130]{1,0:T(2,128)S(1)} %pad_add_fusion.2), channel_id=1, source_target_pairs={{0,4},{4,0},{8,12},{12,8},{16,20},{20,16},{24,28},{28,24},{1,5},{5... | collective-permute-start | bytes 3128 | tf_op jit(solution)/shard_map/ppermute | solution.py:43
  275.2 40.4 %collective-permute-start.5 = (bf16[512,1024]{1,0:T(8,128)(2,1)}, bf16[512,1024]{1,0:T(8,128)(2,1)}, u32[]{:S(2)}, u32[]{:S(2)}) collective-permute-start(bf16[512,1024]{1,0:T(8,128)(2,1)} %get-tuple-element.143.own), channel_id=1, source_target_pairs={{0,1},{1,2},{2,3},{3,0},{4,5},{5,6},{6,7},{7,4},{8,9},{9,10},{10,1... | collective-permute-start | bytes 3145736 | tf_op jit(solution)/shard_map/ppermute | solution.py:30
  317.3 49.0 %collective-permute-start.7 = (bf16[512,1024]{1,0:T(8,128)(2,1)}, bf16[512,1024]{1,0:T(8,128)(2,1)}, u32[]{:S(2)}, u32[]{:S(2)}) collective-permute-start(bf16[512,1024]{1,0:T(8,128)(2,1)} %get-tuple-element.143.own), channel_id=1, source_target_pairs={{0,2},{1,3},{2,0},{3,1},{4,6},{5,7},{6,4},{7,5},{8,10},{9,11},{10,... | collective-permute-start | bytes 3145736 | tf_op jit(solution)/shard_map/ppermute | solution.py:30
  368.9 65.8 %collective-permute-start.18 = (f32[2,8]{1,0:T(2,128)S(1)}, f32[2,8]{1,0:T(2,128)S(1)}, u32[]{:S(2)}, u32[]{:S(2)}) collective-permute-start(f32[2,8]{1,0:T(2,128)S(1)} %copy-done.85), channel_id=1, source_target_pairs={{0,4},{4,0},{8,12},{12,8},{16,20},{20,16},{24,28},{28,24},{1,5},{5... | collective-permute-start | bytes 200 | tf_op jit(solution)/shard_map/ppermute | solution.py:43
  369.3 87.2 %collective-permute-start.19 = (bf16[512,1024]{1,0:T(8,128)(2,1)}, bf16[512,1024]{1,0:T(8,128)(2,1)}, u32[]{:S(2)}, u32[]{:S(2)}) collective-permute-start(bf16[512,1024]{1,0:T(8,128)(2,1)} %get-tuple-element.98), channel_id=1, source_target_pairs={{0,4},{4,0},{8,12},{12,8},{16,20},{20,16},{24,28},{28,24},{1,5},{5... | collective-permute-start | bytes 3145736 | tf_op jit(solution)/shard_map/ppermute | solution.py:43
  395.0 65.0 %collective-permute-start.21 = (bf16[512,1024]{1,0:T(8,128)(2,1)}, bf16[512,1024]{1,0:T(8,128)(2,1)}, u32[]{:S(2)}, u32[]{:S(2)}) collective-permute-start(bf16[512,1024]{1,0:T(8,128)(2,1)} %get-tuple-element.100), channel_id=1, source_target_pairs={{0,4},{4,0},{8,12},{12,8},{16,20},{20,16},{24,28},{28,24},{1,5},{5... | collective-permute-start | bytes 3145736 | tf_op jit(solution)/shard_map/ppermute | solution.py:43
  395.5 72.1 %collective-permute-start.24 = (bf16[512,1024]{1,0:T(8,128)(2,1)}, bf16[512,1024]{1,0:T(8,128)(2,1)}, u32[]{:S(2)}, u32[]{:S(2)}) collective-permute-start(bf16[512,1024]{1,0:T(8,128)(2,1)} %get-tuple-element.102), channel_id=1, source_target_pairs={{0,4},{4,0},{8,12},{12,8},{16,20},{20,16},{24,28},{28,24},{1,5},{5... | collective-permute-start | bytes 3145736 | tf_op jit(solution)/shard_map/ppermute | solution.py:43
  463.4 143.2 %collective-permute-start.23 = (bf16[512,1024]{1,0:T(8,128)(2,1)}, bf16[512,1024]{1,0:T(8,128)(2,1)}, u32[]{:S(2)}, u32[]{:S(2)}) collective-permute-start(bf16[512,1024]{1,0:T(8,128)(2,1)} %join_pass.5.refs_0_), channel_id=1, source_target_pairs={{0,3},{1,0},{2,1},{3,2},{4,7},{5,4},{6,5},{7,6},{8,11},{9,8},{10,9... | collective-permute-start | bytes 3145736 | tf_op jit(solution)/shard_map/ppermute | solution.py:30
  470.6 135.9 %collective-permute-start.26 = (bf16[512,1024]{1,0:T(8,128)(2,1)}, bf16[512,1024]{1,0:T(8,128)(2,1)}, u32[]{:S(2)}, u32[]{:S(2)}) collective-permute-start(bf16[512,1024]{1,0:T(8,128)(2,1)} %join_pass.6.refs_1_), channel_id=1, source_target_pairs={{0,2},{1,3},{2,0},{3,1},{4,6},{5,7},{6,4},{7,5},{8,10},{9,11},{10,... | collective-permute-start | bytes 3145736 | tf_op jit(solution)/shard_map/ppermute | solution.py:30
  478.7 127.9 %collective-permute-start.29 = (bf16[512,1024]{1,0:T(8,128)(2,1)}, bf16[512,1024]{1,0:T(8,128)(2,1)S(1)}, u32[]{:S(2)}, u32[]{:S(2)}) collective-permute-start(bf16[512,1024]{1,0:T(8,128)(2,1)} %join_pass.7.refs_2_), channel_id=1, source_target_pairs={{0,1},{1,2},{2,3},{3,0},{4,5},{5,6},{6,7},{7,4},{8,9},{9,10},{10,1... | collective-permute-start | bytes 3145736 | tf_op jit(solution)/shard_map/ppermute | solution.py:30
  552.4 153.1 %collective-permute-start.31 = (bf16[2,2,7,448,128]{4,3,2,1,0:T(8,128)(2,1)}, bf16[2,2,7,448,128]{4,3,2,1,0:T(8,128)(2,1)}, u32[]{:S(2)}, u32[]{:S(2)}) collective-permute-start(bf16[2,2,7,448,128]{4,3,2,1,0:T(8,128)(2,1)} %dynamic-slice_bitcast_fusion.refs_5_), channel_id=1, source_target_pairs={{0,16},{4,20},{8,24},{12,28},{16,0},{20,4},{24,8},{28,12},{1,17},{... | collective-permute-start | bytes 9633800 | tf_op jit(solution)/shard_map/ppermute | solution.py:43
  605.1 105.9 %collective-permute-start.30 = (bf16[2,2,7,448,128]{4,3,2,1,0:T(8,128)(2,1)}, bf16[2,2,7,448,128]{4,3,2,1,0:T(8,128)(2,1)}, u32[]{:S(2)}, u32[]{:S(2)}) collective-permute-start(bf16[2,2,7,448,128]{4,3,2,1,0:T(8,128)(2,1)} %dynamic-slice_bitcast_fusion.1.refs_4_), channel_id=1, source_target_pairs={{0,8},{4,12},{8,0},{12,4},{16,24},{20,28},{24,16},{28,20},{1,9},{5... | collective-permute-start | bytes 9633800 | tf_op jit(solution)/shard_map/ppermute | solution.py:43
  675.8 265.3 %collective-permute-start.34 = (bf16[2,2,96,1024]{3,2,1,0:T(8,128)(2,1)S(1)}, bf16[2,2,96,1024]{3,2,1,0:T(8,128)(2,1)}, u32[]{:S(2)}, u32[]{:S(2)}) collective-permute-start(bf16[2,2,96,1024]{3,2,1,0:T(8,128)(2,1)S(1)} %get-tuple-element.156.refs_0_), channel_id=1, source_target_pairs={{0,1},{1,2},{2,3},{3,0},{4,5},{5,6},{6,7},{7,4},{8,9},{9,10},{10,1... | collective-permute-start | bytes 2359304 | tf_op jit(solution)/shard_map/ppermute | solution.py:30
  678.6 264.8 %collective-permute-start.35 = (bf16[2,2,96,1024]{3,2,1,0:T(8,128)(2,1)S(1)}, bf16[2,2,96,1024]{3,2,1,0:T(8,128)(2,1)}, u32[]{:S(2)}, u32[]{:S(2)}) collective-permute-start(bf16[2,2,96,1024]{3,2,1,0:T(8,128)(2,1)S(1)} %get-tuple-element.155.refs_1_), channel_id=1, source_target_pairs={{0,2},{1,3},{2,0},{3,1},{4,6},{5,7},{6,4},{7,5},{8,10},{9,11},{10,... | collective-permute-start | bytes 2359304 | tf_op jit(solution)/shard_map/ppermute | solution.py:30
  679.4 271.8 %collective-permute-start.36 = (bf16[2,2,96,1024]{3,2,1,0:T(8,128)(2,1)S(1)}, bf16[2,2,96,1024]{3,2,1,0:T(8,128)(2,1)}, u32[]{:S(2)}, u32[]{:S(2)}) collective-permute-start(bf16[2,2,96,1024]{3,2,1,0:T(8,128)(2,1)S(1)} %get-tuple-element.154.refs_2_), channel_id=1, source_target_pairs={{0,3},{1,0},{2,1},{3,2},{4,7},{5,4},{6,5},{7,6},{8,11},{9,8},{10,9... | collective-permute-start | bytes 2359304 | tf_op jit(solution)/shard_map/ppermute | solution.py:30
  715.5 39.3 %collective-permute-start.32 = (bf16[2,7,448,128]{3,2,1,0:T(8,128)(2,1)}, bf16[2,7,448,128]{3,2,1,0:T(8,128)(2,1)}, u32[]{:S(2)}, u32[]{:S(2)}) collective-permute-start(bf16[2,7,448,128]{3,2,1,0:T(8,128)(2,1)} %dynamic-slice_bitcast_fusion.4.refs_3_), channel_id=1, source_target_pairs={{0,16},{4,20},{8,24},{12,28},{16,0},{20,4},{24,8},{28,12},{1,17},{... | collective-permute-start | bytes 4816904 | tf_op jit(solution)/shard_map/ppermute | solution.py:43
  716.4 40.5 %collective-permute-start.33 = (bf16[2,7,448,128]{3,2,1,0:T(8,128)(2,1)}, bf16[2,7,448,128]{3,2,1,0:T(8,128)(2,1)}, u32[]{:S(2)}, u32[]{:S(2)}) collective-permute-start(bf16[2,7,448,128]{3,2,1,0:T(8,128)(2,1)} %dynamic-slice_bitcast_fusion.3.refs_4_), channel_id=1, source_target_pairs={{0,8},{4,12},{8,0},{12,4},{16,24},{20,28},{24,16},{28,20},{1,9},{5... | collective-permute-start | bytes 4816904 | tf_op jit(solution)/shard_map/ppermute | solution.py:43
  761.5 191.2 %collective-permute-start.37 = (bf16[6272,128]{1,0:T(8,128)(2,1)}, bf16[6272,128]{1,0:T(8,128)(2,1)}, u32[]{:S(2)}, u32[]{:S(2)}) collective-permute-start(bf16[6272,128]{1,0:T(8,128)(2,1)} %get-tuple-element.153), channel_id=1, source_target_pairs={{0,4},{4,0},{8,12},{12,8},{16,20},{20,16},{24,28},{28,24},{1,5},{5... | collective-permute-start | bytes 4816904 | tf_op jit(solution)/shard_map/ppermute | solution.py:43
  (119 other events, 903.7 us)

commit v5 on v4

--- a/solution.py
+++ b/solution.py
@@ -521,30 +521,68 @@
     )(info, ids, own, mate, table, *kept, *earlier)
 
 
-def join_kernel(own, other, own_log, other_log, out):
-    for piece in range(own_log.shape[0]):
-        here = slice(piece * PIECE, (piece + 1) * PIECE)
-        log = jnp.logaddexp(own_log[piece], other_log[piece])
-        left = columns(jnp.exp(own_log[piece] - log))[:, 0:1]
-        right = columns(jnp.exp(other_log[piece] - log))[:, 0:1]
-        out[here, :] = (
-            own[here, :].astype(jnp.float32) * left + other[here, :].astype(jnp.float32) * right
-        ).astype(jnp.bfloat16)
-
-
-def join_pass(own, other, own_log, other_log):
-    rows, width = own.shape
+def join_kernel(count, *refs):
+    owns, others, own_logs, other_logs, outs = (
+        refs[place * count : (place + 1) * count] for place in range(5)
+    )
+    for own, other, own_log, other_log, out in zip(owns, others, own_logs, other_logs, outs):
+        for piece in range(own_log.shape[0]):
+            here = slice(piece * PIECE, (piece + 1) * PIECE)
+            log = jnp.logaddexp(own_log[piece], other_log[piece])
+            left = columns(jnp.exp(own_log[piece] - log))[:, 0:1]
+            right = columns(jnp.exp(other_log[piece] - log))[:, 0:1]
+            out[here, :] = (
+                own[here, :].astype(jnp.float32) * left + other[here, :].astype(jnp.float32) * right
+            ).astype(jnp.bfloat16)
+
+
+def join_pass(owns, others, own_logs, other_logs):
+    count = len(owns)
+    rows, width = owns[0].shape
     flat = pl.BlockSpec((CHUNK, width), lambda i: (i, 0))
     cube = pl.BlockSpec((CHUNK // PIECE, 8, 128), lambda i: (i, 0, 0))
     return pl.pallas_call(
-        join_kernel,
+        functools.partial(join_kernel, count),
         grid=(rows // CHUNK,),
-        in_specs=[flat, flat, cube, cube],
-        out_specs=flat,
-        out_shape=jax.ShapeDtypeStruct((rows, width), jnp.bfloat16),
+        in_specs=[flat] * (2 * count) + [cube] * (2 * count),
+        out_specs=[flat] * count,
+        out_shape=[jax.ShapeDtypeStruct((rows, width), jnp.bfloat16)] * count,
+        compiler_params=pltpu.CompilerParams(vmem_limit_bytes=48 << 20),
         cost_estimate=SMALL,
         name="join_pass",
-    )(own, other, own_log, other_log)
+    )(*owns, *others, *own_logs, *other_logs)
+
+
+def lay_kernel(count, info, *refs):
+    out = refs[-1]
+    step = (info[0] + count - pl.program_id(0)) % count
+    for place in range(count):
+
+        @pl.when(step == place)
+        def _():
+            out[:, 0] = refs[place][...]
+
+
+def lay_blocks(blocks, place, earlier):
+    count = len(blocks)
+    own, questions, steps, width = blocks[0].shape
+    whole = lambda i, s: (0, 0, 0, 0)
+    return pl.pallas_call(
+        functools.partial(lay_kernel, count),
+        grid_spec=pltpu.PrefetchScalarGridSpec(
+            num_scalar_prefetch=1,
+            grid=(count,),
+            in_specs=[pl.BlockSpec(blocks[0].shape, whole, pipeline_mode=pl.Buffered(1))] * count
+            + [pl.BlockSpec(memory_space=pl.ANY)] * len(earlier),
+            out_specs=pl.BlockSpec(
+                (own, 1, questions, steps, width), lambda i, s: (0, i, 0, 0, 0)
+            ),
+        ),
+        out_shape=jax.ShapeDtypeStruct((own, count, questions, steps, width), blocks[0].dtype),
+        compiler_params=pltpu.CompilerParams(vmem_limit_bytes=48 << 20),
+        cost_estimate=SMALL,
+        name="lay_blocks",
+    )(place.reshape(1).astype(jnp.int32), *blocks, *earlier)
 
 
 def home_kernel(count, logs, weight, targets, *refs):
@@ -1169,8 +1207,8 @@
 
     group = pieces * tgt_steps
     moving = three_low.reshape(group, model_width)
+    kept, log_list, joining = (), [], []
     arriving = [moving] + [shifted(moving, "slot", step) for step in range(1, slot_count)]
-    kept, log_list, homes = (), [], []
     for step in range(slot_count):
         moving = arriving[step] if not step else after(arriving[step], own_logs)
         other = shifted(moving, "core", 1)
@@ -1179,11 +1217,10 @@
             step, slot_count, info, ids_rows, moving, other, embedding, cores, kept, earlier
         )
         log_list += [own_logs[:, 0], mate_logs[:, 0]]
-        homes.append(
-            join_pass(
-                own_sums, shifted(mate_sums, "core", 1), own_logs, shifted(mate_logs, "core", 1)
-            )
+        joining.append(
+            (own_sums, shifted(mate_sums, "core", 1), own_logs, shifted(mate_logs, "core", 1))
         )
+    homes = list(join_pass(*zip(*joining)))
 
     def by_slot(value):
         parts = [value] + [shifted(value, "slot", step) for step in range(1, slot_count)]
@@ -1352,7 +1389,11 @@
         grad_inputs,
         after(small, table_send),
     )
-    grad_memory = to_positions(grad_memory, small)
+    grad_memory = [grad_memory[0]] + [
+        shifted(grad_memory[step], "slot", step) for step in range(1, slot_count)
+    ]
+    grad_memory = lay_blocks(grad_memory, place, (small,))
+    grad_memory = grad_memory.reshape((-1,) + grad_memory.shape[2:])
     kept = pick(table_sum, core, 0)
     given = after(shifted(table_send, "core", 1), small)
     grad_embed = jnp.stack([kept, given])

time: 958 us -> 942 us (0.983); the launches traced: 966 us -> 936 us
  Pallas kernels: 561 us -> 538 us
  starting transfers between devices: 97.9 us -> 84.1 us
  local copies, waits for them, and re-layouts: 86.7 us -> 97.7 us
    ppermute x18, starting transfers between devices: 40.7 us -> 28.8 us  [shifted(): lax.ppermute(value, 'slot', [(i, (i + step) % size) for i in range(size)])]
    pallas_call x4, Pallas kernels: 110 us -> 99.4 us  [rows_pass(): pl.pallas_call(functools.partial(rows_kernel, step), grid_spec=pltpu.Pref...]
    unnamed x216 -> x282, local copies, waits for them, and re-layouts: 28.6 us -> 31.1 us
  transfers between devices with their start and end apart: 38 -> 38, of which waited for: 7 -> 5; matrix products, arithmetic and copies ran while one was open for 23% -> 25% of each run, Pallas kernels for 58% -> 54%
where the time goes in v5:
time: 942 us; the launch traced here: 936 us
  Pallas kernels  538 us (57%)
  matrix products  118 us (13%)
  local copies, waits for them, and re-layouts  97.7 us (10%)
  starting transfers between devices  84.1 us (9%)
  other arithmetic  54.1 us (6%)
  waiting for transfers between devices  26.5 us (3%)
  between operations  17.5 us (2%)
    pallas_call x1, Pallas kernels, gather_inputs(): pl.pallas_call(gather_kernel, in_specs=[anywhere] * 5, out_specs=[anywher...  165 us
    pallas_call x1, Pallas kernels, scatter_outputs(): pl.pallas_call(scatter_kernel, in_specs=[anywhere] * 4 + [inside], out_sp...  165 us
    pallas_call x4, Pallas kernels, rows_pass(): pl.pallas_call(functools.partial(rows_kernel, step), grid_spec=pltpu.Pref...  99.4 us
    ppermute x20, starting transfers between devices, shifted(): return lax.ppermute(value, 'pb', pairs)  55.3 us
    pallas_call x1, Pallas kernels, table_pass(): pl.pallas_call(functools.partial(table_kernel, first), grid_spec=pltpu.Pr...  54.7 us
    dot_general x10, matrix products, contract_cols(): lax.dot_general(left, right, (((1,), (1,)), ((), ())), preferred_element_...  51.6 us
    pallas_call x4, Pallas kernels, attend(): pl.pallas_call(functools.partial(kernel, causal), grid_spec=pltpu.Prefetc...  40.8 us
    dot_general x10, matrix products, product(): return jnp.dot(left, right, preferred_element_type=jnp.float32)  36.3 us
  transfers between devices with their start and end apart: 38, of which 5 were waited for; matrix products, arithmetic and copies ran while one was open for 25% of the time, Pallas kernels for 54%

profile of v5, /device:TPU:0, one launch (start us, length us, event | category | flops | bytes accessed | tf_op | source)
XLA Modules:
  0.0 935.5 jit_solution(5555882065213093189)
XLA Ops:
  9.0 164.6 %gather_inputs.1 = (bf16[8,4,256,1024]{3,2,1,0:T(8,128)(2,1)}, bf16[8,4,128,1024]{3,2,1,0:T(8,128)(2,1)}, bf16[8,4,128,1024]{3,2,1,0:T(8,128)(2,1)}, bf16[2,2,4,...) custom-call(bf16[256,1024]{1,0:T(8,128)(2,1)} %refs_0_.1, bf16[128,1024]{1,0:T(8,128)(2,1)} %refs_1_.1, ...), custom_call_target="tpu_custom_call" | custom-call | tf_op jit(solution)/shard_map/gather_inputs/pallas_call | solution.py:859
  176.1 13.2 %gather_fusion.2 = bf16[256,1024]{1,0:T(8,128)(2,1)S(1)} fusion(bf16[12544,1024]{1,0:T(8,128)(2,1)} %table.7, s32[1024]{0:T(1024)S(1)} %pad_clamp_fusion.1), kind=kCustom, calls=%fused_computation.2 | custom fusion | bytes 1049600 | tf_op jit(solution)/shard_map/jit(_take)/gather | solution.py:1189
  192.0 10.0 %fusion.61 = (bf16[1,4,256,1024]{3,2,1,0:T(8,128)(2,1)}, bf16[1,4,256,1024]{3,2,1,0:T(8,128)(2,1)}, bf16[1,4,256,1024]{3,2,1,0:T(8,128)(2,1)}, bf16[1,4,256,1024...) fusion(bf16[8,4,256,1024]{3,2,1,0:T(8,128)(2,1)} %get-tuple-ele, ...), kind=kLoop, calls=%fused_computation.248 | loop fusion | bytes 33554432 | tf_op jit(solution)/shard_map/slice | solution.py:1137
  213.3 7.7 convolution_convert_fusion.2.values
  234.7 10.2 %cross_attend.1 = (bf16[512,1024]{1,0:T(8,128)(2,1)S(1)}, f32[512,128]{1,0:T(8,128)S(1)}) custom-call(s32[4]{0:T(128)S(1)} %reshape.541.info, bf16[512,1024]{1,0:T(8,128)(2,1)S(1)} %multiply_convert_fusion.4.queries, bf16[1536,1024]{1,0:T(8,128)(2,1)S(1)} %copy-done.22, bf16[1536,1024]{1,0:T(8,128)(2,1)} %convolution_convert_fusion.2.values), custom_call_target="tpu_custom_call" | custom-call | flops 3221225472 | bytes 12582912 | tf_op jit(solution)/shard_map/cross_attend/pallas_call | solution.py:335
  248.0 15.1 %multiply_convert_fusion.1 = (bf16[512,4096]{1,0:T(8,128)(2,1)S(1)}, f32[512,4096]{1,0:T(8,128)}) fusion(f32[4096]{0:T(1024)S(1)} %copy-done.93, bf16[4096,1024]{1,0:T(8,128)(2,1)} %bitcast.386, f32[512,1024]{1,0:T(8,128)S(1)} %get-tuple-element.193, f32[1024]{0:T(1024)S(1)} %bitcast.371, f32[1024]{0:T(1024)S(1)} %bitcast.356, f32[512]{0:T(512)S(1)} %add_rsqrt_fusion.1, ...), kind=kOutput, calls=%fused_computation.15 | convolution fusion | flops 4345823232 | bytes 23097344 | tf_op jit(solution)/shard_map/dot_general | solution.py:203
  277.5 26.1 %rows_pass_0.1 = (bf16[4,7,1024,896]{3,2,1,0:T(8,128)(2,1)}, bf16[4,1152,1024]{2,1,0:T(8,128)(2,1)}, f32[4,1152,128]{2,1,0:T(8,128)}, bf16[512,1024]{1,0:T(8,128...) custom-call(s32[37]{0:T(128)} %pad_add_fusion.4.info, ...), custom_call_target="tpu_custom_call" | custom-call | flops 1048576 | bytes 65536 | tf_op jit(solution)/shard_map/rows_pass_0/pallas_call | solution.py:480
  309.7 20.7 %rows_pass_1.1 = (bf16[4,7,1024,896]{3,2,1,0:T(8,128)(2,1)}, bf16[4,1152,1024]{2,1,0:T(8,128)(2,1)}, f32[4,1152,128]{2,1,0:T(8,128)}, bf16[512,1024]{1,0:T(8,128...) custom-call(s32[37]{0:T(128)} %pad_add_fusion.4.info, ...), custom_call_target="tpu_custom_call", output_to_operand_aliasing={{0}: (5, {}), {1}: (6, {}), {2}: (7, {})} | custom-call | flops 1048576 | bytes 65536 | tf_op jit(solution)/shard_map/rows_pass_1/pallas_call | solution.py:480
  332.8 22.4 %collective-permute-done.7 = bf16[512,1024]{1,0:T(8,128)(2,1)S(1)} collective-permute-done((bf16[512,1024]{1,0:T(8,128)(2,1)}, bf16[512,1024]{1,0:T(8,128)(2,1)S(1)}, u32[]{:S(2)}, u32[]{:S(2)}) %collective-permute-start.7) | collective-permute-done | bytes 1048608 | tf_op jit(solution)/shard_map/ppermute | solution.py:30
  361.1 26.1 %rows_pass_2.1 = (bf16[4,7,1024,896]{3,2,1,0:T(8,128)(2,1)}, bf16[4,1152,1024]{2,1,0:T(8,128)(2,1)}, f32[4,1152,128]{2,1,0:T(8,128)}, bf16[512,1024]{1,0:T(8,128...) custom-call(s32[37]{0:T(128)} %pad_add_fusion.4.info, ...), custom_call_target="tpu_custom_call", output_to_operand_aliasing={{0}: (5, {}), {1}: (6, {}), {2}: (7, {})} | custom-call | flops 1048576 | bytes 65536 | tf_op jit(solution)/shard_map/rows_pass_2/pallas_call | solution.py:480
  393.6 26.5 %rows_pass_3.1 = (bf16[4,7,1024,896]{3,2,1,0:T(8,128)(2,1)}, bf16[4,1152,1024]{2,1,0:T(8,128)(2,1)}, f32[4,1152,128]{2,1,0:T(8,128)}, bf16[512,1024]{1,0:T(8,128...) custom-call(s32[37]{0:T(128)} %pad_add_fusion.4.info, ...), custom_call_target="tpu_custom_call", output_to_operand_aliasing={{0}: (5, {}), {1}: (6, {}), {2}: (7, {})} | custom-call | flops 1048576 | bytes 65536 | tf_op jit(solution)/shard_map/rows_pass_3/pallas_call | solution.py:480
  470.8 54.7 %table_pass_0.1 = (bf16[8,7,448,128]{3,2,1,0:T(8,128)(2,1)}, bf16[8,7,448,128]{3,2,1,0:T(8,128)(2,1)}) custom-call(s32[37]{0:T(128)} %pad_add_fusion.4.info, f32[32,8,128]{2,1,0:T(8,128)} %stack.137.facts, f32[4,1152,128]{2,1,0:T(8,128)} %get-tuple-element.113.tops, bf16[4,1152,1024]{2,1,0:T(8,128)(2,1)} %get-tuple-element.114.rows, ...), custom_call_target="tpu_custom_call" | custom-call | flops 1048576 | bytes 65536 | tf_op jit(solution)/shard_map/table_pass_0/pallas_call | solution.py:692
  529.5 40.0 %collective-permute-start.31 = (bf16[2,2,7,448,128]{4,3,2,1,0:T(8,128)(2,1)}, bf16[2,2,7,448,128]{4,3,2,1,0:T(8,128)(2,1)}, u32[]{:S(2)}, u32[]{:S(2)}) collective-permute-start(bf16[2,2,7,448,128]{4,3,2,1,0:T(8,128)(2,1)} %dynamic-slice_bitcast_fusion.refs_5_), channel_id=1, source_target_pairs={{0,16},{4,20},{8,24},{12,28},{16,0},{20,4},{24,8},{28,12},{1,17},{... | collective-permute-start | bytes 9633800 | tf_op jit(solution)/shard_map/ppermute | solution.py:43
  571.4 10.5 %collective-permute-start.30 = (bf16[2,2,7,448,128]{4,3,2,1,0:T(8,128)(2,1)}, bf16[2,2,7,448,128]{4,3,2,1,0:T(8,128)(2,1)}, u32[]{:S(2)}, u32[]{:S(2)}) collective-permute-start(bf16[2,2,7,448,128]{4,3,2,1,0:T(8,128)(2,1)} %dynamic-slice_bitcast_fusion.1.refs_4_), channel_id=1, source_target_pairs={{0,8},{4,12},{8,0},{12,4},{16,24},{20,28},{24,16},{28,20},{1,9},{5... | collective-permute-start | bytes 9633800 | tf_op jit(solution)/shard_map/ppermute | solution.py:43
  592.7 7.8 fusion.19
  600.6 8.1 convert_reduce_fusion
  608.7 9.7 %multiply_reduce_fusion.1 = (f32[1024]{0:T(1024)}, f32[512]{0:T(512)S(1)}, f32[512]{0:T(512)S(1)}, f32[1024]{0:T(1024)}, f32[512,1024]{1,0:T(8,128)S(1)}) fusion(f32[512,1024]{1,0:T(8,128)S(1)} %copy-done.41, f32[512]{0:T(512)S(1)} %copy-done.111, f32[512]{0:T(512)S(1)} %copy-done.92, f32[1024]{0:T(1024)S(1)} %bitcast.358, f32[512,1024]{1,0:T(8,128)S(1)} %copy-done.66, ...), kind=kOutput, calls=%fused_computation.44 | convolution fusion | flops 4300207104 | bytes 18894848 | tf_op jit(solution)/shard_map/dot_general | solution.py:193
  622.0 16.5 %cross_attend_back.1 = (bf16[512,1024]{1,0:T(8,128)(2,1)S(1)}, bf16[1536,1024]{1,0:T(8,128)(2,1)}, bf16[1536,1024]{1,0:T(8,128)(2,1)}) custom-call(s32[4]{0:T(128)S(1)} %copy-done.19, bf16[512,1024]{1,0:T(8,128)(2,1)S(1)} %copy-done.26, bf16[1536,1024]{1,0:T(8,128)(2,1)} %convolution_convert_fusion.3.keys, ...), custom_call_target="tpu_custom_call" | custom-call | flops 8053063680 | bytes 12582912 | tf_op jit(solution)/shard_map/cross_attend_back/pallas_call | solution.py:335
  638.6 5.8 fusion.68
  666.4 7.0 convolution_convert_fusion
  673.4 7.3 convolution_convert_fusion.1
  690.5 9.8 %self_attend_back.1 = (bf16[512,1024]{1,0:T(8,128)(2,1)S(1)}, bf16[512,1024]{1,0:T(8,128)(2,1)S(1)}, bf16[512,1024]{1,0:T(8,128)(2,1)S(1)}) custom-call(s32[4]{0:T(128)S(1)} %copy-done.15, bf16[512,1024]{1,0:T(8,128)(2,1)} %copy-done.5, bf16[512,1024]{1,0:T(8,128)(2,1)} %copy-done.4, bf16[512,1024]{1,0:T(8,128)(2,1)} %copy-done.3, ...), custom_call_target="tpu_custom_call" | custom-call | flops 2684354560 | bytes 4194304 | tf_op jit(solution)/shard_map/self_attend_back/pallas_call | solution.py:335
  737.3 5.8 copy-done.32
  746.2 164.5 %scatter_outputs.1 = (f32[256,1024]{1,0:T(8,128)}, f32[128,1024]{1,0:T(8,128)}, f32[128,1024]{1,0:T(8,128)}, bf16[2,4,2,32,1024]{4,3,2,1,0:T(8,128)(2,1)}, f32[16,1024]{1,0:T(8,128)}) custom-call(bf16[4,2,4,256,1024]{4,3,2,1,0:T(8,128)(2,1)} %bitcast.286, bf16[4,2,4,128,1024]{4,3,2,1,0:T(8,128)(2,1)} %bitcast.293, bf16[4,2,4,128,1024]{4,3,2,1,0:T(8,128)(2,1)} %bitcast.292, ...), custom_call_target="tpu_custom_call" | custom-call | flops 1048576 | bytes 65536 | tf_op jit(solution)/shard_map/scatter_outputs/pallas_call | solution.py:1083
  (543 shorter events, 227.9 us)
Async XLA Ops:
  0.6 228.4 %collective-permute-start = (s32[2,2]{1,0:T(2,128)}, s32[2,2]{1,0:T(2,128)S(1)}, u32[]{:S(2)}, u32[]{:S(2)}) collective-permute-start(s32[2,2]{1,0:T(2,128)} %param.21), channel_id=1, source_target_pairs={{0,1},{1,2},{2,3},{3,0},{4,5},{5,6},{6,7},{7,4},{8,9},{9,10},{10,1... | collective-permute-start | bytes 56 | tf_op jit(solution)/shard_map/ppermute | solution.py:30
  3.7 228.4 %collective-permute-start.1 = (s32[2,2]{1,0:T(2,128)}, s32[2,2]{1,0:T(2,128)S(1)}, u32[]{:S(2)}, u32[]{:S(2)}) collective-permute-start(s32[2,2]{1,0:T(2,128)} %param.21), channel_id=1, source_target_pairs={{0,2},{1,3},{2,0},{3,1},{4,6},{5,7},{6,4},{7,5},{8,10},{9,11},{10,... | collective-permute-start | bytes 56 | tf_op jit(solution)/shard_map/ppermute | solution.py:30
  6.3 225.8 %collective-permute-start.2 = (s32[2,2]{1,0:T(2,128)}, s32[2,2]{1,0:T(2,128)S(1)}, u32[]{:S(2)}, u32[]{:S(2)}) collective-permute-start(s32[2,2]{1,0:T(2,128)} %param.21), channel_id=1, source_target_pairs={{0,3},{1,0},{2,1},{3,2},{4,7},{5,4},{6,5},{7,6},{8,11},{9,8},{10,9... | collective-permute-start | bytes 56 | tf_op jit(solution)/shard_map/ppermute | solution.py:30
  190.2 78.0 %collective-permute-start.11 = (bf16[2,128,1024]{2,1,0:T(8,128)(2,1)}, bf16[2,128,1024]{2,1,0:T(8,128)(2,1)}, u32[]{:S(2)}, u32[]{:S(2)}) collective-permute-start(bf16[2,128,1024]{2,1,0:T(8,128)(2,1)} %select_select_fusion), channel_id=1, source_target_pairs={{0,1},{1,2},{2,3},{3,0},{4,5},{5,6},{6,7},{7,4},{8,9},{9,10},{10,1... | collective-permute-start | bytes 1572872 | tf_op jit(solution)/shard_map/ppermute | solution.py:30
  190.4 77.8 %collective-permute-start.12 = (bf16[2,128,1024]{2,1,0:T(8,128)(2,1)}, bf16[2,128,1024]{2,1,0:T(8,128)(2,1)}, u32[]{:S(2)}, u32[]{:S(2)}) collective-permute-start(bf16[2,128,1024]{2,1,0:T(8,128)(2,1)} %select_select_fusion), channel_id=1, source_target_pairs={{0,2},{1,3},{2,0},{3,1},{4,6},{5,7},{6,4},{7,5},{8,10},{9,11},{10,... | collective-permute-start | bytes 1572872 | tf_op jit(solution)/shard_map/ppermute | solution.py:30
  229.1 39.2 %collective-permute-start.13 = (bf16[2,128,1024]{2,1,0:T(8,128)(2,1)}, bf16[2,128,1024]{2,1,0:T(8,128)(2,1)}, u32[]{:S(2)}, u32[]{:S(2)}) collective-permute-start(bf16[2,128,1024]{2,1,0:T(8,128)(2,1)} %select_select_fusion), channel_id=1, source_target_pairs={{0,3},{1,0},{2,1},{3,2},{4,7},{5,4},{6,5},{7,6},{8,11},{9,8},{10,9... | collective-permute-start | bytes 1572872 | tf_op jit(solution)/shard_map/ppermute | solution.py:30
  232.1 41.7 %collective-permute-start.3 = (s32[2,130]{1,0:T(2,128)S(1)}, s32[2,130]{1,0:T(2,128)S(1)}, u32[]{:S(2)}, u32[]{:S(2)}) collective-permute-start(s32[2,130]{1,0:T(2,128)S(1)} %pad_add_fusion.2), channel_id=1, source_target_pairs={{0,4},{4,0},{8,12},{12,8},{16,20},{20,16},{24,28},{28,24},{1,5},{5... | collective-permute-start | bytes 3128 | tf_op jit(solution)/shard_map/ppermute | solution.py:43
  273.3 32.6 %collective-permute-start.5 = (bf16[512,1024]{1,0:T(8,128)(2,1)}, bf16[512,1024]{1,0:T(8,128)(2,1)S(1)}, u32[]{:S(2)}, u32[]{:S(2)}) collective-permute-start(bf16[512,1024]{1,0:T(8,128)(2,1)} %get-tuple-element.151.own), channel_id=1, source_target_pairs={{0,1},{1,2},{2,3},{3,0},{4,5},{5,6},{6,7},{7,4},{8,9},{9,10},{10,1... | collective-permute-start | bytes 3145736 | tf_op jit(solution)/shard_map/ppermute | solution.py:30
  306.3 48.9 %collective-permute-start.7 = (bf16[512,1024]{1,0:T(8,128)(2,1)}, bf16[512,1024]{1,0:T(8,128)(2,1)S(1)}, u32[]{:S(2)}, u32[]{:S(2)}) collective-permute-start(bf16[512,1024]{1,0:T(8,128)(2,1)} %get-tuple-element.151.own), channel_id=1, source_target_pairs={{0,2},{1,3},{2,0},{3,1},{4,6},{5,7},{6,4},{7,5},{8,10},{9,11},{10,... | collective-permute-start | bytes 3145736 | tf_op jit(solution)/shard_map/ppermute | solution.py:30
  355.4 34.5 %collective-permute-start.9 = (bf16[512,1024]{1,0:T(8,128)(2,1)}, bf16[512,1024]{1,0:T(8,128)(2,1)S(1)}, u32[]{:S(2)}, u32[]{:S(2)}) collective-permute-start(bf16[512,1024]{1,0:T(8,128)(2,1)} %get-tuple-element.151.own), channel_id=1, source_target_pairs={{0,3},{1,0},{2,1},{3,2},{4,7},{5,4},{6,5},{7,6},{8,11},{9,8},{10,9... | collective-permute-start | bytes 3145736 | tf_op jit(solution)/shard_map/ppermute | solution.py:30
  430.3 21.2 %collective-permute-start.20 = (bf16[512,1024]{1,0:T(8,128)(2,1)}, bf16[512,1024]{1,0:T(8,128)(2,1)S(1)}, u32[]{:S(2)}, u32[]{:S(2)}) collective-permute-start(bf16[512,1024]{1,0:T(8,128)(2,1)} %get-tuple-element.106), channel_id=1, source_target_pairs={{0,4},{4,0},{8,12},{12,8},{16,20},{20,16},{24,28},{28,24},{1,5},{5... | collective-permute-start | bytes 3145736 | tf_op jit(solution)/shard_map/ppermute | solution.py:43
  430.8 20.7 %collective-permute-start.21 = (bf16[512,1024]{1,0:T(8,128)(2,1)}, bf16[512,1024]{1,0:T(8,128)(2,1)S(1)}, u32[]{:S(2)}, u32[]{:S(2)}) collective-permute-start(bf16[512,1024]{1,0:T(8,128)(2,1)} %get-tuple-element.107), channel_id=1, source_target_pairs={{0,4},{4,0},{8,12},{12,8},{16,20},{20,16},{24,28},{28,24},{1,5},{5... | collective-permute-start | bytes 3145736 | tf_op jit(solution)/shard_map/ppermute | solution.py:43
  431.7 19.8 %collective-permute-start.22 = (bf16[512,1024]{1,0:T(8,128)(2,1)}, bf16[512,1024]{1,0:T(8,128)(2,1)}, u32[]{:S(2)}, u32[]{:S(2)}) collective-permute-start(bf16[512,1024]{1,0:T(8,128)(2,1)} %get-tuple-element.108), channel_id=1, source_target_pairs={{0,4},{4,0},{8,12},{12,8},{16,20},{20,16},{24,28},{28,24},{1,5},{5... | collective-permute-start | bytes 3145736 | tf_op jit(solution)/shard_map/ppermute | solution.py:43
  459.3 122.6 %collective-permute-start.27 = (bf16[512,1024]{1,0:T(8,128)(2,1)S(1)}, bf16[512,1024]{1,0:T(8,128)(2,1)}, u32[]{:S(2)}, u32[]{:S(2)}) collective-permute-start(bf16[512,1024]{1,0:T(8,128)(2,1)S(1)} %get-tuple-element.110.refs_0_), channel_id=1, source_target_pairs={{0,3},{1,0},{2,1},{3,2},{4,7},{5,4},{6,5},{7,6},{8,11},{9,8},{10,9... | collective-permute-start | bytes 3145736 | tf_op jit(solution)/shard_map/ppermute | solution.py:30
  462.6 119.3 %collective-permute-start.28 = (bf16[512,1024]{1,0:T(8,128)(2,1)S(1)}, bf16[512,1024]{1,0:T(8,128)(2,1)}, u32[]{:S(2)}, u32[]{:S(2)}) collective-permute-start(bf16[512,1024]{1,0:T(8,128)(2,1)S(1)} %get-tuple-element.111.refs_1_), channel_id=1, source_target_pairs={{0,2},{1,3},{2,0},{3,1},{4,6},{5,7},{6,4},{7,5},{8,10},{9,11},{10,... | collective-permute-start | bytes 3145736 | tf_op jit(solution)/shard_map/ppermute | solution.py:30
  462.8 119.1 %collective-permute-start.29 = (bf16[512,1024]{1,0:T(8,128)(2,1)S(1)}, bf16[512,1024]{1,0:T(8,128)(2,1)}, u32[]{:S(2)}, u32[]{:S(2)}) collective-permute-start(bf16[512,1024]{1,0:T(8,128)(2,1)S(1)} %get-tuple-element.112.refs_2_), channel_id=1, source_target_pairs={{0,1},{1,2},{2,3},{3,0},{4,5},{5,6},{6,7},{7,4},{8,9},{9,10},{10,1... | collective-permute-start | bytes 3145736 | tf_op jit(solution)/shard_map/ppermute | solution.py:30
  529.5 151.2 %collective-permute-start.31 = (bf16[2,2,7,448,128]{4,3,2,1,0:T(8,128)(2,1)}, bf16[2,2,7,448,128]{4,3,2,1,0:T(8,128)(2,1)}, u32[]{:S(2)}, u32[]{:S(2)}) collective-permute-start(bf16[2,2,7,448,128]{4,3,2,1,0:T(8,128)(2,1)} %dynamic-slice_bitcast_fusion.refs_5_), channel_id=1, source_target_pairs={{0,16},{4,20},{8,24},{12,28},{16,0},{20,4},{24,8},{28,12},{1,17},{... | collective-permute-start | bytes 9633800 | tf_op jit(solution)/shard_map/ppermute | solution.py:43
  571.4 114.7 %collective-permute-start.30 = (bf16[2,2,7,448,128]{4,3,2,1,0:T(8,128)(2,1)}, bf16[2,2,7,448,128]{4,3,2,1,0:T(8,128)(2,1)}, u32[]{:S(2)}, u32[]{:S(2)}) collective-permute-start(bf16[2,2,7,448,128]{4,3,2,1,0:T(8,128)(2,1)} %dynamic-slice_bitcast_fusion.1.refs_4_), channel_id=1, source_target_pairs={{0,8},{4,12},{8,0},{12,4},{16,24},{20,28},{24,16},{28,20},{1,9},{5... | collective-permute-start | bytes 9633800 | tf_op jit(solution)/shard_map/ppermute | solution.py:43
  651.5 266.8 %collective-permute-start.34 = (bf16[2,2,96,1024]{3,2,1,0:T(8,128)(2,1)S(1)}, bf16[2,2,96,1024]{3,2,1,0:T(8,128)(2,1)}, u32[]{:S(2)}, u32[]{:S(2)}) collective-permute-start(bf16[2,2,96,1024]{3,2,1,0:T(8,128)(2,1)S(1)} %get-tuple-element.165.refs_0_), channel_id=1, source_target_pairs={{0,1},{1,2},{2,3},{3,0},{4,5},{5,6},{6,7},{7,4},{8,9},{9,10},{10,1... | collective-permute-start | bytes 2359304 | tf_op jit(solution)/shard_map/ppermute | solution.py:30
  654.4 263.9 %collective-permute-start.35 = (bf16[2,2,96,1024]{3,2,1,0:T(8,128)(2,1)S(1)}, bf16[2,2,96,1024]{3,2,1,0:T(8,128)(2,1)}, u32[]{:S(2)}, u32[]{:S(2)}) collective-permute-start(bf16[2,2,96,1024]{3,2,1,0:T(8,128)(2,1)S(1)} %get-tuple-element.164.refs_1_), channel_id=1, source_target_pairs={{0,2},{1,3},{2,0},{3,1},{4,6},{5,7},{6,4},{7,5},{8,10},{9,11},{10,... | collective-permute-start | bytes 2359304 | tf_op jit(solution)/shard_map/ppermute | solution.py:30
  655.5 262.7 %collective-permute-start.36 = (bf16[2,2,96,1024]{3,2,1,0:T(8,128)(2,1)S(1)}, bf16[2,2,96,1024]{3,2,1,0:T(8,128)(2,1)}, u32[]{:S(2)}, u32[]{:S(2)}) collective-permute-start(bf16[2,2,96,1024]{3,2,1,0:T(8,128)(2,1)S(1)} %get-tuple-element.163.refs_2_), channel_id=1, source_target_pairs={{0,3},{1,0},{2,1},{3,2},{4,7},{5,4},{6,5},{7,6},{8,11},{9,8},{10,9... | collective-permute-start | bytes 2359304 | tf_op jit(solution)/shard_map/ppermute | solution.py:30
  689.4 36.7 %collective-permute-start.32 = (bf16[2,7,448,128]{3,2,1,0:T(8,128)(2,1)S(1)}, bf16[2,7,448,128]{3,2,1,0:T(8,128)(2,1)}, u32[]{:S(2)}, u32[]{:S(2)}) collective-permute-start(bf16[2,7,448,128]{3,2,1,0:T(8,128)(2,1)S(1)} %dynamic-slice_bitcast_fusion.4.refs_3_), channel_id=1, source_target_pairs={{0,16},{4,20},{8,24},{12,28},{16,0},{20,4},{24,8},{28,12},{1,17},{... | collective-permute-start | bytes 4816904 | tf_op jit(solution)/shard_map/ppermute | solution.py:43
  690.4 37.7 %collective-permute-start.33 = (bf16[2,7,448,128]{3,2,1,0:T(8,128)(2,1)}, bf16[2,7,448,128]{3,2,1,0:T(8,128)(2,1)S(1)}, u32[]{:S(2)}, u32[]{:S(2)}) collective-permute-start(bf16[2,7,448,128]{3,2,1,0:T(8,128)(2,1)} %dynamic-slice_bitcast_fusion.3.refs_4_), channel_id=1, source_target_pairs={{0,8},{4,12},{8,0},{12,4},{16,24},{20,28},{24,16},{28,20},{1,9},{5... | collective-permute-start | bytes 4816904 | tf_op jit(solution)/shard_map/ppermute | solution.py:43
  731.1 191.8 %collective-permute-start.37 = (bf16[6272,128]{1,0:T(8,128)(2,1)}, bf16[6272,128]{1,0:T(8,128)(2,1)}, u32[]{:S(2)}, u32[]{:S(2)}) collective-permute-start(bf16[6272,128]{1,0:T(8,128)(2,1)} %get-tuple-element.161), channel_id=1, source_target_pairs={{0,4},{4,0},{8,12},{12,8},{16,20},{20,16},{24,28},{28,24},{1,5},{5... | collective-permute-start | bytes 4816904 | tf_op jit(solution)/shard_map/ppermute | solution.py:43
  (152 other events, 1900.4 us)

commit v6 on v4

--- a/solution.py
+++ b/solution.py
@@ -547,6 +547,38 @@
     )(own, other, own_log, other_log)
 
 
+def lay_kernel(count, info, *refs):
+    out = refs[-1]
+    step = (info[0] + count - pl.program_id(0)) % count
+    for place in range(count):
+
+        @pl.when(step == place)
+        def _():
+            out[:, 0] = refs[place][...]
+
+
+def lay_blocks(blocks, place, earlier):
+    count = len(blocks)
+    own, questions, steps, width = blocks[0].shape
+    whole = lambda i, s: (0, 0, 0, 0)
+    return pl.pallas_call(
+        functools.partial(lay_kernel, count),
+        grid_spec=pltpu.PrefetchScalarGridSpec(
+            num_scalar_prefetch=1,
+            grid=(count,),
+            in_specs=[pl.BlockSpec(blocks[0].shape, whole, pipeline_mode=pl.Buffered(1))] * count
+            + [pl.BlockSpec(memory_space=pl.ANY)] * len(earlier),
+            out_specs=pl.BlockSpec(
+                (own, 1, questions, steps, width), lambda i, s: (0, i, 0, 0, 0)
+            ),
+        ),
+        out_shape=jax.ShapeDtypeStruct((own, count, questions, steps, width), blocks[0].dtype),
+        compiler_params=pltpu.CompilerParams(vmem_limit_bytes=48 << 20),
+        cost_estimate=SMALL,
+        name="lay_blocks",
+    )(place.reshape(1).astype(jnp.int32), *blocks, *earlier)
+
+
 def home_kernel(count, logs, weight, targets, *refs):
     parts, out = refs[:count], refs[-1]
     log = logs[0]
@@ -1352,7 +1384,11 @@
         grad_inputs,
         after(small, table_send),
     )
-    grad_memory = to_positions(grad_memory, small)
+    grad_memory = [grad_memory[0]] + [
+        shifted(grad_memory[step], "slot", step) for step in range(1, slot_count)
+    ]
+    grad_memory = lay_blocks(grad_memory, place, (small,))
+    grad_memory = grad_memory.reshape((-1,) + grad_memory.shape[2:])
     kept = pick(table_sum, core, 0)
     given = after(shifted(table_send, "core", 1), small)
     grad_embed = jnp.stack([kept, given])

time: 958 us -> 940 us (0.981); the launches traced: 966 us -> 927 us
  starting transfers between devices: 97.9 us -> 27.1 us
  Pallas kernels: 561 us -> 598 us
    ppermute x20, starting transfers between devices: 57.2 us -> 6.76 us  [shifted(): return lax.ppermute(value, 'pb', pairs)]
    ppermute x18, starting transfers between devices: 40.7 us -> 20.3 us  [shifted(): lax.ppermute(value, 'slot', [(i, (i + step) % size) for i in range(size)])]
    pallas_call x4, Pallas kernels: 110 us -> 129 us  [rows_pass(): pl.pallas_call(functools.partial(rows_kernel, step), grid_spec=pltpu.Pref...]
    pallas_call x1, Pallas kernels: 64.1 us -> 77.8 us  [table_pass(): pl.pallas_call(functools.partial(table_kernel, first), grid_spec=pltpu.Pr...]
    unnamed x216 -> x226, local copies, waits for them, and re-layouts: 28.6 us -> 31.1 us
  transfers between devices with their start and end apart: 38 -> 38, of which waited for: 7 -> 10; matrix products, arithmetic and copies ran while one was open for 23% -> 23% of each run, Pallas kernels for 58% -> 64%
where the time goes in v6:
time: 940 us; the launch traced here: 927 us
  Pallas kernels  598 us (64%)
  matrix products  117 us (12%)
  local copies, waits for them, and re-layouts  86.1 us (9%)
  other arithmetic  49.6 us (5%)
  waiting for transfers between devices  31.5 us (3%)
  starting transfers between devices  27.1 us (3%)
  between operations  17.6 us (2%)
    pallas_call x1, Pallas kernels, gather_inputs(): pl.pallas_call(gather_kernel, in_specs=[anywhere] * 5, out_specs=[anywher...  165 us
    pallas_call x1, Pallas kernels, scatter_outputs(): pl.pallas_call(scatter_kernel, in_specs=[anywhere] * 4 + [inside], out_sp...  164 us
    pallas_call x4, Pallas kernels, rows_pass(): pl.pallas_call(functools.partial(rows_kernel, step), grid_spec=pltpu.Pref...  129 us
    pallas_call x1, Pallas kernels, table_pass(): pl.pallas_call(functools.partial(table_kernel, first), grid_spec=pltpu.Pr...  77.8 us
    dot_general x10, matrix products, contract_cols(): lax.dot_general(left, right, (((1,), (1,)), ((), ())), preferred_element_...  49.2 us
    pallas_call x4, Pallas kernels, attend(): pl.pallas_call(functools.partial(kernel, causal), grid_spec=pltpu.Prefetc...  41.5 us
    dot_general x10, matrix products, product(): return jnp.dot(left, right, preferred_element_type=jnp.float32)  38.2 us
    unnamed x226, local copies, waits for them, and re-layouts  31.1 us
  transfers between devices with their start and end apart: 38, of which 10 were waited for; matrix products, arithmetic and copies ran while one was open for 23% of the time, Pallas kernels for 64%

profile of v6, /device:TPU:0, one launch (start us, length us, event | category | flops | bytes accessed | tf_op | source)
XLA Modules:
  0.0 927.0 jit_solution(16805114428791262253)
XLA Ops:
  8.1 164.7 %gather_inputs.1 = (bf16[8,4,256,1024]{3,2,1,0:T(8,128)(2,1)}, bf16[8,4,128,1024]{3,2,1,0:T(8,128)(2,1)}, bf16[8,4,128,1024]{3,2,1,0:T(8,128)(2,1)}, bf16[2,2,4,...) custom-call(bf16[256,1024]{1,0:T(8,128)(2,1)} %refs_0_.1, bf16[128,1024]{1,0:T(8,128)(2,1)} %refs_1_.1, ...), custom_call_target="tpu_custom_call" | custom-call | tf_op jit(solution)/shard_map/gather_inputs/pallas_call | solution.py:853
  175.4 13.2 %gather_fusion.2 = bf16[256,1024]{1,0:T(8,128)(2,1)S(1)} fusion(bf16[12544,1024]{1,0:T(8,128)(2,1)} %table.7, s32[1024]{0:T(1024)S(1)} %pad_clamp_fusion.1), kind=kCustom, calls=%fused_computation.2 | custom fusion | bytes 1049600 | tf_op jit(solution)/shard_map/jit(_take)/gather | solution.py:1183
  192.4 8.9 fusion.61
  213.0 4.8 convolution_convert_fusion.2.values
  217.8 4.8 convolution_convert_fusion.3.keys
  232.5 10.4 %cross_attend.1 = (bf16[512,1024]{1,0:T(8,128)(2,1)S(1)}, f32[512,128]{1,0:T(8,128)S(1)}) custom-call(s32[4]{0:T(128)S(1)} %reshape.541.info, bf16[512,1024]{1,0:T(8,128)(2,1)S(1)} %multiply_convert_fusion.4.queries, bf16[1536,1024]{1,0:T(8,128)(2,1)S(1)} %copy-done.10, bf16[1536,1024]{1,0:T(8,128)(2,1)} %convolution_convert_fusion.2.values), custom_call_target="tpu_custom_call" | custom-call | flops 3221225472 | bytes 12582912 | tf_op jit(solution)/shard_map/cross_attend/pallas_call | solution.py:335
  247.5 13.2 %multiply_convert_fusion.1 = (bf16[512,4096]{1,0:T(8,128)(2,1)S(1)}, f32[512,4096]{1,0:T(8,128)}) fusion(f32[4096]{0:T(1024)S(1)} %copy-done.69, bf16[4096,1024]{1,0:T(8,128)(2,1)S(1)} %bitcast.393, f32[512,1024]{1,0:T(8,128)S(1)} %get-tuple-element.185, f32[1024]{0:T(1024)S(1)} %bitcast.375, f32[1024]{0:T(1024)S(1)} %bitcast.360, ...), kind=kOutput, calls=%fused_computation.15 | convolution fusion | flops 4345823232 | bytes 23097344 | tf_op jit(solution)/shard_map/dot_general | solution.py:203
  260.7 8.8 fusion.67
  279.3 34.2 %rows_pass_0.1 = (bf16[4,7,1024,896]{3,2,1,0:T(8,128)(2,1)}, bf16[4,1152,1024]{2,1,0:T(8,128)(2,1)}, f32[4,1152,128]{2,1,0:T(8,128)}, bf16[512,1024]{1,0:T(8,128...) custom-call(s32[37]{0:T(128)} %pad_add_fusion.4.info, ...), custom_call_target="tpu_custom_call" | custom-call | flops 1048576 | bytes 65536 | tf_op jit(solution)/shard_map/rows_pass_0/pallas_call | solution.py:480
  321.2 26.4 %rows_pass_1.1 = (bf16[4,7,1024,896]{3,2,1,0:T(8,128)(2,1)}, bf16[4,1152,1024]{2,1,0:T(8,128)(2,1)}, f32[4,1152,128]{2,1,0:T(8,128)}, bf16[512,1024]{1,0:T(8,128...) custom-call(s32[37]{0:T(128)} %pad_add_fusion.4.info, ...), custom_call_target="tpu_custom_call", output_to_operand_aliasing={{0}: (5, {}), {1}: (6, {}), {2}: (7, {})} | custom-call | flops 1048576 | bytes 65536 | tf_op jit(solution)/shard_map/rows_pass_1/pallas_call | solution.py:480
  350.2 15.9 %collective-permute-done.7 = bf16[512,1024]{1,0:T(8,128)(2,1)} collective-permute-done((bf16[512,1024]{1,0:T(8,128)(2,1)}, bf16[512,1024]{1,0:T(8,128)(2,1)}, u32[]{:S(2)}, u32[]{:S(2)}) %collective-permute-start.7) | collective-permute-done | bytes 1048608 | tf_op jit(solution)/shard_map/ppermute | solution.py:30
  370.2 34.2 %rows_pass_2.1 = (bf16[4,7,1024,896]{3,2,1,0:T(8,128)(2,1)}, bf16[4,1152,1024]{2,1,0:T(8,128)(2,1)}, f32[4,1152,128]{2,1,0:T(8,128)}, bf16[512,1024]{1,0:T(8,128...) custom-call(s32[37]{0:T(128)} %pad_add_fusion.4.info, ...), custom_call_target="tpu_custom_call", output_to_operand_aliasing={{0}: (5, {}), {1}: (6, {}), {2}: (7, {})} | custom-call | flops 1048576 | bytes 65536 | tf_op jit(solution)/shard_map/rows_pass_2/pallas_call | solution.py:480
  412.1 34.5 %rows_pass_3.1 = (bf16[4,7,1024,896]{3,2,1,0:T(8,128)(2,1)}, bf16[4,1152,1024]{2,1,0:T(8,128)(2,1)}, f32[4,1152,128]{2,1,0:T(8,128)}, bf16[512,1024]{1,0:T(8,128...) custom-call(s32[37]{0:T(128)} %pad_add_fusion.4.info, ...), custom_call_target="tpu_custom_call", output_to_operand_aliasing={{0}: (5, {}), {1}: (6, {}), {2}: (7, {})} | custom-call | flops 1048576 | bytes 65536 | tf_op jit(solution)/shard_map/rows_pass_3/pallas_call | solution.py:480
  484.2 77.8 %table_pass_0.1 = (bf16[8,7,448,128]{3,2,1,0:T(8,128)(2,1)}, bf16[8,7,448,128]{3,2,1,0:T(8,128)(2,1)}) custom-call(s32[37]{0:T(128)} %pad_add_fusion.4.info, f32[32,8,128]{2,1,0:T(8,128)} %stack.137.facts, f32[4,1152,128]{2,1,0:T(8,128)} %get-tuple-element.105.tops, bf16[4,1152,1024]{2,1,0:T(8,128)(2,1)} %get-tuple-element.106.rows, ...), custom_call_target="tpu_custom_call" | custom-call | flops 1048576 | bytes 65536 | tf_op jit(solution)/shard_map/table_pass_0/pallas_call | solution.py:686
  571.6 5.5 home_pass.1
  581.2 11.3 %fusion.19 = f32[512,4096]{1,0:T(8,128)} fusion(bf16[4096,1024]{1,0:T(8,128)(2,1)} %bitcast.395, f32[512,1024]{1,0:T(8,128)S(1)} %subtract_multiply_fusion.2), kind=kOutput, calls=%fused_computation.105 | convolution fusion | flops 4295491584 | bytes 18874368 | tf_op jit(solution)/shard_map/dot_general | solution.py:203
  592.5 9.8 %convert_reduce_fusion = (f32[4096]{0:T(1024)S(1)}, bf16[512,4096]{1,0:T(8,128)(2,1)S(1)}) fusion(f32[512,4096]{1,0:T(8,128)} %fusion.19, f32[512,4096]{1,0:T(8,128)S(1)} %bitcast.289, f32[4096]{0:T(1024)S(1)} %copy-done.69), kind=kLoop, calls=%fused_computation.12 | loop fusion | flops 62910464 | bytes 21004288 | tf_op jit(solution)/shard_map/reduce_sum | solution.py:1319
  602.3 9.7 %multiply_reduce_fusion.1 = (f32[1024]{0:T(1024)}, f32[512]{0:T(512)S(1)}, f32[512]{0:T(512)S(1)}, f32[1024]{0:T(1024)}, f32[512,1024]{1,0:T(8,128)S(1)}) fusion(f32[512,1024]{1,0:T(8,128)S(1)} %copy-done.26, f32[512]{0:T(512)S(1)} %add_rsqrt_fusion.1, f32[512]{0:T(512)S(1)} %broadcast_multiply_fusion.7, f32[1024]{0:T(1024)S(1)} %bitcast.362, ...), kind=kOutput, calls=%fused_computation.44 | convolution fusion | flops 4300207104 | bytes 18894848 | tf_op jit(solution)/shard_map/dot_general | solution.py:193
  615.0 16.8 %cross_attend_back.1 = (bf16[512,1024]{1,0:T(8,128)(2,1)S(1)}, bf16[1536,1024]{1,0:T(8,128)(2,1)}, bf16[1536,1024]{1,0:T(8,128)(2,1)}) custom-call(s32[4]{0:T(128)S(1)} %reshape.541.info, bf16[512,1024]{1,0:T(8,128)(2,1)S(1)} %multiply_convert_fusion.4.queries, bf16[1536,1024]{1,0:T(8,128)(2,1)} %convolution_convert_fusion.3.keys, ...), custom_call_target="tpu_custom_call" | custom-call | flops 8053063680 | bytes 12582912 | tf_op jit(solution)/shard_map/cross_attend_back/pallas_call | solution.py:335
  657.2 7.1 convolution_convert_fusion
  664.3 7.3 convolution_convert_fusion.1
  681.8 9.8 %self_attend_back.1 = (bf16[512,1024]{1,0:T(8,128)(2,1)S(1)}, bf16[512,1024]{1,0:T(8,128)(2,1)S(1)}, bf16[512,1024]{1,0:T(8,128)(2,1)S(1)}) custom-call(s32[4]{0:T(128)S(1)} %copy-done.5, bf16[512,1024]{1,0:T(8,128)(2,1)} %copy-done.2, bf16[512,1024]{1,0:T(8,128)(2,1)} %copy-done.1, bf16[512,1024]{1,0:T(8,128)(2,1)} %copy-done, ...), custom_call_target="tpu_custom_call" | custom-call | flops 2684354560 | bytes 4194304 | tf_op jit(solution)/shard_map/self_attend_back/pallas_call | solution.py:335
  729.0 5.8 copy-done.16
  738.0 164.3 %scatter_outputs.1 = (f32[256,1024]{1,0:T(8,128)}, f32[128,1024]{1,0:T(8,128)}, f32[128,1024]{1,0:T(8,128)}, bf16[2,4,2,32,1024]{4,3,2,1,0:T(8,128)(2,1)}, f32[16,1024]{1,0:T(8,128)}) custom-call(bf16[4,2,4,256,1024]{4,3,2,1,0:T(8,128)(2,1)} %bitcast.286, bf16[4,2,4,128,1024]{4,3,2,1,0:T(8,128)(2,1)} %bitcast.293, bf16[4,2,4,128,1024]{4,3,2,1,0:T(8,128)(2,1)} %bitcast.292, ...), custom_call_target="tpu_custom_call" | custom-call | flops 1048576 | bytes 65536 | tf_op jit(solution)/shard_map/scatter_outputs/pallas_call | solution.py:1077
  (492 shorter events, 210.3 us)
Async XLA Ops:
  0.6 225.6 %collective-permute-start = (s32[2,2]{1,0:T(2,128)}, s32[2,2]{1,0:T(2,128)S(1)}, u32[]{:S(2)}, u32[]{:S(2)}) collective-permute-start(s32[2,2]{1,0:T(2,128)} %param.21), channel_id=1, source_target_pairs={{0,1},{1,2},{2,3},{3,0},{4,5},{5,6},{6,7},{7,4},{8,9},{9,10},{10,1... | collective-permute-start | bytes 56 | tf_op jit(solution)/shard_map/ppermute | solution.py:30
  3.7 226.2 %collective-permute-start.2 = (s32[2,2]{1,0:T(2,128)}, s32[2,2]{1,0:T(2,128)S(1)}, u32[]{:S(2)}, u32[]{:S(2)}) collective-permute-start(s32[2,2]{1,0:T(2,128)} %param.21), channel_id=1, source_target_pairs={{0,3},{1,0},{2,1},{3,2},{4,7},{5,4},{6,5},{7,6},{8,11},{9,8},{10,9... | collective-permute-start | bytes 56 | tf_op jit(solution)/shard_map/ppermute | solution.py:30
  5.8 224.1 %collective-permute-start.1 = (s32[2,2]{1,0:T(2,128)}, s32[2,2]{1,0:T(2,128)S(1)}, u32[]{:S(2)}, u32[]{:S(2)}) collective-permute-start(s32[2,2]{1,0:T(2,128)} %param.21), channel_id=1, source_target_pairs={{0,2},{1,3},{2,0},{3,1},{4,6},{5,7},{6,4},{7,5},{8,10},{9,11},{10,... | collective-permute-start | bytes 56 | tf_op jit(solution)/shard_map/ppermute | solution.py:30
  189.5 80.4 %collective-permute-start.12 = (bf16[2,128,1024]{2,1,0:T(8,128)(2,1)}, bf16[2,128,1024]{2,1,0:T(8,128)(2,1)S(1)}, u32[]{:S(2)}, u32[]{:S(2)}) collective-permute-start(bf16[2,128,1024]{2,1,0:T(8,128)(2,1)} %select_select_fusion), channel_id=1, source_target_pairs={{0,2},{1,3},{2,0},{3,1},{4,6},{5,7},{6,4},{7,5},{8,10},{9,11},{10,... | collective-permute-start | bytes 1572872 | tf_op jit(solution)/shard_map/ppermute | solution.py:30
  191.2 78.7 %collective-permute-start.11 = (bf16[2,128,1024]{2,1,0:T(8,128)(2,1)}, bf16[2,128,1024]{2,1,0:T(8,128)(2,1)S(1)}, u32[]{:S(2)}, u32[]{:S(2)}) collective-permute-start(bf16[2,128,1024]{2,1,0:T(8,128)(2,1)} %select_select_fusion), channel_id=1, source_target_pairs={{0,1},{1,2},{2,3},{3,0},{4,5},{5,6},{6,7},{7,4},{8,9},{9,10},{10,1... | collective-permute-start | bytes 1572872 | tf_op jit(solution)/shard_map/ppermute | solution.py:30
  226.2 45.5 %collective-permute-start.13 = (bf16[2,128,1024]{2,1,0:T(8,128)(2,1)}, bf16[2,128,1024]{2,1,0:T(8,128)(2,1)}, u32[]{:S(2)}, u32[]{:S(2)}) collective-permute-start(bf16[2,128,1024]{2,1,0:T(8,128)(2,1)} %select_select_fusion), channel_id=1, source_target_pairs={{0,3},{1,0},{2,1},{3,2},{4,7},{5,4},{6,5},{7,6},{8,11},{9,8},{10,9... | collective-permute-start | bytes 1572872 | tf_op jit(solution)/shard_map/ppermute | solution.py:30
  229.9 46.0 %collective-permute-start.3 = (s32[2,130]{1,0:T(2,128)S(1)}, s32[2,130]{1,0:T(2,128)S(1)}, u32[]{:S(2)}, u32[]{:S(2)}) collective-permute-start(s32[2,130]{1,0:T(2,128)S(1)} %pad_add_fusion.2), channel_id=1, source_target_pairs={{0,4},{4,0},{8,12},{12,8},{16,20},{20,16},{24,28},{28,24},{1,5},{5... | collective-permute-start | bytes 3128 | tf_op jit(solution)/shard_map/ppermute | solution.py:43
  275.2 40.9 %collective-permute-start.5 = (bf16[512,1024]{1,0:T(8,128)(2,1)}, bf16[512,1024]{1,0:T(8,128)(2,1)}, u32[]{:S(2)}, u32[]{:S(2)}) collective-permute-start(bf16[512,1024]{1,0:T(8,128)(2,1)} %get-tuple-element.143.own), channel_id=1, source_target_pairs={{0,1},{1,2},{2,3},{3,0},{4,5},{5,6},{6,7},{7,4},{8,9},{9,10},{10,1... | collective-permute-start | bytes 3145736 | tf_op jit(solution)/shard_map/ppermute | solution.py:30
  317.9 48.2 %collective-permute-start.7 = (bf16[512,1024]{1,0:T(8,128)(2,1)}, bf16[512,1024]{1,0:T(8,128)(2,1)}, u32[]{:S(2)}, u32[]{:S(2)}) collective-permute-start(bf16[512,1024]{1,0:T(8,128)(2,1)} %get-tuple-element.143.own), channel_id=1, source_target_pairs={{0,2},{1,3},{2,0},{3,1},{4,6},{5,7},{6,4},{7,5},{8,10},{9,11},{10,... | collective-permute-start | bytes 3145736 | tf_op jit(solution)/shard_map/ppermute | solution.py:30
  367.5 39.6 %collective-permute-start.9 = (bf16[512,1024]{1,0:T(8,128)(2,1)}, bf16[512,1024]{1,0:T(8,128)(2,1)}, u32[]{:S(2)}, u32[]{:S(2)}) collective-permute-start(bf16[512,1024]{1,0:T(8,128)(2,1)} %get-tuple-element.143.own), channel_id=1, source_target_pairs={{0,3},{1,0},{2,1},{3,2},{4,7},{5,4},{6,5},{7,6},{8,11},{9,8},{10,9... | collective-permute-start | bytes 3145736 | tf_op jit(solution)/shard_map/ppermute | solution.py:30
  367.8 80.7 %collective-permute-start.18 = (f32[2,8]{1,0:T(2,128)S(1)}, f32[2,8]{1,0:T(2,128)S(1)}, u32[]{:S(2)}, u32[]{:S(2)}) collective-permute-start(f32[2,8]{1,0:T(2,128)S(1)} %copy-done.87), channel_id=1, source_target_pairs={{0,4},{4,0},{8,12},{12,8},{16,20},{20,16},{24,28},{28,24},{1,5},{5... | collective-permute-start | bytes 200 | tf_op jit(solution)/shard_map/ppermute | solution.py:43
  368.2 90.6 %collective-permute-start.19 = (bf16[512,1024]{1,0:T(8,128)(2,1)}, bf16[512,1024]{1,0:T(8,128)(2,1)}, u32[]{:S(2)}, u32[]{:S(2)}) collective-permute-start(bf16[512,1024]{1,0:T(8,128)(2,1)} %get-tuple-element.98), channel_id=1, source_target_pairs={{0,4},{4,0},{8,12},{12,8},{16,20},{20,16},{24,28},{28,24},{1,5},{5... | collective-permute-start | bytes 3145736 | tf_op jit(solution)/shard_map/ppermute | solution.py:43
  408.7 53.6 %collective-permute-start.21 = (bf16[512,1024]{1,0:T(8,128)(2,1)}, bf16[512,1024]{1,0:T(8,128)(2,1)}, u32[]{:S(2)}, u32[]{:S(2)}) collective-permute-start(bf16[512,1024]{1,0:T(8,128)(2,1)} %get-tuple-element.100), channel_id=1, source_target_pairs={{0,4},{4,0},{8,12},{12,8},{16,20},{20,16},{24,28},{28,24},{1,5},{5... | collective-permute-start | bytes 3145736 | tf_op jit(solution)/shard_map/ppermute | solution.py:43
  409.1 57.0 %collective-permute-start.24 = (bf16[512,1024]{1,0:T(8,128)(2,1)}, bf16[512,1024]{1,0:T(8,128)(2,1)}, u32[]{:S(2)}, u32[]{:S(2)}) collective-permute-start(bf16[512,1024]{1,0:T(8,128)(2,1)} %get-tuple-element.102), channel_id=1, source_target_pairs={{0,4},{4,0},{8,12},{12,8},{16,20},{20,16},{24,28},{28,24},{1,5},{5... | collective-permute-start | bytes 3145736 | tf_op jit(solution)/shard_map/ppermute | solution.py:43
  465.6 105.0 %collective-permute-start.23 = (bf16[512,1024]{1,0:T(8,128)(2,1)}, bf16[512,1024]{1,0:T(8,128)(2,1)}, u32[]{:S(2)}, u32[]{:S(2)}) collective-permute-start(bf16[512,1024]{1,0:T(8,128)(2,1)} %join_pass.5.refs_0_), channel_id=1, source_target_pairs={{0,3},{1,0},{2,1},{3,2},{4,7},{5,4},{6,5},{7,6},{8,11},{9,8},{10,9... | collective-permute-start | bytes 3145736 | tf_op jit(solution)/shard_map/ppermute | solution.py:30
  469.5 101.1 %collective-permute-start.26 = (bf16[512,1024]{1,0:T(8,128)(2,1)}, bf16[512,1024]{1,0:T(8,128)(2,1)}, u32[]{:S(2)}, u32[]{:S(2)}) collective-permute-start(bf16[512,1024]{1,0:T(8,128)(2,1)} %join_pass.6.refs_1_), channel_id=1, source_target_pairs={{0,2},{1,3},{2,0},{3,1},{4,6},{5,7},{6,4},{7,5},{8,10},{9,11},{10,... | collective-permute-start | bytes 3145736 | tf_op jit(solution)/shard_map/ppermute | solution.py:30
  476.1 94.5 %collective-permute-start.29 = (bf16[512,1024]{1,0:T(8,128)(2,1)}, bf16[512,1024]{1,0:T(8,128)(2,1)S(1)}, u32[]{:S(2)}, u32[]{:S(2)}) collective-permute-start(bf16[512,1024]{1,0:T(8,128)(2,1)} %join_pass.7.refs_2_), channel_id=1, source_target_pairs={{0,1},{1,2},{2,3},{3,0},{4,5},{5,6},{6,7},{7,4},{8,9},{9,10},{10,1... | collective-permute-start | bytes 3145736 | tf_op jit(solution)/shard_map/ppermute | solution.py:30
  566.0 105.6 %collective-permute-start.30 = (bf16[2,2,7,448,128]{4,3,2,1,0:T(8,128)(2,1)}, bf16[2,2,7,448,128]{4,3,2,1,0:T(8,128)(2,1)}, u32[]{:S(2)}, u32[]{:S(2)}) collective-permute-start(bf16[2,2,7,448,128]{4,3,2,1,0:T(8,128)(2,1)} %dynamic-slice_bitcast_fusion.1.refs_4_), channel_id=1, source_target_pairs={{0,8},{4,12},{8,0},{12,4},{16,24},{20,28},{24,16},{28,20},{1,9},{5... | collective-permute-start | bytes 9633800 | tf_op jit(solution)/shard_map/ppermute | solution.py:43
  568.8 107.5 %collective-permute-start.31 = (bf16[2,2,7,448,128]{4,3,2,1,0:T(8,128)(2,1)}, bf16[2,2,7,448,128]{4,3,2,1,0:T(8,128)(2,1)}, u32[]{:S(2)}, u32[]{:S(2)}) collective-permute-start(bf16[2,2,7,448,128]{4,3,2,1,0:T(8,128)(2,1)} %dynamic-slice_bitcast_fusion.refs_5_), channel_id=1, source_target_pairs={{0,16},{4,20},{8,24},{12,28},{16,0},{20,4},{24,8},{28,12},{1,17},{... | collective-permute-start | bytes 9633800 | tf_op jit(solution)/shard_map/ppermute | solution.py:43
  642.6 267.1 %collective-permute-start.36 = (bf16[2,2,96,1024]{3,2,1,0:T(8,128)(2,1)S(1)}, bf16[2,2,96,1024]{3,2,1,0:T(8,128)(2,1)}, u32[]{:S(2)}, u32[]{:S(2)}) collective-permute-start(bf16[2,2,96,1024]{3,2,1,0:T(8,128)(2,1)S(1)} %get-tuple-element.155.refs_2_), channel_id=1, source_target_pairs={{0,3},{1,0},{2,1},{3,2},{4,7},{5,4},{6,5},{7,6},{8,11},{9,8},{10,9... | collective-permute-start | bytes 2359304 | tf_op jit(solution)/shard_map/ppermute | solution.py:30
  645.1 264.6 %collective-permute-start.35 = (bf16[2,2,96,1024]{3,2,1,0:T(8,128)(2,1)S(1)}, bf16[2,2,96,1024]{3,2,1,0:T(8,128)(2,1)}, u32[]{:S(2)}, u32[]{:S(2)}) collective-permute-start(bf16[2,2,96,1024]{3,2,1,0:T(8,128)(2,1)S(1)} %get-tuple-element.156.refs_1_), channel_id=1, source_target_pairs={{0,2},{1,3},{2,0},{3,1},{4,6},{5,7},{6,4},{7,5},{8,10},{9,11},{10,... | collective-permute-start | bytes 2359304 | tf_op jit(solution)/shard_map/ppermute | solution.py:30
  646.2 263.5 %collective-permute-start.34 = (bf16[2,2,96,1024]{3,2,1,0:T(8,128)(2,1)S(1)}, bf16[2,2,96,1024]{3,2,1,0:T(8,128)(2,1)}, u32[]{:S(2)}, u32[]{:S(2)}) collective-permute-start(bf16[2,2,96,1024]{3,2,1,0:T(8,128)(2,1)S(1)} %get-tuple-element.157.refs_0_), channel_id=1, source_target_pairs={{0,1},{1,2},{2,3},{3,0},{4,5},{5,6},{6,7},{7,4},{8,9},{9,10},{10,1... | collective-permute-start | bytes 2359304 | tf_op jit(solution)/shard_map/ppermute | solution.py:30
  676.1 42.3 %collective-permute-start.32 = (bf16[2,7,448,128]{3,2,1,0:T(8,128)(2,1)}, bf16[2,7,448,128]{3,2,1,0:T(8,128)(2,1)}, u32[]{:S(2)}, u32[]{:S(2)}) collective-permute-start(bf16[2,7,448,128]{3,2,1,0:T(8,128)(2,1)} %dynamic-slice_bitcast_fusion.4.refs_3_), channel_id=1, source_target_pairs={{0,16},{4,20},{8,24},{12,28},{16,0},{20,4},{24,8},{28,12},{1,17},{... | collective-permute-start | bytes 4816904 | tf_op jit(solution)/shard_map/ppermute | solution.py:43
  722.8 191.5 %collective-permute-start.37 = (bf16[6272,128]{1,0:T(8,128)(2,1)}, bf16[6272,128]{1,0:T(8,128)(2,1)}, u32[]{:S(2)}, u32[]{:S(2)}) collective-permute-start(bf16[6272,128]{1,0:T(8,128)(2,1)} %get-tuple-element.153), channel_id=1, source_target_pairs={{0,4},{4,0},{8,12},{12,8},{16,20},{20,16},{24,28},{28,24},{1,5},{5... | collective-permute-start | bytes 4816904 | tf_op jit(solution)/shard_map/ppermute | solution.py:43
  (125 other events, 1086.6 us)
